TPU v7x, 768 devices: a whole 4x8x12 slice. The times are simulated.
768 devices in a mesh: strip: 12 (over z), tile: 64 (over x, y, core).
Axes of the slice: x: 4, y: 8, z: 12, core: 2. Of those that a mesh axis runs over, the one named last changes fastest.
Arguments:
- coords: float32 [36864, 3, 128], P(('strip', 'tile')), may hold values from -0.25 to 12288.25, as said below
- displacement: float32 [36864, 3, 128], P(('strip', 'tile')), may hold values from -0.75 to 0.75
- pairs: int32 [49152, 2], P(('strip', 'tile')), may hold values from 0 to 36863, as said below
- intact: int32 [49152, 128, 128], P(('strip', 'tile')), may hold values 0 or 1
Outputs:
- force: float32 [36864, 3, 128], P(('strip', 'tile'))
Inputs may be any that keep to these rules, and one draw needn't show every extreme that they name: `coords`: each point sits within 0.25 of its lattice site: tile t covers a 4 x 4 x 8 block of unit lattice sites starting at (4 (t // 3072), 4 (t % 3072), 0), point i at offset (i % 4, (i // 4) % 4, i // 16). `pairs`: the rows of one device (device number d = strip index * 64 + tile index) name as first tile one of the 48 tiles that this device holds, and as second tile a different one whose strip differs from the first's by at most one and whose place within its strip differs from the first's place within its strip by at most one.
All inputs are finite; a program needn't handle non-finite values. No bound on the sum of `intact` on one device may be relied on, other than what follows from the above.
Results may differ from a plain program's by a relative error of at most 0.0003.
Values sent between devices are 32-bit elements; how exact they have to be, the bound alone decides.
No kernel may reach another device: no remote copies, remote signals or barrier semaphores. Data moves between devices by JAX's collectives and lax.ppermute only.
A program may use at most 32 MiB of HBM per device.

v0:
```python
import math

import jax
import jax.numpy as jnp
from jax import lax
from jax.sharding import PartitionSpec as P

horizon = 3.0
stiffness = 2.0
onset_stretch = 0.02
final_stretch = 0.05


def from_behind(value, axis, steps):
    count = lax.axis_size(axis)
    first, last = (max(0, -steps), min(count, count - steps))
    return lax.ppermute(value, axis, [(source, source + steps) for source in range(first, last)])


def padded(block, sides, width):
    for axis, dim in sides:
        count = lax.axis_size(axis)
        forward = [(i, i + 1) for i in range(count - 1)]
        backward = [(target, source) for source, target in forward]
        low = lax.ppermute(
            lax.slice_in_dim(block, block.shape[dim] - width, None, axis=dim), axis, forward
        )
        high = lax.ppermute(lax.slice_in_dim(block, 0, width, axis=dim), axis, backward)
        block = jnp.concatenate([low, block, high], axis=dim)
    return block


def block_forces(first_block, second, bond_mask):
    bond_ref = second[0:3, None, :] - first_block[0:3, :, None]
    bond_now = bond_ref + second[3:6, None, :] - first_block[3:6, :, None]
    length_ref = jnp.sqrt(jnp.sum(bond_ref * bond_ref, axis=0))
    length_now = jnp.sqrt(jnp.sum(bond_now * bond_now, axis=0))
    stretch = (length_now - length_ref) / length_ref
    influence = jnp.maximum(0.0, 1.0 - length_ref / horizon)
    soften = jnp.clip((final_stretch - stretch) / (final_stretch - onset_stretch), 0.0, 1.0)
    pull_scale = (
        stiffness * stretch * influence * soften * bond_mask.astype(jnp.float32) / length_now
    )
    bond_force = pull_scale[None] * bond_now
    return (jnp.sum(bond_force, axis=2), -jnp.sum(bond_force, axis=1))


def strip_pass(below_part, above_part):
    from_above = from_behind(below_part, "strip", -1)
    from_below = from_behind(above_part, "strip", 1)
    return from_above + from_below


def tile_pass(left_edge, right_edge):
    to_last = from_behind(left_edge, "tile", -1)
    to_first = from_behind(right_edge, "tile", 1)
    return (to_last, to_first)


def on_device(coords, displacement, pairs, intact):
    owned = jnp.concatenate([coords, displacement], axis=1)
    per_device = owned.shape[0]
    span = per_device + 2
    points = owned.shape[-1]
    strip_tiles = per_device * lax.axis_size("tile")
    framed = padded(owned[None], (("strip", 0), ("tile", 1)), 1)
    framed = framed.reshape(3 * span, 6, points)
    strip_index = lax.axis_index("strip")
    tile_index = lax.axis_index("tile")

    def place(tile_ids):
        row_part = (tile_ids // strip_tiles - strip_index + 1) * span
        return row_part + tile_ids % strip_tiles - tile_index * per_device + 1

    group_size = math.gcd(pairs.shape[0], 8)
    grouped_pairs = pairs.reshape(-1, group_size, 2)
    grouped_bonds = intact.reshape(-1, group_size, intact.shape[1], intact.shape[2])

    def visit(forces, scan_item):
        couple, bond_mask = scan_item
        first_slots = place(couple[:, 0])
        second_slots = place(couple[:, 1])
        gain_first, gain_second = jax.vmap(block_forces)(
            framed[first_slots], framed[second_slots], bond_mask
        )
        forces = forces.at[first_slots].add(gain_first)
        forces = forces.at[second_slots].add(gain_second)
        return (forces, None)

    zero_forces = jnp.zeros((3 * span, 3, points), jnp.float32)
    forces, unused = lax.scan(visit, zero_forces, (grouped_pairs, grouped_bonds))
    buffer = forces.reshape(3, span, 3, points)
    strip_row = buffer[1] + strip_pass(buffer[0], buffer[2])
    to_last, to_first = tile_pass(strip_row[0], strip_row[span - 1])
    result = strip_row[1 : span - 1]
    result = result.at[per_device - 1].add(to_last)
    result = result.at[0].add(to_first)
    return result


def solution(mesh):
    placed = (
        P(("strip", "tile"), None, None),
        P(("strip", "tile"), None, None),
        P(("strip", "tile"), None),
        P(("strip", "tile"), None, None),
    )
    return jax.shard_map(
        on_device,
        mesh=mesh,
        in_specs=placed,
        out_specs=P(("strip", "tile"), None, None),
        check_vma=False,
    )
```

profile of v0, /device:TPU:196, one launch (start us, length us, event | category | flops | bytes accessed | tf_op | source)
XLA Modules:
  0.0 102.4 jit_solution(3973684532246139097)
XLA Ops:
  0.9 5.5 %collective-permute-start = (f32[1,48,6,128]{3,1,2,0:T(8,128)S(1)}, f32[1,48,6,128]{3,1,2,0:T(8,128)S(1)}, u32[]{:S(2)}, u32[]{:S(2)}) collective-permute-start(f32[1,48,6,128]{3,1,2,0:T(8,128)S(1)} %maximum_bitcast_fusion), channel_id=1, source_target_pairs={{0,64},{64,128},{128,192},{192,256},{256,320},{320,384},{384,448},... | collective-permute-start | bytes 442376 | tf_op jit(solution)/shard_map/ppermute | solution.py:25
  6.4 1.9 %collective-permute-start.1 = (f32[1,48,6,128]{3,1,2,0:T(8,128)S(1)}, f32[1,48,6,128]{3,1,2,0:T(8,128)S(1)}, u32[]{:S(2)}, u32[]{:S(2)}) collective-permute-start(f32[1,48,6,128]{3,1,2,0:T(8,128)S(1)} %maximum_bitcast_fusion), channel_id=1, source_target_pairs={{64,0},{128,64},{192,128},{256,192},{320,256},{384,320},{448,384},... | collective-permute-start | bytes 442376 | tf_op jit(solution)/shard_map/ppermute | solution.py:28
  9.5 5.3 %collective-permute-done.1 = f32[1,48,6,128]{3,1,2,0:T(8,128)S(1)} collective-permute-done((f32[1,48,6,128]{3,1,2,0:T(8,128)S(1)}, f32[1,48,6,128]{3,1,2,0:T(8,128)S(1)}, u32[]{:S(2)}, u32[]{:S(2)}) %collective-permute-start.1) | collective-permute-done | bytes 147488 | tf_op jit(solution)/shard_map/ppermute | solution.py:28
  14.9 1.9 %collective-permute-start.2 = (f32[3,1,6,128]{3,1,2,0:T(1,128)S(1)}, f32[3,1,6,128]{3,1,2,0:T(1,128)S(1)}, u32[]{:S(2)}, u32[]{:S(2)}) collective-permute-start(f32[3,1,6,128]{3,1,2,0:T(1,128)S(1)} %get-tuple-element.205), channel_id=1, source_target_pairs={{0,1},{1,2},{2,3},{3,4},{4,5},{5,6},{6,7},{7,8},{8,9},{9,10},{10,1... | collective-permute-start | bytes 27656 | tf_op jit(solution)/shard_map/ppermute | solution.py:25
  16.8 5.8 %collective-permute-start.3 = (f32[3,1,6,128]{3,1,2,0:T(1,128)S(1)}, f32[3,1,6,128]{3,1,2,0:T(1,128)S(1)}, u32[]{:S(2)}, u32[]{:S(2)}) collective-permute-start(f32[3,1,6,128]{3,1,2,0:T(1,128)S(1)} %get-tuple-element.206), channel_id=1, source_target_pairs={{1,0},{2,1},{3,2},{4,3},{5,4},{6,5},{7,6},{8,7},{9,8},{10,9},{11,1... | collective-permute-start | bytes 27656 | tf_op jit(solution)/shard_map/ppermute | solution.py:28
  24.1 56.5 %while.15 = (s32[]{:T(128)}, f32[150,3,128]{2,1,0:T(4,128)S(1)}, s32[8,8,2]{1,0,2:T(8,128)S(1)}, s32[]{:T(128)}, s32[]{:T(128)}, /*index=5*/f32[150,6,128]{2,1,0:T(8,128)S(1)}, s32[8,8,128,128]{3,2,1,0:T(8,128)}, s32[]{:T(128)}) while((s32[]{:T(128)}, f32[150,3,128]{2,1,0:T(4,128)S(1)}, s32[8,8,2]{1,0,2:T(8,128)S(1)}, s32[]{:T(128)}, ...), condition=%wide.region_7.8_spmd, body=%wide.region_0.7_spmd.sunk | while | flops 6690130 | bytes 4096549 | solution.py:91
  26.4 1.6 %fusion.27 = f32[8,128,128]{2,1,0:T(8,128)S(1)} fusion(s32[8,8,128,128]{3,2,1,0:T(8,128)} %get-tuple-element.300, s32[]{:T(128)} %get-tuple-element.286, f32[8,128,128]{2,1,0:T(8,128)S(1)} %get-tuple-element.274, f32[8,128,128]{2,1,0:T(8,128)S(1)} %get-tuple-element.275), kind=kLoop, calls=%fused_computation.15.clone.1 | loop fusion | flops 1835008 | bytes 2097156 | tf_op jit(solution)/shard_map/while/body/eval_jaxpr/vmap()/div | solution.py:42
  28.0 1.6 %fusion.28 = (f32[8,3,128]{2,1,0:T(4,128)S(1)}, f32[8,3,128]{2,1,0:T(4,128)S(1)}) fusion(f32[8,128,128]{2,1,0:T(8,128)S(1)} %fusion.27, f32[8,3,128]{2,1,0:T(4,128)S(1)} %get-tuple-element.269, f32[8,3,128]{2,1,0:T(4,128)S(1)} %get-tuple-element.271, f32[8,3,128]{2,1,0:T(4,128)S(1)} %get-tuple-element.272, f32[8,3,128]{2,1,0:T(4,128)S(1)} %get-tuple-element.273), kind=kLoop, calls=%fused_computation.9.clone.1 | loop fusion | flops 2353152 | bytes 598016 | tf_op jit(solution)/shard_map/while/body/eval_jaxpr/vmap()/reduce_sum | solution.py:45
  33.5 1.6 %fusion.27 = f32[8,128,128]{2,1,0:T(8,128)S(1)} fusion(s32[8,8,128,128]{3,2,1,0:T(8,128)} %get-tuple-element.300, s32[]{:T(128)} %get-tuple-element.286, f32[8,128,128]{2,1,0:T(8,128)S(1)} %get-tuple-element.274, f32[8,128,128]{2,1,0:T(8,128)S(1)} %get-tuple-element.275), kind=kLoop, calls=%fused_computation.15.clone.1 | loop fusion | flops 1835008 | bytes 2097156 | tf_op jit(solution)/shard_map/while/body/eval_jaxpr/vmap()/div | solution.py:42
  35.1 1.6 %fusion.28 = (f32[8,3,128]{2,1,0:T(4,128)S(1)}, f32[8,3,128]{2,1,0:T(4,128)S(1)}) fusion(f32[8,128,128]{2,1,0:T(8,128)S(1)} %fusion.27, f32[8,3,128]{2,1,0:T(4,128)S(1)} %get-tuple-element.269, f32[8,3,128]{2,1,0:T(4,128)S(1)} %get-tuple-element.271, f32[8,3,128]{2,1,0:T(4,128)S(1)} %get-tuple-element.272, f32[8,3,128]{2,1,0:T(4,128)S(1)} %get-tuple-element.273), kind=kLoop, calls=%fused_computation.9.clone.1 | loop fusion | flops 2353152 | bytes 598016 | tf_op jit(solution)/shard_map/while/body/eval_jaxpr/vmap()/reduce_sum | solution.py:45
  42.1 1.6 %fusion.28 = (f32[8,3,128]{2,1,0:T(4,128)S(1)}, f32[8,3,128]{2,1,0:T(4,128)S(1)}) fusion(f32[8,128,128]{2,1,0:T(8,128)S(1)} %fusion.27, f32[8,3,128]{2,1,0:T(4,128)S(1)} %get-tuple-element.269, f32[8,3,128]{2,1,0:T(4,128)S(1)} %get-tuple-element.271, f32[8,3,128]{2,1,0:T(4,128)S(1)} %get-tuple-element.272, f32[8,3,128]{2,1,0:T(4,128)S(1)} %get-tuple-element.273), kind=kLoop, calls=%fused_computation.9.clone.1 | loop fusion | flops 2353152 | bytes 598016 | tf_op jit(solution)/shard_map/while/body/eval_jaxpr/vmap()/reduce_sum | solution.py:45
  47.6 1.6 %fusion.27 = f32[8,128,128]{2,1,0:T(8,128)S(1)} fusion(s32[8,8,128,128]{3,2,1,0:T(8,128)} %get-tuple-element.300, s32[]{:T(128)} %get-tuple-element.286, f32[8,128,128]{2,1,0:T(8,128)S(1)} %get-tuple-element.274, f32[8,128,128]{2,1,0:T(8,128)S(1)} %get-tuple-element.275), kind=kLoop, calls=%fused_computation.15.clone.1 | loop fusion | flops 1835008 | bytes 2097156 | tf_op jit(solution)/shard_map/while/body/eval_jaxpr/vmap()/div | solution.py:42
  49.2 1.6 %fusion.28 = (f32[8,3,128]{2,1,0:T(4,128)S(1)}, f32[8,3,128]{2,1,0:T(4,128)S(1)}) fusion(f32[8,128,128]{2,1,0:T(8,128)S(1)} %fusion.27, f32[8,3,128]{2,1,0:T(4,128)S(1)} %get-tuple-element.269, f32[8,3,128]{2,1,0:T(4,128)S(1)} %get-tuple-element.271, f32[8,3,128]{2,1,0:T(4,128)S(1)} %get-tuple-element.272, f32[8,3,128]{2,1,0:T(4,128)S(1)} %get-tuple-element.273), kind=kLoop, calls=%fused_computation.9.clone.1 | loop fusion | flops 2353152 | bytes 598016 | tf_op jit(solution)/shard_map/while/body/eval_jaxpr/vmap()/reduce_sum | solution.py:45
  54.7 1.6 %fusion.27 = f32[8,128,128]{2,1,0:T(8,128)S(1)} fusion(s32[8,8,128,128]{3,2,1,0:T(8,128)} %get-tuple-element.300, s32[]{:T(128)} %get-tuple-element.286, f32[8,128,128]{2,1,0:T(8,128)S(1)} %get-tuple-element.274, f32[8,128,128]{2,1,0:T(8,128)S(1)} %get-tuple-element.275), kind=kLoop, calls=%fused_computation.15.clone.1 | loop fusion | flops 1835008 | bytes 2097156 | tf_op jit(solution)/shard_map/while/body/eval_jaxpr/vmap()/div | solution.py:42
  56.3 1.6 %fusion.28 = (f32[8,3,128]{2,1,0:T(4,128)S(1)}, f32[8,3,128]{2,1,0:T(4,128)S(1)}) fusion(f32[8,128,128]{2,1,0:T(8,128)S(1)} %fusion.27, f32[8,3,128]{2,1,0:T(4,128)S(1)} %get-tuple-element.269, f32[8,3,128]{2,1,0:T(4,128)S(1)} %get-tuple-element.271, f32[8,3,128]{2,1,0:T(4,128)S(1)} %get-tuple-element.272, f32[8,3,128]{2,1,0:T(4,128)S(1)} %get-tuple-element.273), kind=kLoop, calls=%fused_computation.9.clone.1 | loop fusion | flops 2353152 | bytes 598016 | tf_op jit(solution)/shard_map/while/body/eval_jaxpr/vmap()/reduce_sum | solution.py:45
  63.3 1.6 %fusion.28 = (f32[8,3,128]{2,1,0:T(4,128)S(1)}, f32[8,3,128]{2,1,0:T(4,128)S(1)}) fusion(f32[8,128,128]{2,1,0:T(8,128)S(1)} %fusion.27, f32[8,3,128]{2,1,0:T(4,128)S(1)} %get-tuple-element.269, f32[8,3,128]{2,1,0:T(4,128)S(1)} %get-tuple-element.271, f32[8,3,128]{2,1,0:T(4,128)S(1)} %get-tuple-element.272, f32[8,3,128]{2,1,0:T(4,128)S(1)} %get-tuple-element.273), kind=kLoop, calls=%fused_computation.9.clone.1 | loop fusion | flops 2353152 | bytes 598016 | tf_op jit(solution)/shard_map/while/body/eval_jaxpr/vmap()/reduce_sum | solution.py:45
  68.8 1.6 %fusion.27 = f32[8,128,128]{2,1,0:T(8,128)S(1)} fusion(s32[8,8,128,128]{3,2,1,0:T(8,128)} %get-tuple-element.300, s32[]{:T(128)} %get-tuple-element.286, f32[8,128,128]{2,1,0:T(8,128)S(1)} %get-tuple-element.274, f32[8,128,128]{2,1,0:T(8,128)S(1)} %get-tuple-element.275), kind=kLoop, calls=%fused_computation.15.clone.1 | loop fusion | flops 1835008 | bytes 2097156 | tf_op jit(solution)/shard_map/while/body/eval_jaxpr/vmap()/div | solution.py:42
  70.4 1.6 %fusion.28 = (f32[8,3,128]{2,1,0:T(4,128)S(1)}, f32[8,3,128]{2,1,0:T(4,128)S(1)}) fusion(f32[8,128,128]{2,1,0:T(8,128)S(1)} %fusion.27, f32[8,3,128]{2,1,0:T(4,128)S(1)} %get-tuple-element.269, f32[8,3,128]{2,1,0:T(4,128)S(1)} %get-tuple-element.271, f32[8,3,128]{2,1,0:T(4,128)S(1)} %get-tuple-element.272, f32[8,3,128]{2,1,0:T(4,128)S(1)} %get-tuple-element.273), kind=kLoop, calls=%fused_computation.9.clone.1 | loop fusion | flops 2353152 | bytes 598016 | tf_op jit(solution)/shard_map/while/body/eval_jaxpr/vmap()/reduce_sum | solution.py:45
  77.5 1.6 %fusion.28 = (f32[8,3,128]{2,1,0:T(4,128)S(1)}, f32[8,3,128]{2,1,0:T(4,128)S(1)}) fusion(f32[8,128,128]{2,1,0:T(8,128)S(1)} %fusion.27, f32[8,3,128]{2,1,0:T(4,128)S(1)} %get-tuple-element.269, f32[8,3,128]{2,1,0:T(4,128)S(1)} %get-tuple-element.271, f32[8,3,128]{2,1,0:T(4,128)S(1)} %get-tuple-element.272, f32[8,3,128]{2,1,0:T(4,128)S(1)} %get-tuple-element.273), kind=kLoop, calls=%fused_computation.9.clone.1 | loop fusion | flops 2353152 | bytes 598016 | tf_op jit(solution)/shard_map/while/body/eval_jaxpr/vmap()/reduce_sum | solution.py:45
  80.7 1.9 %collective-permute-start.4 = (f32[50,3,128]{2,1,0:T(4,128)S(1)}, f32[50,3,128]{2,1,0:T(4,128)S(1)}, u32[]{:S(2)}, u32[]{:S(2)}) collective-permute-start(f32[50,3,128]{2,1,0:T(4,128)S(1)} %get-tuple-element.208), channel_id=1, source_target_pairs={{64,0},{128,64},{192,128},{256,192},{320,256},{384,320},{448,384},... | collective-permute-start | bytes 230408 | tf_op jit(solution)/shard_map/ppermute | solution.py:17
  82.7 5.1 %collective-permute-start.5 = (f32[50,3,128]{2,1,0:T(4,128)S(1)}, f32[50,3,128]{2,1,0:T(4,128)S(1)}, u32[]{:S(2)}, u32[]{:S(2)}) collective-permute-start(f32[50,3,128]{2,1,0:T(4,128)S(1)} %get-tuple-element.207), channel_id=1, source_target_pairs={{0,64},{64,128},{128,192},{192,256},{256,320},{320,384},{384,448},... | collective-permute-start | bytes 230408 | tf_op jit(solution)/shard_map/ppermute | solution.py:17
  90.1 4.6 %collective-permute-start.6 = (f32[3,128]{1,0:T(4,128)S(1)}, f32[3,128]{1,0:T(4,128)S(1)}, u32[]{:S(2)}, u32[]{:S(2)}) collective-permute-start(f32[3,128]{1,0:T(4,128)S(1)} %get-tuple-element.210), channel_id=1, source_target_pairs={{1,0},{2,1},{3,2},{4,3},{5,4},{6,5},{7,6},{8,7},{9,8},{10,9},{11,1... | collective-permute-start | bytes 4616 | tf_op jit(solution)/shard_map/ppermute | solution.py:17
  94.7 1.9 %collective-permute-start.7 = (f32[3,128]{1,0:T(4,128)S(1)}, f32[3,128]{1,0:T(4,128)S(1)}, u32[]{:S(2)}, u32[]{:S(2)}) collective-permute-start(f32[3,128]{1,0:T(4,128)S(1)} %get-tuple-element.209), channel_id=1, source_target_pairs={{0,1},{1,2},{2,3},{3,4},{4,5},{5,6},{6,7},{7,8},{8,9},{9,10},{10,1... | collective-permute-start | bytes 4616 | tf_op jit(solution)/shard_map/ppermute | solution.py:17
  96.7 5.1 %collective-permute-done.7 = f32[3,128]{1,0:T(4,128)S(1)} collective-permute-done((f32[3,128]{1,0:T(4,128)S(1)}, f32[3,128]{1,0:T(4,128)S(1)}, u32[]{:S(2)}, u32[]{:S(2)}) %collective-permute-start.7) | collective-permute-done | bytes 1568 | tf_op jit(solution)/shard_map/ppermute | solution.py:17
  (110 shorter events, 41.6 us)
Async XLA Ops:
  0.9 8.6 %collective-permute-start = (f32[1,48,6,128]{3,1,2,0:T(8,128)S(1)}, f32[1,48,6,128]{3,1,2,0:T(8,128)S(1)}, u32[]{:S(2)}, u32[]{:S(2)}) collective-permute-start(f32[1,48,6,128]{3,1,2,0:T(8,128)S(1)} %maximum_bitcast_fusion), channel_id=1, source_target_pairs={{0,64},{64,128},{128,192},{192,256},{256,320},{320,384},{384,448},... | collective-permute-start | bytes 442376 | tf_op jit(solution)/shard_map/ppermute | solution.py:25
  6.4 8.4 %collective-permute-start.1 = (f32[1,48,6,128]{3,1,2,0:T(8,128)S(1)}, f32[1,48,6,128]{3,1,2,0:T(8,128)S(1)}, u32[]{:S(2)}, u32[]{:S(2)}) collective-permute-start(f32[1,48,6,128]{3,1,2,0:T(8,128)S(1)} %maximum_bitcast_fusion), channel_id=1, source_target_pairs={{64,0},{128,64},{192,128},{256,192},{320,256},{384,320},{448,384},... | collective-permute-start | bytes 442376 | tf_op jit(solution)/shard_map/ppermute | solution.py:28
  14.9 8.5 %collective-permute-start.2 = (f32[3,1,6,128]{3,1,2,0:T(1,128)S(1)}, f32[3,1,6,128]{3,1,2,0:T(1,128)S(1)}, u32[]{:S(2)}, u32[]{:S(2)}) collective-permute-start(f32[3,1,6,128]{3,1,2,0:T(1,128)S(1)} %get-tuple-element.205), channel_id=1, source_target_pairs={{0,1},{1,2},{2,3},{3,4},{4,5},{5,6},{6,7},{7,8},{8,9},{9,10},{10,1... | collective-permute-start | bytes 27656 | tf_op jit(solution)/shard_map/ppermute | solution.py:25
  16.8 7.1 %collective-permute-start.3 = (f32[3,1,6,128]{3,1,2,0:T(1,128)S(1)}, f32[3,1,6,128]{3,1,2,0:T(1,128)S(1)}, u32[]{:S(2)}, u32[]{:S(2)}) collective-permute-start(f32[3,1,6,128]{3,1,2,0:T(1,128)S(1)} %get-tuple-element.206), channel_id=1, source_target_pairs={{1,0},{2,1},{3,2},{4,3},{5,4},{6,5},{7,6},{8,7},{9,8},{10,9},{11,1... | collective-permute-start | bytes 27656 | tf_op jit(solution)/shard_map/ppermute | solution.py:28
  80.7 7.8 %collective-permute-start.4 = (f32[50,3,128]{2,1,0:T(4,128)S(1)}, f32[50,3,128]{2,1,0:T(4,128)S(1)}, u32[]{:S(2)}, u32[]{:S(2)}) collective-permute-start(f32[50,3,128]{2,1,0:T(4,128)S(1)} %get-tuple-element.208), channel_id=1, source_target_pairs={{64,0},{128,64},{192,128},{256,192},{320,256},{384,320},{448,384},... | collective-permute-start | bytes 230408 | tf_op jit(solution)/shard_map/ppermute | solution.py:17
  82.7 7.4 %collective-permute-start.5 = (f32[50,3,128]{2,1,0:T(4,128)S(1)}, f32[50,3,128]{2,1,0:T(4,128)S(1)}, u32[]{:S(2)}, u32[]{:S(2)}) collective-permute-start(f32[50,3,128]{2,1,0:T(4,128)S(1)} %get-tuple-element.207), channel_id=1, source_target_pairs={{0,64},{64,128},{128,192},{192,256},{256,320},{320,384},{384,448},... | collective-permute-start | bytes 230408 | tf_op jit(solution)/shard_map/ppermute | solution.py:17
  90.1 6.6 %collective-permute-start.6 = (f32[3,128]{1,0:T(4,128)S(1)}, f32[3,128]{1,0:T(4,128)S(1)}, u32[]{:S(2)}, u32[]{:S(2)}) collective-permute-start(f32[3,128]{1,0:T(4,128)S(1)} %get-tuple-element.210), channel_id=1, source_target_pairs={{1,0},{2,1},{3,2},{4,3},{5,4},{6,5},{7,6},{8,7},{9,8},{10,9},{11,1... | collective-permute-start | bytes 4616 | tf_op jit(solution)/shard_map/ppermute | solution.py:17
  94.7 7.0 %collective-permute-start.7 = (f32[3,128]{1,0:T(4,128)S(1)}, f32[3,128]{1,0:T(4,128)S(1)}, u32[]{:S(2)}, u32[]{:S(2)}) collective-permute-start(f32[3,128]{1,0:T(4,128)S(1)} %get-tuple-element.209), channel_id=1, source_target_pairs={{0,1},{1,2},{2,3},{3,4},{4,5},{5,6},{6,7},{7,8},{8,9},{9,10},{10,1... | collective-permute-start | bytes 4616 | tf_op jit(solution)/shard_map/ppermute | solution.py:17
where the time goes:
time: 103 us; the launch traced here: 102 us
  other arithmetic  47.7 us (46%)
  starting transfers between devices  28.7 us (28%)
  waiting for transfers between devices  14.4 us (14%)
  local copies, waits for them, and re-layouts  10.7 us (10%)
    ppermute x4, starting transfers between devices, from_behind(): lax.ppermute(value, axis, [(source, source + steps) for source in range(f...  13.6 us
    reduce_sum x8, other arithmetic, block_forces(): return (jnp.sum(bond_force, axis=2), -jnp.sum(bond_force, axis=1))  12.9 us
    div x8, other arithmetic, block_forces(): stiffness * stretch * influence * soften * bond_mask.astype(jnp.float32)  12.6 us
    reduce_sum x8, other arithmetic, block_forces(): length_now = jnp.sqrt(jnp.sum(bond_now * bond_now, axis=0))  8.35 us
    ppermute x2, starting transfers between devices, padded(): lax.ppermute(lax.slice_in_dim(block, 0, width, axis=dim), axis, backward)  7.67 us
    ppermute x2, starting transfers between devices, padded(): lax.ppermute(lax.slice_in_dim(block, block.shape[dim] - width, None, axis...  7.41 us
    ppermute x4, waiting for transfers between devices, from_behind(): lax.ppermute(value, axis, [(source, source + steps) for source in range(f...  7.29 us
    scatter-add x8, other arithmetic, visit(): forces = forces.at[first_slots].add(gain_first)  6.24 us
  transfers between devices with their start and end apart: 8, of which 6 were waited for; matrix products, arithmetic and copies ran while one was open for 1% of the time, Pallas kernels for 0%

commit v1 on v0

v1 whole, which is shorter than its diff:
```python
import functools

import jax
import jax.numpy as jnp
from jax import lax
from jax.experimental import pallas as pl
from jax.experimental.pallas import tpu as pltpu
from jax.sharding import PartitionSpec as P

HORIZON = 3.0
STIFFNESS = 2.0
ONSET = 0.02
FINAL = 0.05

GROUP = 4
VMEM = pl.BlockSpec(memory_space=pltpu.VMEM)
HBM = pl.BlockSpec(memory_space=pltpu.HBM)
SMEM = pl.BlockSpec(memory_space=pltpu.SMEM)


def shifted(value, axis, step):
    count = lax.axis_size(axis)
    first, last = max(0, -step), min(count, count - step)
    return lax.ppermute(value, axis, [(i, i + step) for i in range(first, last)])


def in_hbm(value):
    return pltpu.with_memory_space_constraint(value, pltpu.HBM)


def padded_rows(rows):
    return (rows + 7) // 8 * 8


def pack_kernel(held, coords, displacement, out, first, last, arrived):
    rows = 3 * held
    copies = [
        pltpu.make_async_copy(source, out.at[pl.ds(i * rows, rows)], arrived.at[i])
        for i, source in enumerate((coords, displacement))
    ]
    for copy in copies:
        copy.start()
    out[2 * rows :] = jnp.zeros((out.shape[0] - 2 * rows, out.shape[1]), jnp.float32)
    for copy in copies:
        copy.wait()
    for t, edge in ((0, first), (held - 1, last)):
        edge[...] = out[pl.ds(t, 6, stride=held)]


def frame_kernel(held, payload, left, right, out):
    out[6 * held : 6 * held + 6] = left[...]
    out[6 * held + 6 : 6 * held + 12] = right[...]


def pieces(value):
    first = value.astype(jnp.bfloat16).astype(jnp.float32)
    rest = value - first
    second = rest.astype(jnp.bfloat16).astype(jnp.float32)
    return first, second, rest - second


def side_rows(tile, middle, row):
    here = tile - middle
    moved = pltpu.roll(here, 5, axis=0)
    now = here + moved
    low = row < 3
    square = jnp.sum(jnp.where(low, here * here, 0.0), axis=0, keepdims=True)
    growth = jnp.sum(jnp.where(low, moved * (here + now), 0.0), axis=0, keepdims=True)
    return here, moved, now, square, growth


def now_rows(now, row):
    first = now.astype(jnp.bfloat16).astype(jnp.float32)
    second = now - first
    top = jnp.where(row < 3, first, jnp.where(row == 3, 1.0, 0.0))
    rows = jnp.concatenate([top, jnp.where(row < 3, second, 0.0)], axis=0)
    rows = rows.astype(jnp.bfloat16)
    return jnp.concatenate([rows, rows], axis=1)


def pair_forces(tile_a, tile_b, mid_x, mid_y, bond_mask, mid_z):
    points = tile_a.shape[-1]
    row = lax.broadcasted_iota(jnp.int32, (8, points), 0)
    middle = jnp.where(
        row == 0, mid_x, jnp.where(row == 1, mid_y, jnp.where(row == 2, mid_z, 0.0))
    )
    here_a, _, now_a, square_a, growth_a = side_rows(tile_a, middle, row)
    here_b, moved_b, now_b, square_b, growth_b = side_rows(tile_b, middle, row)

    six, seven = row == 6, row == 7
    left = jnp.where(row < 6, -2.0 * here_a, jnp.where(six, square_a, growth_a))
    l1, l2, l3 = pieces(left)

    def ones(value):
        return jnp.where(row < 6, value, jnp.where(six, 1.0, 0.0))

    o1, o2 = ones(l1), ones(l2)
    lhs = jnp.concatenate([l1, l2, l3, o1, o2, o1], axis=0).astype(jnp.bfloat16)

    shifted_b = pltpu.roll(now_b, 3, axis=0)
    right_ref = jnp.where(row < 3, here_b, jnp.where(six, square_b, 0.0))
    right_gain = jnp.where(
        row < 3, moved_b, jnp.where(row < 6, shifted_b, jnp.where(six, growth_b, 0.0))
    )

    def stack(value, at_six, at_seven):
        p1, p2, p3 = pieces(value)
        base = jnp.where(six, at_six, jnp.where(seven, at_seven, p1))
        mixed = jnp.where(six, p1, p2)
        return jnp.concatenate([base, base, base, mixed, p2, p3], axis=0)

    rhs = jnp.concatenate([stack(right_ref, 1.0, 0.0), stack(right_gain, 0.0, 1.0)], axis=1)
    both = lax.dot_general(
        lhs, rhs.astype(jnp.bfloat16), (((0,), (0,)), ((), ())), preferred_element_type=jnp.float32
    )
    ref2, gain2 = both[:, :points], both[:, points:]

    now2 = jnp.maximum(ref2 + gain2, 1e-6)
    per_ref, per_now = lax.rsqrt(ref2), lax.rsqrt(now2)
    length_ref, length_now = ref2 * per_ref, now2 * per_now
    stretch = gain2 * per_ref / (length_now + length_ref)
    influence = jnp.maximum(1.0 - length_ref * (1.0 / HORIZON), 0.0)
    spread = FINAL - ONSET
    soften = jnp.clip(FINAL / spread - stretch * (1.0 / spread), 0.0, 1.0)
    pull = (
        (STIFFNESS * stretch) * (influence * soften) * (per_now * bond_mask.astype(jnp.float32))
    )
    high = pull.astype(jnp.bfloat16)
    low = (pull - high.astype(jnp.float32)).astype(jnp.bfloat16)

    on_b = jnp.dot(
        now_rows(now_a, row),
        jnp.concatenate([high, low], axis=0),
        preferred_element_type=jnp.float32,
    )
    on_a = lax.dot_general(
        now_rows(now_b, row),
        jnp.concatenate([high, low], axis=1),
        (((1,), (1,)), ((), ())),
        preferred_element_type=jnp.float32,
    )
    sum_a, sum_b = on_a[0:8] + on_a[8:16], on_b[0:8] + on_b[8:16]
    return sum_a - now_a * sum_a[3:4], sum_b - now_b * sum_b[3:4]


def bond_kernel(mid_z, held, info, below, own, above, intact, force, down, up, edges, table, total, held_bonds, arrived):
    count = intact.shape[0]
    steps = count // GROUP

    def bonds(step):
        part = pl.ds(step * GROUP, GROUP)
        return pltpu.make_async_copy(intact.at[part], held_bonds.at[part], arrived.at[step])

    for step in range(steps):
        bonds(step).start()
    span = held + 2
    for r, payload in enumerate((below, own, above)):
        for t in range(held):
            table[r * span + t, 0:6] = payload[pl.ds(t, 6, stride=held)]
        table[r * span + held, 0:6] = payload[6 * held : 6 * held + 6]
        table[r * span + held + 1, 0:6] = payload[6 * held + 6 : 6 * held + 12]
    total[...] = jnp.zeros_like(total)

    def visit(step, carry):
        bonds(step).wait()
        gains = []
        for g in range(GROUP):
            k = step * GROUP + g
            slot_a, slot_b = info[0, k], info[1, k]
            mid_x = info[2, k].astype(jnp.float32) + 1.5
            mid_y = info[3, k].astype(jnp.float32) + 1.5
            gain_a, gain_b = pair_forces(
                table[slot_a], table[slot_b], mid_x, mid_y, held_bonds[k], mid_z
            )
            gains.append((slot_a, gain_a))
            gains.append((slot_b, gain_b))
        for slot, gain in gains:
            total[slot] += gain
        return carry

    lax.fori_loop(0, steps, visit, 0)

    for r, out in enumerate((down, force, up)):
        for t in range(held):
            out[pl.ds(t, 3, stride=held)] = total[r * span + t, 0:3]
    for r, out, at in ((0, down, 3 * held), (1, edges, 0), (2, up, 3 * held)):
        out[at : at + 3] = total[r * span + held, 0:3]
        out[at + 3 : at + 6] = total[r * span + held + 1, 0:3]
    for out in (down, up):
        end = 3 * span
        out[end:] = jnp.zeros((out.shape[0] - end, out.shape[1]), jnp.float32)


def merge_kernel(held, force, from_above, from_below, to_first, to_last, out):
    rows = 3 * held
    out[...] = force[...] + (from_above[0:rows] + from_below[0:rows])
    out[pl.ds(0, 3, stride=held)] += to_first[...]
    out[pl.ds(held - 1, 3, stride=held)] += to_last[...]


def limit(mebibytes):
    return pltpu.CompilerParams(vmem_limit_bytes=mebibytes * 1024 * 1024)


def bond_call(held, count, points):
    span = held + 2
    f32 = jnp.float32
    sent = jax.ShapeDtypeStruct((padded_rows(3 * span), points), f32)
    return pl.pallas_call(
        functools.partial(bond_kernel, 3.5, held),
        out_shape=(
            jax.ShapeDtypeStruct((3 * held, points), f32),
            sent,
            sent,
            jax.ShapeDtypeStruct((6, points), f32),
        ),
        in_specs=[SMEM] + [VMEM] * 3 + [HBM],
        out_specs=(VMEM,) * 4,
        scratch_shapes=[pltpu.VMEM((3 * span, 8, points), f32)] * 2
        + [
            pltpu.VMEM((count, points, points), jnp.int32),
            pltpu.SemaphoreType.DMA((count // GROUP,)),
        ],
        compiler_params=limit(8),
        name="bond_forces",
    )


def on_device(coords, displacement, pairs, intact):
    held, _, points = coords.shape
    span = held + 2
    strip_tiles = held * lax.axis_size("tile")
    f32 = jnp.float32

    edge = jax.ShapeDtypeStruct((6, points), f32)
    packed = jax.ShapeDtypeStruct((padded_rows(6 * span), points), f32)
    inside, first, last = pl.pallas_call(
        functools.partial(pack_kernel, held),
        out_shape=(packed, edge, edge),
        in_specs=[HBM] * 2,
        out_specs=(VMEM,) * 3,
        scratch_shapes=[pltpu.SemaphoreType.DMA((2,))],
        compiler_params=limit(1),
        name="pack_payload",
    )(
        in_hbm(jnp.transpose(coords, (1, 0, 2)).reshape(-1, points)),
        in_hbm(jnp.transpose(displacement, (1, 0, 2)).reshape(-1, points)),
    )
    left = shifted(last, "tile", 1)
    right = shifted(first, "tile", -1)
    own = pl.pallas_call(
        functools.partial(frame_kernel, held),
        out_shape=packed,
        in_specs=[VMEM] * 3,
        out_specs=VMEM,
        input_output_aliases={0: 0},
        compiler_params=limit(1),
        name="frame_payload",
    )(inside, left, right)
    below = shifted(own, "strip", 1)
    above = shifted(own, "strip", -1)

    strip_of, place = pairs // strip_tiles, pairs % strip_tiles
    row = strip_of - lax.axis_index("strip") + 1
    local = place - lax.axis_index("tile") * held
    column = jnp.where(local < 0, held, jnp.where(local >= held, held + 1, local))
    slots = row * span + column
    info = jnp.stack(
        [
            slots[:, 0],
            slots[:, 1],
            2 * (strip_of[:, 0] + strip_of[:, 1]),
            2 * (place[:, 0] + place[:, 1]),
        ]
    )
    force, down, up, edges = bond_call(held, intact.shape[0], points)(info, below, own, above, in_hbm(intact))
    from_above = shifted(down, "strip", -1)
    from_below = shifted(up, "strip", 1)
    tail = slice(3 * held, 3 * held + 6)
    edge = edges + (from_above[tail] + from_below[tail])
    to_last = shifted(edge[0:3], "tile", -1)
    to_first = shifted(edge[3:6], "tile", 1)
    merged = pl.pallas_call(
        functools.partial(merge_kernel, held),
        out_shape=jax.ShapeDtypeStruct((3 * held, points), f32),
        in_specs=[VMEM] * 5,
        out_specs=VMEM,
        compiler_params=limit(1),
        name="merge_forces",
    )(force, from_above, from_below, to_first, to_last)
    return jnp.transpose(merged.reshape(3, held, points), (1, 0, 2))


def solution(mesh):
    placed = P(("strip", "tile"), None, None)
    return jax.shard_map(
        on_device,
        mesh=mesh,
        in_specs=(placed, placed, P(("strip", "tile"), None), placed),
        out_specs=placed,
        check_vma=False,
    )
```

time: 103 us -> 60.9 us (0.59)
  the two profiles are of different devices: /device:TPU:196 before, /device:TPU:518 now
where the time goes in v1:
time: 60.9 us; the launch traced here: 60.6 us
  starting transfers between devices  25.4 us (42%)
  Pallas kernels  19 us (31%)
  waiting for transfers between devices  15.4 us (25%)
  other arithmetic  0.72 us (1%)
    ppermute x8, starting transfers between devices, shifted(): lax.ppermute(value, axis, [(i, i + step) for i in range(first, last)])  25.4 us
    pallas_call x1, Pallas kernels, on_device(): bond_call(held, intact.shape[0], points)  17.4 us
    ppermute x8, waiting for transfers between devices, shifted(): lax.ppermute(value, axis, [(i, i + step) for i in range(first, last)])  15.4 us
  transfers between devices with their start and end apart: 8, of which 6 were waited for; matrix products, arithmetic and copies ran while one was open for 1% of the time, Pallas kernels for 0%

profile of v1, /device:TPU:518, one launch (start us, length us, event | category | flops | bytes accessed | tf_op | source)
XLA Modules:
  0.0 60.6 jit_solution(8172551137855347875)
XLA Ops:
  0.0 0.9 %pack_payload.1 = (f32[304,128]{1,0:T(8,128)S(1)}, f32[6,128]{1,0:T(8,128)S(1)}, f32[6,128]{1,0:T(8,128)S(1)}) custom-call(f32[144,128]{1,0:T(8,128)} %bitcast.17, f32[144,128]{1,0:T(8,128)} %bitcast.18), custom_call_target="tpu_custom_call" | custom-call | tf_op jit(solution)/shard_map/pack_payload/pallas_call | solution.py:237
  0.9 1.9 %collective-permute-start = (f32[6,128]{1,0:T(8,128)S(1)}, f32[6,128]{1,0:T(8,128)S(1)}, u32[]{:S(2)}, u32[]{:S(2)}) collective-permute-start(f32[6,128]{1,0:T(8,128)S(1)} %get-tuple-element.13), channel_id=1, source_target_pairs={{0,1},{1,2},{2,3},{3,4},{4,5},{5,6},{6,7},{7,8},{8,9},{9,10},{10,1... | collective-permute-start | bytes 9224 | tf_op jit(solution)/shard_map/ppermute | solution.py:24
  2.9 5.8 %collective-permute-start.1 = (f32[6,128]{1,0:T(8,128)S(1)}, f32[6,128]{1,0:T(8,128)S(1)}, u32[]{:S(2)}, u32[]{:S(2)}) collective-permute-start(f32[6,128]{1,0:T(8,128)S(1)} %get-tuple-element.14), channel_id=1, source_target_pairs={{1,0},{2,1},{3,2},{4,3},{5,4},{6,5},{7,6},{8,7},{9,8},{10,9},{11,1... | collective-permute-start | bytes 9224 | tf_op jit(solution)/shard_map/ppermute | solution.py:24
  8.6 0.7 %fusion.1 = (s32[64,2]{0,1:T(2,128)S(1)}, s32[64,2]{0,1:T(2,128)S(1)}, s32[64,2]{0,1:T(2,128)S(1)}) fusion(s32[]{:T(128)S(6)} %mul.37, s32[]{:T(128)S(6)} %axis_index.23, s32[64,2]{0,1:T(2,128)} %param.6), kind=kLoop, calls=%fused_computation.7 | loop fusion | flops 2688 | bytes 2056 | tf_op jit(solution)/shard_map/add | solution.py:267
  9.4 0.0 collective-permute-done.left
  9.4 0.6 collective-permute-done.1.right
  9.9 3.7 %collective-permute-start.3 = (f32[304,128]{1,0:T(8,128)S(1)}, f32[304,128]{1,0:T(8,128)S(1)}, u32[]{:S(2)}, u32[]{:S(2)}) collective-permute-start(f32[304,128]{1,0:T(8,128)S(1)} %frame_payload.1.own), channel_id=1, source_target_pairs={{64,0},{128,64},{192,128},{256,192},{320,256},{384,320},{448,384},... | collective-permute-start | bytes 466952 | tf_op jit(solution)/shard_map/ppermute | solution.py:24
  13.6 2.2 %collective-permute-start.2 = (f32[304,128]{1,0:T(8,128)S(1)}, f32[304,128]{1,0:T(8,128)S(1)}, u32[]{:S(2)}, u32[]{:S(2)}) collective-permute-start(f32[304,128]{1,0:T(8,128)S(1)} %frame_payload.1.own), channel_id=1, source_target_pairs={{0,64},{64,128},{128,192},{192,256},{256,320},{320,384},{384,448},... | collective-permute-start | bytes 466952 | tf_op jit(solution)/shard_map/ppermute | solution.py:24
  15.8 1.5 %collective-permute-done.3.above = f32[304,128]{1,0:T(8,128)S(1)} collective-permute-done((f32[304,128]{1,0:T(8,128)S(1)}, f32[304,128]{1,0:T(8,128)S(1)}, u32[]{:S(2)}, u32[]{:S(2)}) %collective-permute-start.3) | collective-permute-done | bytes 155680 | tf_op jit(solution)/shard_map/ppermute | solution.py:24
  17.3 4.7 %collective-permute-done.2.below = f32[304,128]{1,0:T(8,128)S(1)} collective-permute-done((f32[304,128]{1,0:T(8,128)S(1)}, f32[304,128]{1,0:T(8,128)S(1)}, u32[]{:S(2)}, u32[]{:S(2)}) %collective-permute-start.2) | collective-permute-done | bytes 155680 | tf_op jit(solution)/shard_map/ppermute | solution.py:24
  21.9 17.4 %bond_forces.1 = (f32[144,128]{1,0:T(8,128)S(1)}, f32[152,128]{1,0:T(8,128)S(1)}, f32[152,128]{1,0:T(8,128)S(1)}, f32[6,128]{1,0:T(8,128)S(1)}) custom-call(s32[4,64]{1,0:T(4,128)S(1)} %pad_add_fusion.info, f32[304,128]{1,0:T(8,128)S(1)} %collective-permute-done.2.below, f32[304,128]{1,0:T(8,128)S(1)} %frame_payload.1.own, ...), custom_call_target="tpu_custom_call" | custom-call | tf_op jit(solution)/shard_map/bond_forces/pallas_call | solution.py:276
  39.3 1.9 %collective-permute-start.4 = (f32[152,128]{1,0:T(8,128)S(1)}, f32[152,128]{1,0:T(8,128)S(1)}, u32[]{:S(2)}, u32[]{:S(2)}) collective-permute-start(f32[152,128]{1,0:T(8,128)S(1)} %get-tuple-element.16), channel_id=1, source_target_pairs={{64,0},{128,64},{192,128},{256,192},{320,256},{384,320},{448,384},... | collective-permute-start | bytes 233480 | tf_op jit(solution)/shard_map/ppermute | solution.py:24
  41.3 3.9 %collective-permute-start.5 = (f32[152,128]{1,0:T(8,128)S(1)}, f32[152,128]{1,0:T(8,128)S(1)}, u32[]{:S(2)}, u32[]{:S(2)}) collective-permute-start(f32[152,128]{1,0:T(8,128)S(1)} %get-tuple-element.17), channel_id=1, source_target_pairs={{0,64},{64,128},{128,192},{192,256},{256,320},{320,384},{384,448},... | collective-permute-start | bytes 233480 | tf_op jit(solution)/shard_map/ppermute | solution.py:24
  45.2 0.4 collective-permute-done.4.from_above
  45.6 3.1 %collective-permute-done.5.from_below = f32[152,128]{1,0:T(8,128)S(1)} collective-permute-done((f32[152,128]{1,0:T(8,128)S(1)}, f32[152,128]{1,0:T(8,128)S(1)}, u32[]{:S(2)}, u32[]{:S(2)}) %collective-permute-start.5) | collective-permute-done | bytes 77856 | tf_op jit(solution)/shard_map/ppermute | solution.py:24
  48.8 4.1 %collective-permute-start.7 = (f32[3,128]{1,0:T(4,128)S(1)}, f32[3,128]{1,0:T(4,128)S(1)}, u32[]{:S(2)}, u32[]{:S(2)}) collective-permute-start(f32[3,128]{1,0:T(4,128)S(1)} %get-tuple-element.21), channel_id=1, source_target_pairs={{1,0},{2,1},{3,2},{4,3},{5,4},{6,5},{7,6},{8,7},{9,8},{10,9},{11,1... | collective-permute-start | bytes 4616 | tf_op jit(solution)/shard_map/ppermute | solution.py:24
  52.9 1.9 %collective-permute-start.6 = (f32[3,128]{1,0:T(4,128)S(1)}, f32[3,128]{1,0:T(4,128)S(1)}, u32[]{:S(2)}, u32[]{:S(2)}) collective-permute-start(f32[3,128]{1,0:T(4,128)S(1)} %get-tuple-element.22), channel_id=1, source_target_pairs={{0,1},{1,2},{2,3},{3,4},{4,5},{5,6},{6,7},{7,8},{8,9},{9,10},{10,1... | collective-permute-start | bytes 4616 | tf_op jit(solution)/shard_map/ppermute | solution.py:24
  54.9 0.0 collective-permute-done.7.to_last
  54.9 5.1 %collective-permute-done.6.to_first = f32[3,128]{1,0:T(4,128)S(1)} collective-permute-done((f32[3,128]{1,0:T(4,128)S(1)}, f32[3,128]{1,0:T(4,128)S(1)}, u32[]{:S(2)}, u32[]{:S(2)}) %collective-permute-start.6) | collective-permute-done | bytes 1568 | tf_op jit(solution)/shard_map/ppermute | solution.py:24
  59.9 0.7 %merge_forces.1 = f32[144,128]{1,0:T(8,128)} custom-call(f32[144,128]{1,0:T(8,128)S(1)} %get-tuple-element.15.force, f32[152,128]{1,0:T(8,128)S(1)} %collective-permute-done.4.from_above, f32[152,128]{1,0:T(8,128)S(1)} %collective-permute-done.5.from_below, f32[3,128]{1,0:T(4,128)S(1)} %collective-permute-done.6.to_first, ...), custom_call_target="tpu_custom_call" | custom-call | tf_op jit(solution)/shard_map/merge_forces/pallas_call | solution.py:283
  (6 shorter events, 0.0 us)
Async XLA Ops:
  0.9 8.4 %collective-permute-start = (f32[6,128]{1,0:T(8,128)S(1)}, f32[6,128]{1,0:T(8,128)S(1)}, u32[]{:S(2)}, u32[]{:S(2)}) collective-permute-start(f32[6,128]{1,0:T(8,128)S(1)} %get-tuple-element.13), channel_id=1, source_target_pairs={{0,1},{1,2},{2,3},{3,4},{4,5},{5,6},{6,7},{7,8},{8,9},{9,10},{10,1... | collective-permute-start | bytes 9224 | tf_op jit(solution)/shard_map/ppermute | solution.py:24
  2.9 7.1 %collective-permute-start.1 = (f32[6,128]{1,0:T(8,128)S(1)}, f32[6,128]{1,0:T(8,128)S(1)}, u32[]{:S(2)}, u32[]{:S(2)}) collective-permute-start(f32[6,128]{1,0:T(8,128)S(1)} %get-tuple-element.14), channel_id=1, source_target_pairs={{1,0},{2,1},{3,2},{4,3},{5,4},{6,5},{7,6},{8,7},{9,8},{10,9},{11,1... | collective-permute-start | bytes 9224 | tf_op jit(solution)/shard_map/ppermute | solution.py:24
  9.9 7.4 %collective-permute-start.3 = (f32[304,128]{1,0:T(8,128)S(1)}, f32[304,128]{1,0:T(8,128)S(1)}, u32[]{:S(2)}, u32[]{:S(2)}) collective-permute-start(f32[304,128]{1,0:T(8,128)S(1)} %frame_payload.1.own), channel_id=1, source_target_pairs={{64,0},{128,64},{192,128},{256,192},{320,256},{384,320},{448,384},... | collective-permute-start | bytes 466952 | tf_op jit(solution)/shard_map/ppermute | solution.py:24
  13.6 8.3 %collective-permute-start.2 = (f32[304,128]{1,0:T(8,128)S(1)}, f32[304,128]{1,0:T(8,128)S(1)}, u32[]{:S(2)}, u32[]{:S(2)}) collective-permute-start(f32[304,128]{1,0:T(8,128)S(1)} %frame_payload.1.own), channel_id=1, source_target_pairs={{0,64},{64,128},{128,192},{192,256},{256,320},{320,384},{384,448},... | collective-permute-start | bytes 466952 | tf_op jit(solution)/shard_map/ppermute | solution.py:24
  39.3 6.3 %collective-permute-start.4 = (f32[152,128]{1,0:T(8,128)S(1)}, f32[152,128]{1,0:T(8,128)S(1)}, u32[]{:S(2)}, u32[]{:S(2)}) collective-permute-start(f32[152,128]{1,0:T(8,128)S(1)} %get-tuple-element.16), channel_id=1, source_target_pairs={{64,0},{128,64},{192,128},{256,192},{320,256},{384,320},{448,384},... | collective-permute-start | bytes 233480 | tf_op jit(solution)/shard_map/ppermute | solution.py:24
  41.3 7.5 %collective-permute-start.5 = (f32[152,128]{1,0:T(8,128)S(1)}, f32[152,128]{1,0:T(8,128)S(1)}, u32[]{:S(2)}, u32[]{:S(2)}) collective-permute-start(f32[152,128]{1,0:T(8,128)S(1)} %get-tuple-element.17), channel_id=1, source_target_pairs={{0,64},{64,128},{128,192},{192,256},{256,320},{320,384},{384,448},... | collective-permute-start | bytes 233480 | tf_op jit(solution)/shard_map/ppermute | solution.py:24
  48.8 6.1 %collective-permute-start.7 = (f32[3,128]{1,0:T(4,128)S(1)}, f32[3,128]{1,0:T(4,128)S(1)}, u32[]{:S(2)}, u32[]{:S(2)}) collective-permute-start(f32[3,128]{1,0:T(4,128)S(1)} %get-tuple-element.21), channel_id=1, source_target_pairs={{1,0},{2,1},{3,2},{4,3},{5,4},{6,5},{7,6},{8,7},{9,8},{10,9},{11,1... | collective-permute-start | bytes 4616 | tf_op jit(solution)/shard_map/ppermute | solution.py:24
  52.9 7.0 %collective-permute-start.6 = (f32[3,128]{1,0:T(4,128)S(1)}, f32[3,128]{1,0:T(4,128)S(1)}, u32[]{:S(2)}, u32[]{:S(2)}) collective-permute-start(f32[3,128]{1,0:T(4,128)S(1)} %get-tuple-element.22), channel_id=1, source_target_pairs={{0,1},{1,2},{2,3},{3,4},{4,5},{5,6},{6,7},{7,8},{8,9},{9,10},{10,1... | collective-permute-start | bytes 4616 | tf_op jit(solution)/shard_map/ppermute | solution.py:24

commit v2 on v1

v2 whole, which is shorter than its diff:
```python
import functools

import jax
import jax.numpy as jnp
from jax import lax
from jax.experimental import pallas as pl
from jax.experimental.pallas import tpu as pltpu
from jax.sharding import PartitionSpec as P

HORIZON = 3.0
STIFFNESS = 2.0
ONSET = 0.02
FINAL = 0.05

GROUP = 8
EDGES = 4
VMEM = pl.BlockSpec(memory_space=pltpu.VMEM)
HBM = pl.BlockSpec(memory_space=pltpu.HBM)
SMEM = pl.BlockSpec(memory_space=pltpu.SMEM)


def shifted(value, axis, step):
    count = lax.axis_size(axis)
    first, last = max(0, -step), min(count, count - step)
    return lax.ppermute(value, axis, [(i, i + step) for i in range(first, last)])


def in_hbm(value):
    return pltpu.with_memory_space_constraint(value, pltpu.HBM)


def padded_rows(rows):
    return (rows + 7) // 8 * 8


def pack_kernel(held, coords, displacement, out, edges, arrived):
    rows = 3 * held
    copies = [
        pltpu.make_async_copy(source, out.at[pl.ds(i * rows, rows)], arrived.at[i])
        for i, source in enumerate((coords, displacement))
    ]
    for copy in copies:
        copy.start()
    for copy in copies:
        copy.wait()
    for i, t in enumerate((0, held - 1)):
        edges[6 * i : 6 * i + 6] = out[pl.ds(t, 6, stride=held)]


def frame_kernel(held, payload, near, far, out):
    end = 6 * held
    out[end : end + 12] = near[...]
    out[end + 12 : end + 24] = far[...]


def stage_kernel(payload, bonds, out, arrived):
    copy = pltpu.make_async_copy(bonds, out, arrived)
    copy.start()
    copy.wait()


def pieces(value):
    first = value.astype(jnp.bfloat16).astype(jnp.float32)
    rest = value - first
    second = rest.astype(jnp.bfloat16).astype(jnp.float32)
    return first, second, rest - second


def middle_of(mid_x, mid_y, mid_z, points):
    row = lax.broadcasted_iota(jnp.int32, (8, points), 0)
    return jnp.where(
        row == 0, mid_x, jnp.where(row == 1, mid_y, jnp.where(row == 2, mid_z, 0.0))
    )


def side_rows(here, row):
    moved = pltpu.roll(here, 5, axis=0)
    now = here + moved
    low = row < 3
    square = jnp.sum(jnp.where(low, here * here, 0.0), axis=0, keepdims=True)
    growth = jnp.sum(jnp.where(low, moved * (here + now), 0.0), axis=0, keepdims=True)
    return moved, now, square, growth


def now_rows(now, row):
    first = now.astype(jnp.bfloat16).astype(jnp.float32)
    second = now - first
    top = jnp.where(row < 3, first, jnp.where(row == 3, 1.0, 0.0))
    rows = jnp.concatenate([top, jnp.where(row < 3, second, 0.0)], axis=0)
    rows = rows.astype(jnp.bfloat16)
    return jnp.concatenate([rows, rows], axis=1)


def pair_squares(here_a, here_b):
    points = here_a.shape[-1]
    row = lax.broadcasted_iota(jnp.int32, (8, points), 0)
    _, _, square_a, growth_a = side_rows(here_a, row)
    moved_b, now_b, square_b, growth_b = side_rows(here_b, row)

    six, seven = row == 6, row == 7
    left = jnp.where(row < 6, -2.0 * here_a, jnp.where(six, square_a, growth_a))
    l1, l2, l3 = pieces(left)

    def ones(value):
        return jnp.where(row < 6, value, jnp.where(six, 1.0, 0.0))

    o1, o2 = ones(l1), ones(l2)
    lhs = jnp.concatenate([l1, l2, l3, o1, o2, o1], axis=0).astype(jnp.bfloat16)

    shifted_b = pltpu.roll(now_b, 3, axis=0)
    right_ref = jnp.where(row < 3, here_b, jnp.where(six, square_b, 0.0))
    right_gain = jnp.where(
        row < 3, moved_b, jnp.where(row < 6, shifted_b, jnp.where(six, growth_b, 0.0))
    )

    def stack(value, at_six, at_seven):
        p1, p2, p3 = pieces(value)
        base = jnp.where(six, at_six, jnp.where(seven, at_seven, p1))
        mixed = jnp.where(six, p1, p2)
        return jnp.concatenate([base, base, base, mixed, p2, p3], axis=0)

    rhs = jnp.concatenate([stack(right_ref, 1.0, 0.0), stack(right_gain, 0.0, 1.0)], axis=1)
    return lax.dot_general(
        lhs, rhs.astype(jnp.bfloat16), (((0,), (0,)), ((), ())), preferred_element_type=jnp.float32
    )


def pull_of(both, bond_mask):
    points = bond_mask.shape[-1]
    ref2, gain2 = both[:, :points], both[:, points:]
    now2 = jnp.maximum(ref2 + gain2, 1e-7)
    per_ref, per_now = lax.rsqrt(ref2), lax.rsqrt(now2)
    length_ref, length_now = ref2 * per_ref, now2 * per_now
    stretch = (gain2 * per_ref) * (1.0 / (length_now + length_ref))
    influence = jnp.maximum(1.0 - length_ref, 0.0)
    soften = jnp.clip(FINAL - stretch, 0.0, FINAL - ONSET)
    pull = ((stretch * influence) * soften) * (per_now * bond_mask.astype(jnp.float32))
    high = pull.astype(jnp.bfloat16)
    low = (pull - high.astype(jnp.float32)).astype(jnp.bfloat16)
    return high, low


def gather_pair(now_a, now_b, high, low):
    row = lax.broadcasted_iota(jnp.int32, now_a.shape, 0)
    on_b = jnp.dot(
        now_rows(now_a, row),
        jnp.concatenate([high, low], axis=0),
        preferred_element_type=jnp.float32,
    )
    on_a = lax.dot_general(
        now_rows(now_b, row),
        jnp.concatenate([high, low], axis=1),
        (((1,), (1,)), ((), ())),
        preferred_element_type=jnp.float32,
    )
    sum_a, sum_b = on_a[0:8] + on_a[8:16], on_b[0:8] + on_b[8:16]
    scale = STIFFNESS / (FINAL - ONSET)
    return scale * (sum_a - now_a * sum_a[3:4]), scale * (sum_b - now_b * sum_b[3:4])


def bond_kernel(
    mid_z, held, info, below, own, above, bonds, force, down, up, edges,
    table, total, squares0, squares1, pulls0, pulls1
):
    count, points, _ = bonds.shape
    steps = count // GROUP
    span = held + EDGES
    for r, payload in enumerate((below, own, above)):
        for t in range(held):
            table[r * span + t, 0:6] = payload[pl.ds(t, 6, stride=held)]
        for i in range(EDGES):
            at = 6 * (held + i)
            table[r * span + held + i, 0:6] = payload[at : at + 6]
    total[...] = jnp.zeros_like(total)

    def ends(k):
        mid_x = info[2, k].astype(jnp.float32) + 1.5
        mid_y = info[3, k].astype(jnp.float32) + 1.5
        middle = middle_of(mid_x, mid_y, mid_z, points)
        return (table[info[0, k]] - middle) * (1.0 / HORIZON), (
            table[info[1, k]] - middle
        ) * (1.0 / HORIZON)

    def measure(step, squares):
        for g in range(GROUP):
            squares[g] = pair_squares(*ends(step * GROUP + g))

    def visit(step, squares, pulls):
        for g in range(GROUP):
            high, low = pull_of(squares[g], bonds[step * GROUP + g])
            pulls[g, 0:points], pulls[g, points:] = high, low

    def collect(step, pulls):
        gains = []
        for g in range(GROUP):
            k = step * GROUP + g
            here_a, here_b = ends(k)
            gain_a, gain_b = gather_pair(
                here_a + pltpu.roll(here_a, 5, axis=0),
                here_b + pltpu.roll(here_b, 5, axis=0),
                pulls[g, 0:points],
                pulls[g, points:],
            )
            gains.append((info[0, k], gain_a))
            gains.append((info[1, k], gain_b))
        for slot, gain in gains:
            total[slot] += gain

    measure(0, squares0)
    measure(1, squares1)
    visit(0, squares0, pulls0)

    @pl.loop(1, steps // 2)
    def _(twice):
        step = 2 * twice
        measure(step, squares0)
        visit(step - 1, squares1, pulls1)
        collect(step - 2, pulls0)
        measure(step + 1, squares1)
        visit(step, squares0, pulls0)
        collect(step - 1, pulls1)

    visit(steps - 1, squares1, pulls1)
    collect(steps - 2, pulls0)
    collect(steps - 1, pulls1)

    for r, out in enumerate((down, force, up)):
        for t in range(held):
            out[pl.ds(t, 3, stride=held)] = total[r * span + t, 0:3]
    for r, out, at in ((0, down, 3 * held), (1, edges, 0), (2, up, 3 * held)):
        for i in range(EDGES):
            out[at + 3 * i : at + 3 * i + 3] = total[r * span + held + i, 0:3]
    for out in (down, up):
        end = 3 * span
        if end < out.shape[0]:
            out[end:] = jnp.zeros((out.shape[0] - end, out.shape[1]), jnp.float32)


def merge_kernel(held, force, from_above, from_below, near, far, out):
    rows = 3 * held
    out[...] = force[...] + (from_above[0:rows] + from_below[0:rows])
    out[pl.ds(0, 3, stride=held)] += near[0:3] + far[0:3]
    out[pl.ds(held - 1, 3, stride=held)] += near[3:6] + far[3:6]


def limit(mebibytes):
    return pltpu.CompilerParams(vmem_limit_bytes=mebibytes * 1024 * 1024)


def bond_call(held, count, points):
    span = held + EDGES
    f32 = jnp.float32
    sent = jax.ShapeDtypeStruct((padded_rows(3 * span), points), f32)
    return pl.pallas_call(
        functools.partial(bond_kernel, 3.5, held),
        out_shape=(
            jax.ShapeDtypeStruct((3 * held, points), f32),
            sent,
            sent,
            jax.ShapeDtypeStruct((3 * EDGES, points), f32),
        ),
        in_specs=[SMEM] + [VMEM] * 4,
        out_specs=(VMEM,) * 4,
        scratch_shapes=[pltpu.VMEM((3 * span, 8, points), f32)] * 2
        + [pltpu.VMEM((GROUP, points, 2 * points), f32)] * 2
        + [pltpu.VMEM((GROUP, 2 * points, points), jnp.bfloat16)] * 2,
        compiler_params=limit(8),
        name="bond_forces",
    )


def swapped(value, axis, phase):
    pairs = []
    for i in range(phase, lax.axis_size(axis) - 1, 2):
        pairs += [(i, i + 1), (i + 1, i)]
    return lax.ppermute(value, axis, pairs)


def on_device(coords, displacement, pairs, intact):
    held, _, points = coords.shape
    span = held + EDGES
    strip_tiles = held * lax.axis_size("tile")
    f32 = jnp.float32

    packed = jax.ShapeDtypeStruct((padded_rows(6 * span), points), f32)
    inside, ends = pl.pallas_call(
        functools.partial(pack_kernel, held),
        out_shape=(packed, jax.ShapeDtypeStruct((12, points), f32)),
        in_specs=[HBM] * 2,
        out_specs=(VMEM,) * 2,
        scratch_shapes=[pltpu.SemaphoreType.DMA((2,))],
        compiler_params=limit(1),
        name="pack_payload",
    )(
        in_hbm(jnp.transpose(coords, (1, 0, 2)).reshape(-1, points)),
        in_hbm(jnp.transpose(displacement, (1, 0, 2)).reshape(-1, points)),
    )
    near = swapped(ends, "tile", 0)
    far = swapped(ends, "tile", 1)

    tile_index = lax.axis_index("tile")
    strip_of, place = pairs // strip_tiles, pairs % strip_tiles
    row = strip_of - lax.axis_index("strip") + 1
    local = place - tile_index * held
    odd = tile_index % 2
    column = jnp.where(
        local < 0, held + 3 - 2 * odd, jnp.where(local >= held, held + 2 * odd, local)
    )
    slots = row * span + column
    info = jnp.stack(
        [
            slots[:, 0],
            slots[:, 1],
            2 * (strip_of[:, 0] + strip_of[:, 1]),
            2 * (place[:, 0] + place[:, 1]),
        ]
    )

    own = pl.pallas_call(
        functools.partial(frame_kernel, held),
        out_shape=packed,
        in_specs=[VMEM] * 3,
        out_specs=VMEM,
        input_output_aliases={0: 0},
        compiler_params=limit(1),
        name="frame_payload",
    )(inside, near, far)
    below = shifted(own, "strip", 1)
    above = shifted(own, "strip", -1)
    bonds = pl.pallas_call(
        stage_kernel,
        out_shape=jax.ShapeDtypeStruct(intact.shape, intact.dtype),
        in_specs=[VMEM, HBM],
        out_specs=VMEM,
        scratch_shapes=[pltpu.SemaphoreType.DMA],
        compiler_params=limit(1),
        cost_estimate=pl.CostEstimate(
            flops=0, bytes_accessed=4 * intact.size, transcendentals=0
        ),
        name="stage_bonds",
    )(own, in_hbm(intact))

    force, down, up, edges = bond_call(held, intact.shape[0], points)(
        info, below, own, above, bonds
    )
    from_above = shifted(down, "strip", -1)
    from_below = shifted(up, "strip", 1)
    tail = slice(3 * held, 3 * span)
    edge = edges + (from_above[tail] + from_below[tail])
    near_force = swapped(edge[0:6], "tile", 0)
    far_force = swapped(edge[6:12], "tile", 1)
    merged = pl.pallas_call(
        functools.partial(merge_kernel, held),
        out_shape=jax.ShapeDtypeStruct((3 * held, points), f32),
        in_specs=[VMEM] * 5,
        out_specs=VMEM,
        compiler_params=limit(1),
        name="merge_forces",
    )(force, from_above, from_below, near_force, far_force)
    return jnp.transpose(merged.reshape(3, held, points), (1, 0, 2))


def solution(mesh):
    placed = P(("strip", "tile"), None, None)
    return jax.shard_map(
        on_device,
        mesh=mesh,
        in_specs=(placed, placed, P(("strip", "tile"), None), placed),
        out_specs=placed,
        check_vma=False,
    )
```

time: 60.9 us -> 46.2 us (0.76)
  Pallas kernels: 19 us -> 10.7 us
  waiting for transfers between devices: 15.4 us -> 11 us
  starting transfers between devices: 25.4 us -> 23.3 us
    ppermute x8 -> x4, starting transfers between devices: 25.4 us -> 11.7 us  [shifted(): lax.ppermute(value, axis, [(i, i + step) for i in range(first, last)])]
    ppermute x0 -> x4, starting transfers between devices: none -> 11.6 us  [swapped(): return lax.ppermute(value, axis, pairs)]
    pallas_call x2 -> x3, Pallas kernels: 18.3 us -> 10 us  [the longest x1 6.88 us: on_device(): bond_call(held, intact.shape[0], points)(info, below, own, above, bonds)]
    ppermute x8 -> x4, waiting for transfers between devices: 15.4 us -> 8.2 us  [shifted(): lax.ppermute(value, axis, [(i, i + step) for i in range(first, last)])]
    ppermute x0 -> x4, waiting for transfers between devices: none -> 2.79 us  [swapped(): return lax.ppermute(value, axis, pairs)]
  transfers between devices with their start and end apart: 8 -> 8, of which waited for: 6 -> 5; matrix products, arithmetic and copies ran while one was open for 1% -> 2% of each run, Pallas kernels for 0% -> 5%
where the time goes in v2:
time: 46.2 us; the launch traced here: 45.8 us
  starting transfers between devices  23.3 us (50%)
  waiting for transfers between devices  11 us (24%)
  Pallas kernels  10.7 us (23%)
  other arithmetic  0.72 us (2%)
    ppermute x4, starting transfers between devices, shifted(): lax.ppermute(value, axis, [(i, i + step) for i in range(first, last)])  11.7 us
    ppermute x4, starting transfers between devices, swapped(): return lax.ppermute(value, axis, pairs)  11.6 us
    ppermute x4, waiting for transfers between devices, shifted(): lax.ppermute(value, axis, [(i, i + step) for i in range(first, last)])  8.2 us
    pallas_call x1, Pallas kernels, on_device(): bond_call(held, intact.shape[0], points)(info, below, own, above, bonds)  6.88 us
    ppermute x4, waiting for transfers between devices, swapped(): return lax.ppermute(value, axis, pairs)  2.79 us
    pallas_call x1, Pallas kernels, on_device(): pl.pallas_call(stage_kernel, out_shape=jax.ShapeDtypeStruct(intact.shape,...  2.2 us
    pallas_call x1, Pallas kernels, on_device(): pl.pallas_call(functools.partial(pack_kernel, held), out_shape=(packed, j...  0.94 us
  transfers between devices with their start and end apart: 8, of which 5 were waited for; matrix products, arithmetic and copies ran while one was open for 2% of the time, Pallas kernels for 5%

profile of v2, /device:TPU:518, one launch (start us, length us, event | category | flops | bytes accessed | tf_op | source)
XLA Modules:
  0.0 45.8 jit_solution(4340984328250604580)
XLA Ops:
  0.0 0.9 %pack_payload.1 = (f32[312,128]{1,0:T(8,128)S(1)}, f32[12,128]{1,0:T(8,128)S(1)}) custom-call(f32[144,128]{1,0:T(8,128)} %bitcast.17, f32[144,128]{1,0:T(8,128)} %bitcast.18), custom_call_target="tpu_custom_call" | custom-call | tf_op jit(solution)/shard_map/pack_payload/pallas_call | solution.py:286
  0.9 5.1 %collective-permute-start.1 = (f32[12,128]{1,0:T(8,128)S(1)}, f32[12,128]{1,0:T(8,128)S(1)}, u32[]{:S(2)}, u32[]{:S(2)}) collective-permute-start(f32[12,128]{1,0:T(8,128)S(1)} %get-tuple-element.12), channel_id=1, source_target_pairs={{1,2},{2,1},{3,4},{4,3},{5,6},{6,5},{7,8},{8,7},{9,10},{10,9},{11,... | collective-permute-start | bytes 18440 | tf_op jit(solution)/shard_map/ppermute | solution.py:276
  6.0 1.9 %collective-permute-start = (f32[12,128]{1,0:T(8,128)S(1)}, f32[12,128]{1,0:T(8,128)S(1)}, u32[]{:S(2)}, u32[]{:S(2)}) collective-permute-start(f32[12,128]{1,0:T(8,128)S(1)} %get-tuple-element.12), channel_id=1, source_target_pairs={{0,1},{1,0},{2,3},{3,2},{4,5},{5,4},{6,7},{7,6},{8,9},{9,8},{10,11... | collective-permute-start | bytes 18440 | tf_op jit(solution)/shard_map/ppermute | solution.py:276
  8.0 0.7 %fusion.1 = (s32[64,2]{0,1:T(2,128)S(1)}, s32[64,2]{0,1:T(2,128)S(1)}, s32[64,2]{0,1:T(2,128)S(1)}) fusion(s32[]{:T(128)S(6)} %add.52, s32[]{:T(128)S(6)} %sub.26, s32[]{:T(128)S(6)} %mul.41, s32[]{:T(128)S(6)} %axis_index.23, s32[64,2]{0,1:T(2,128)} %param.6), kind=kLoop, calls=%fused_computation.7 | loop fusion | flops 2688 | bytes 2064 | tf_op jit(solution)/shard_map/add | solution.py:309
  8.7 0.0 collective-permute-done.1.far
  8.7 0.4 collective-permute-done.near
  9.1 3.7 %collective-permute-start.3 = (f32[312,128]{1,0:T(8,128)S(1)}, f32[312,128]{1,0:T(8,128)S(1)}, u32[]{:S(2)}, u32[]{:S(2)}) collective-permute-start(f32[312,128]{1,0:T(8,128)S(1)} %frame_payload.1.payload.own), channel_id=1, source_target_pairs={{64,0},{128,64},{192,128},{256,192},{320,256},{384,320},{448,384},... | collective-permute-start | bytes 479240 | tf_op jit(solution)/shard_map/ppermute | solution.py:25
  12.8 2.2 %collective-permute-start.2 = (f32[312,128]{1,0:T(8,128)S(1)}, f32[312,128]{1,0:T(8,128)S(1)}, u32[]{:S(2)}, u32[]{:S(2)}) collective-permute-start(f32[312,128]{1,0:T(8,128)S(1)} %frame_payload.1.payload.own), channel_id=1, source_target_pairs={{0,64},{64,128},{128,192},{192,256},{256,320},{320,384},{384,448},... | collective-permute-start | bytes 479240 | tf_op jit(solution)/shard_map/ppermute | solution.py:25
  15.0 2.2 %stage_bonds.1.bonds = s32[64,128,128]{2,1,0:T(8,128)S(1)} custom-call(f32[312,128]{1,0:T(8,128)S(1)} %frame_payload.1.payload.own, s32[64,128,128]{2,1,0:T(8,128)} %bonds.1), custom_call_target="tpu_custom_call" | custom-call | bytes 4194304 | tf_op jit(solution)/shard_map/stage_bonds/pallas_call | solution.py:330
  17.2 0.0 collective-permute-done.3.above
  17.2 4.6 %collective-permute-done.2.below = f32[312,128]{1,0:T(8,128)S(1)} collective-permute-done((f32[312,128]{1,0:T(8,128)S(1)}, f32[312,128]{1,0:T(8,128)S(1)}, u32[]{:S(2)}, u32[]{:S(2)}) %collective-permute-start.2) | collective-permute-done | bytes 159776 | tf_op jit(solution)/shard_map/ppermute | solution.py:25
  21.8 6.9 %bond_forces.1 = (f32[144,128]{1,0:T(8,128)S(1)}, f32[160,128]{1,0:T(8,128)S(1)}, f32[160,128]{1,0:T(8,128)S(1)}, f32[12,128]{1,0:T(8,128)S(1)}) custom-call(s32[4,64]{1,0:T(4,128)S(1)} %pad_add_fusion.info, f32[312,128]{1,0:T(8,128)S(1)} %collective-permute-done.2.below, f32[312,128]{1,0:T(8,128)S(1)} %frame_payload.1.payload.own, ...), custom_call_target="tpu_custom_call" | custom-call | tf_op jit(solution)/shard_map/bond_forces/pallas_call | solution.py:343
  28.7 1.9 %collective-permute-start.4 = (f32[160,128]{1,0:T(8,128)S(1)}, f32[160,128]{1,0:T(8,128)S(1)}, u32[]{:S(2)}, u32[]{:S(2)}) collective-permute-start(f32[160,128]{1,0:T(8,128)S(1)} %get-tuple-element.14), channel_id=1, source_target_pairs={{64,0},{128,64},{192,128},{256,192},{320,256},{384,320},{448,384},... | collective-permute-start | bytes 245768 | tf_op jit(solution)/shard_map/ppermute | solution.py:25
  30.6 3.9 %collective-permute-start.5 = (f32[160,128]{1,0:T(8,128)S(1)}, f32[160,128]{1,0:T(8,128)S(1)}, u32[]{:S(2)}, u32[]{:S(2)}) collective-permute-start(f32[160,128]{1,0:T(8,128)S(1)} %get-tuple-element.15), channel_id=1, source_target_pairs={{0,64},{64,128},{128,192},{192,256},{256,320},{320,384},{384,448},... | collective-permute-start | bytes 245768 | tf_op jit(solution)/shard_map/ppermute | solution.py:25
  34.5 0.5 %collective-permute-done.4.from_above = f32[160,128]{1,0:T(8,128)S(1)} collective-permute-done((f32[160,128]{1,0:T(8,128)S(1)}, f32[160,128]{1,0:T(8,128)S(1)}, u32[]{:S(2)}, u32[]{:S(2)}) %collective-permute-start.4) | collective-permute-done | bytes 81952 | tf_op jit(solution)/shard_map/ppermute | solution.py:25
  35.0 3.1 %collective-permute-done.5.from_below = f32[160,128]{1,0:T(8,128)S(1)} collective-permute-done((f32[160,128]{1,0:T(8,128)S(1)}, f32[160,128]{1,0:T(8,128)S(1)}, u32[]{:S(2)}, u32[]{:S(2)}) %collective-permute-start.5) | collective-permute-done | bytes 81952 | tf_op jit(solution)/shard_map/ppermute | solution.py:25
  38.2 2.7 %collective-permute-start.7 = (f32[6,128]{1,0:T(8,128)S(1)}, f32[6,128]{1,0:T(8,128)S(1)}, u32[]{:S(2)}, u32[]{:S(2)}) collective-permute-start(f32[6,128]{1,0:T(8,128)S(1)} %get-tuple-element.19), channel_id=1, source_target_pairs={{1,2},{2,1},{3,4},{4,3},{5,6},{6,5},{7,8},{8,7},{9,10},{10,9},{11,... | collective-permute-start | bytes 9224 | tf_op jit(solution)/shard_map/ppermute | solution.py:276
  40.9 1.9 %collective-permute-start.6 = (f32[6,128]{1,0:T(8,128)S(1)}, f32[6,128]{1,0:T(8,128)S(1)}, u32[]{:S(2)}, u32[]{:S(2)}) collective-permute-start(f32[6,128]{1,0:T(8,128)S(1)} %get-tuple-element.20), channel_id=1, source_target_pairs={{0,1},{1,0},{2,3},{3,2},{4,5},{5,4},{6,7},{7,6},{8,9},{9,8},{10,11... | collective-permute-start | bytes 9224 | tf_op jit(solution)/shard_map/ppermute | solution.py:276
  42.8 2.4 %collective-permute-done.7.far = f32[6,128]{1,0:T(8,128)S(1)} collective-permute-done((f32[6,128]{1,0:T(8,128)S(1)}, f32[6,128]{1,0:T(8,128)S(1)}, u32[]{:S(2)}, u32[]{:S(2)}) %collective-permute-start.7) | collective-permute-done | bytes 3104 | tf_op jit(solution)/shard_map/ppermute | solution.py:276
  45.2 0.0 collective-permute-done.6.near
  45.2 0.7 %merge_forces.1 = f32[144,128]{1,0:T(8,128)} custom-call(f32[144,128]{1,0:T(8,128)S(1)} %get-tuple-element.13.force, f32[160,128]{1,0:T(8,128)S(1)} %collective-permute-done.4.from_above, f32[160,128]{1,0:T(8,128)S(1)} %collective-permute-done.5.from_below, f32[6,128]{1,0:T(8,128)S(1)} %collective-permute-done.6.near, f32[6,128]{1,0:T(8,128)S(1)} %collective-permute-done.7.far), custom_call_target="tpu_custom_call" | custom-call | tf_op jit(solution)/shard_map/merge_forces/pallas_call | solution.py:352
  (6 shorter events, 0.0 us)
Async XLA Ops:
  0.9 7.8 %collective-permute-start.1 = (f32[12,128]{1,0:T(8,128)S(1)}, f32[12,128]{1,0:T(8,128)S(1)}, u32[]{:S(2)}, u32[]{:S(2)}) collective-permute-start(f32[12,128]{1,0:T(8,128)S(1)} %get-tuple-element.12), channel_id=1, source_target_pairs={{1,2},{2,1},{3,4},{4,3},{5,6},{6,5},{7,8},{8,7},{9,10},{10,9},{11,... | collective-permute-start | bytes 18440 | tf_op jit(solution)/shard_map/ppermute | solution.py:276
  6.0 3.1 %collective-permute-start = (f32[12,128]{1,0:T(8,128)S(1)}, f32[12,128]{1,0:T(8,128)S(1)}, u32[]{:S(2)}, u32[]{:S(2)}) collective-permute-start(f32[12,128]{1,0:T(8,128)S(1)} %get-tuple-element.12), channel_id=1, source_target_pairs={{0,1},{1,0},{2,3},{3,2},{4,5},{5,4},{6,7},{7,6},{8,9},{9,8},{10,11... | collective-permute-start | bytes 18440 | tf_op jit(solution)/shard_map/ppermute | solution.py:276
  9.1 8.1 %collective-permute-start.3 = (f32[312,128]{1,0:T(8,128)S(1)}, f32[312,128]{1,0:T(8,128)S(1)}, u32[]{:S(2)}, u32[]{:S(2)}) collective-permute-start(f32[312,128]{1,0:T(8,128)S(1)} %frame_payload.1.payload.own), channel_id=1, source_target_pairs={{64,0},{128,64},{192,128},{256,192},{320,256},{384,320},{448,384},... | collective-permute-start | bytes 479240 | tf_op jit(solution)/shard_map/ppermute | solution.py:25
  12.8 9.0 %collective-permute-start.2 = (f32[312,128]{1,0:T(8,128)S(1)}, f32[312,128]{1,0:T(8,128)S(1)}, u32[]{:S(2)}, u32[]{:S(2)}) collective-permute-start(f32[312,128]{1,0:T(8,128)S(1)} %frame_payload.1.payload.own), channel_id=1, source_target_pairs={{0,64},{64,128},{128,192},{192,256},{256,320},{320,384},{384,448},... | collective-permute-start | bytes 479240 | tf_op jit(solution)/shard_map/ppermute | solution.py:25
  28.7 6.3 %collective-permute-start.4 = (f32[160,128]{1,0:T(8,128)S(1)}, f32[160,128]{1,0:T(8,128)S(1)}, u32[]{:S(2)}, u32[]{:S(2)}) collective-permute-start(f32[160,128]{1,0:T(8,128)S(1)} %get-tuple-element.14), channel_id=1, source_target_pairs={{64,0},{128,64},{192,128},{256,192},{320,256},{384,320},{448,384},... | collective-permute-start | bytes 245768 | tf_op jit(solution)/shard_map/ppermute | solution.py:25
  30.6 7.5 %collective-permute-start.5 = (f32[160,128]{1,0:T(8,128)S(1)}, f32[160,128]{1,0:T(8,128)S(1)}, u32[]{:S(2)}, u32[]{:S(2)}) collective-permute-start(f32[160,128]{1,0:T(8,128)S(1)} %get-tuple-element.15), channel_id=1, source_target_pairs={{0,64},{64,128},{128,192},{192,256},{256,320},{320,384},{384,448},... | collective-permute-start | bytes 245768 | tf_op jit(solution)/shard_map/ppermute | solution.py:25
  38.2 7.0 %collective-permute-start.7 = (f32[6,128]{1,0:T(8,128)S(1)}, f32[6,128]{1,0:T(8,128)S(1)}, u32[]{:S(2)}, u32[]{:S(2)}) collective-permute-start(f32[6,128]{1,0:T(8,128)S(1)} %get-tuple-element.19), channel_id=1, source_target_pairs={{1,2},{2,1},{3,4},{4,3},{5,6},{6,5},{7,8},{8,7},{9,10},{10,9},{11,... | collective-permute-start | bytes 9224 | tf_op jit(solution)/shard_map/ppermute | solution.py:276
  40.9 4.3 %collective-permute-start.6 = (f32[6,128]{1,0:T(8,128)S(1)}, f32[6,128]{1,0:T(8,128)S(1)}, u32[]{:S(2)}, u32[]{:S(2)}) collective-permute-start(f32[6,128]{1,0:T(8,128)S(1)} %get-tuple-element.20), channel_id=1, source_target_pairs={{0,1},{1,0},{2,3},{3,2},{4,5},{5,4},{6,7},{7,6},{8,9},{9,8},{10,11... | collective-permute-start | bytes 9224 | tf_op jit(solution)/shard_map/ppermute | solution.py:276

commit v3 on v2

--- a/solution.py
+++ b/solution.py
@@ -12,8 +12,10 @@
 ONSET = 0.02
 FINAL = 0.05
 
-GROUP = 8
+GROUP = 2
 EDGES = 4
+ROOM = 80
+ABOVE, BELOW, SAME = 0, 1, 2
 VMEM = pl.BlockSpec(memory_space=pltpu.VMEM)
 HBM = pl.BlockSpec(memory_space=pltpu.HBM)
 SMEM = pl.BlockSpec(memory_space=pltpu.SMEM)
@@ -53,9 +55,46 @@
     out[end + 12 : end + 24] = far[...]
 
 
-def stage_kernel(payload, bonds, out, arrived):
-    copy = pltpu.make_async_copy(bonds, out, arrived)
+def stage_kernel(held, strip_tiles, payload, pairs, intact, bonds, info, arrived):
+    copy = pltpu.make_async_copy(intact, bonds, arrived)
     copy.start()
+    device = lax.div(pairs[0, 0], held)
+    base = device * held
+    strip = lax.div(base, strip_tiles)
+    start = base - strip * strip_tiles
+    odd = device % 2
+
+    def place(k, counts):
+        first, second = pairs[0, k] - base, pairs[1, k] - base
+        half = strip_tiles // 2
+        side = jnp.where(second > half, 1, jnp.where(second < -half, -1, 0))
+        local = second - side * strip_tiles
+        column = jnp.where(
+            local < 0, held + 3 - 2 * odd, jnp.where(local >= held, held + 2 * odd, local)
+        )
+        above, below, same = counts
+        at = jnp.where(
+            side > 0,
+            ABOVE * ROOM + above,
+            jnp.where(side < 0, BELOW * ROOM + below, SAME * ROOM + same),
+        )
+        info[0, at] = first
+        info[1, at] = column
+        info[2, at] = 2 * (2 * strip + side)
+        info[3, at] = 2 * (2 * start + first + local)
+        info[4, at] = k
+        up, down = jnp.where(side > 0, 1, 0), jnp.where(side < 0, 1, 0)
+        return above + up, below + down, same + (1 - up - down)
+
+    zero = jnp.int32(0)
+    counts = lax.fori_loop(0, pairs.shape[1], place, (zero, zero, zero), unroll=4)
+    for kind, count in enumerate(counts):
+        info[5, kind] = count
+        for i in range(2 * GROUP):
+            at = kind * ROOM + count + i
+            info[0, at], info[1, at] = held, held + EDGES
+            for field in (2, 3, 4):
+                info[field, at] = 0
     copy.wait()
 
 
@@ -158,42 +197,47 @@
     return scale * (sum_a - now_a * sum_a[3:4]), scale * (sum_b - now_b * sum_b[3:4])
 
 
-def bond_kernel(
-    mid_z, held, info, below, own, above, bonds, force, down, up, edges,
-    table, total, squares0, squares1, pulls0, pulls1
+def sum_bonds(
+    kind, mid_z, held, info, own, other, bonds,
+    first_table, second_table, first_total, second_total,
+    squares0, squares1, pulls0, pulls1
 ):
-    count, points, _ = bonds.shape
-    steps = count // GROUP
-    span = held + EDGES
-    for r, payload in enumerate((below, own, above)):
-        for t in range(held):
-            table[r * span + t, 0:6] = payload[pl.ds(t, 6, stride=held)]
-        for i in range(EDGES):
-            at = 6 * (held + i)
-            table[r * span + held + i, 0:6] = payload[at : at + 6]
-    total[...] = jnp.zeros_like(total)
+    points = bonds.shape[-1]
+    for t in range(held):
+        first_table[t, 0:6] = own[pl.ds(t, 6, stride=held)]
+        second_table[t, 0:6] = other[pl.ds(t, 6, stride=held)]
+    for i in range(EDGES):
+        at = 6 * (held + i)
+        second_table[held + i, 0:6] = other[at : at + 6]
+    first_total[...] = jnp.zeros_like(first_total)
+    second_total[...] = jnp.zeros_like(second_total)
+    pairs_a_turn = 2 * GROUP
+    turns = jnp.maximum(lax.div(info[5, kind] + (pairs_a_turn - 1), pairs_a_turn), 1)
+    steps = 2 * turns
 
     def ends(k):
         mid_x = info[2, k].astype(jnp.float32) + 1.5
         mid_y = info[3, k].astype(jnp.float32) + 1.5
         middle = middle_of(mid_x, mid_y, mid_z, points)
-        return (table[info[0, k]] - middle) * (1.0 / HORIZON), (
-            table[info[1, k]] - middle
+        return (first_table[info[0, k]] - middle) * (1.0 / HORIZON), (
+            second_table[info[1, k]] - middle
         ) * (1.0 / HORIZON)
 
+    def members(step):
+        return [kind * ROOM + step * GROUP + g for g in range(GROUP)]
+
     def measure(step, squares):
-        for g in range(GROUP):
-            squares[g] = pair_squares(*ends(step * GROUP + g))
+        for g, k in enumerate(members(step)):
+            squares[g] = pair_squares(*ends(k))
 
     def visit(step, squares, pulls):
-        for g in range(GROUP):
-            high, low = pull_of(squares[g], bonds[step * GROUP + g])
+        for g, k in enumerate(members(step)):
+            high, low = pull_of(squares[g], bonds[info[4, k]])
             pulls[g, 0:points], pulls[g, points:] = high, low
 
     def collect(step, pulls):
         gains = []
-        for g in range(GROUP):
-            k = step * GROUP + g
+        for g, k in enumerate(members(step)):
             here_a, here_b = ends(k)
             gain_a, gain_b = gather_pair(
                 here_a + pltpu.roll(here_a, 5, axis=0),
@@ -201,16 +245,16 @@
                 pulls[g, 0:points],
                 pulls[g, points:],
             )
-            gains.append((info[0, k], gain_a))
-            gains.append((info[1, k], gain_b))
-        for slot, gain in gains:
-            total[slot] += gain
+            gains.append((info[0, k], gain_a, info[1, k], gain_b))
+        for slot_a, gain_a, slot_b, gain_b in gains:
+            first_total[slot_a] += gain_a
+            second_total[slot_b] += gain_b
 
     measure(0, squares0)
     measure(1, squares1)
     visit(0, squares0, pulls0)
 
-    @pl.loop(1, steps // 2)
+    @pl.loop(1, turns)
     def _(twice):
         step = 2 * twice
         measure(step, squares0)
@@ -224,21 +268,42 @@
     collect(steps - 2, pulls0)
     collect(steps - 1, pulls1)
 
-    for r, out in enumerate((down, force, up)):
-        for t in range(held):
-            out[pl.ds(t, 3, stride=held)] = total[r * span + t, 0:3]
-    for r, out, at in ((0, down, 3 * held), (1, edges, 0), (2, up, 3 * held)):
-        for i in range(EDGES):
-            out[at + 3 * i : at + 3 * i + 3] = total[r * span + held + i, 0:3]
-    for out in (down, up):
-        end = 3 * span
-        if end < out.shape[0]:
-            out[end:] = jnp.zeros((out.shape[0] - end, out.shape[1]), jnp.float32)
-
-
-def merge_kernel(held, force, from_above, from_below, near, far, out):
+
+def across_kernel(kind, mid_z, held, info, own, other, bonds, before, force, sent, *scratch):
+    sum_bonds(kind, mid_z, held, info, own, other, bonds, *scratch)
+    first_total, second_total = scratch[2:4]
+    for t in range(held):
+        force[pl.ds(t, 3, stride=held)] = first_total[t, 0:3]
+        sent[pl.ds(t, 3, stride=held)] = second_total[t, 0:3]
+    for i in range(EDGES):
+        at = 3 * (held + i)
+        sent[at : at + 3] = second_total[held + i, 0:3]
+    end = 3 * (held + EDGES)
+    if end < sent.shape[0]:
+        sent[end:] = jnp.zeros((sent.shape[0] - end, sent.shape[1]), jnp.float32)
+    if before is not None:
+        force[...] += before[...]
+
+
+def first_across_kernel(kind, mid_z, held, info, own, other, bonds, *rest):
+    across_kernel(kind, mid_z, held, info, own, other, bonds, None, *rest)
+
+
+def within_kernel(mid_z, held, info, own, bonds, before, from_below, force, edges, *scratch):
+    sum_bonds(SAME, mid_z, held, info, own, own, bonds, *scratch)
+    first_total, second_total = scratch[2:4]
+    for t in range(held):
+        force[pl.ds(t, 3, stride=held)] = first_total[t, 0:3] + second_total[t, 0:3]
+    for i in range(EDGES):
+        edges[3 * i : 3 * i + 3] = second_total[held + i, 0:3]
     rows = 3 * held
-    out[...] = force[...] + (from_above[0:rows] + from_below[0:rows])
+    force[...] += before[...] + from_below[0:rows]
+    edges[...] += from_below[rows : rows + 3 * EDGES]
+
+
+def merge_kernel(held, force, from_above, near, far, out):
+    rows = 3 * held
+    out[...] = force[...] + from_above[0:rows]
     out[pl.ds(0, 3, stride=held)] += near[0:3] + far[0:3]
     out[pl.ds(held - 1, 3, stride=held)] += near[3:6] + far[3:6]
 
@@ -247,26 +312,71 @@
     return pltpu.CompilerParams(vmem_limit_bytes=mebibytes * 1024 * 1024)
 
 
-def bond_call(held, count, points):
+MID_Z = 3.5
+
+
+def bond_call(kernel, held, points, inputs, last_rows, name, megabytes):
     span = held + EDGES
     f32 = jnp.float32
-    sent = jax.ShapeDtypeStruct((padded_rows(3 * span), points), f32)
     return pl.pallas_call(
-        functools.partial(bond_kernel, 3.5, held),
+        kernel,
         out_shape=(
             jax.ShapeDtypeStruct((3 * held, points), f32),
-            sent,
-            sent,
-            jax.ShapeDtypeStruct((3 * EDGES, points), f32),
+            jax.ShapeDtypeStruct((last_rows, points), f32),
         ),
-        in_specs=[SMEM] + [VMEM] * 4,
-        out_specs=(VMEM,) * 4,
-        scratch_shapes=[pltpu.VMEM((3 * span, 8, points), f32)] * 2
+        in_specs=[SMEM] + [VMEM] * inputs,
+        out_specs=(VMEM, VMEM),
+        scratch_shapes=[
+            pltpu.VMEM((held + 1, 8, points), f32),
+            pltpu.VMEM((span + 1, 8, points), f32),
+            pltpu.VMEM((held + 1, 8, points), f32),
+            pltpu.VMEM((span + 1, 8, points), f32),
+        ]
         + [pltpu.VMEM((GROUP, points, 2 * points), f32)] * 2
         + [pltpu.VMEM((GROUP, 2 * points, points), jnp.bfloat16)] * 2,
-        compiler_params=limit(8),
-        name="bond_forces",
-    )
+        compiler_params=limit(4),
+        cost_estimate=pl.CostEstimate(
+            flops=0, bytes_accessed=megabytes << 20, transcendentals=0
+        ),
+        name=name,
+    )
+
+
+def stage_call(held, strip_tiles, intact):
+    return pl.pallas_call(
+        functools.partial(stage_kernel, held, strip_tiles),
+        out_shape=(
+            jax.ShapeDtypeStruct(intact.shape, intact.dtype),
+            jax.ShapeDtypeStruct((6, 256), jnp.int32),
+        ),
+        in_specs=[VMEM, SMEM, HBM],
+        out_specs=(VMEM, SMEM),
+        scratch_shapes=[pltpu.SemaphoreType.DMA],
+        compiler_params=limit(1),
+        cost_estimate=pl.CostEstimate(
+            flops=0, bytes_accessed=4 * intact.size, transcendentals=0
+        ),
+        name="stage_bonds",
+    )
+
+
+def bond_sums(held, points, info, own, below, above, bonds, send_up, send_down):
+    sent_rows = padded_rows(3 * (held + EDGES))
+    force, up = bond_call(
+        functools.partial(first_across_kernel, ABOVE, MID_Z, held),
+        held, points, 3, sent_rows, "bonds_above", 8,
+    )(info, own, above, bonds)
+    from_below = send_up(up)
+    force, down = bond_call(
+        functools.partial(across_kernel, BELOW, MID_Z, held),
+        held, points, 4, sent_rows, "bonds_below", 8,
+    )(info, own, below, bonds, force)
+    from_above = send_down(down)
+    force, edges = bond_call(
+        functools.partial(within_kernel, MID_Z, held),
+        held, points, 4, 3 * EDGES, "bonds_within", 8,
+    )(info, own, bonds, force, from_below)
+    return force, edges, from_above
 
 
 def swapped(value, axis, phase):
@@ -298,24 +408,6 @@
     near = swapped(ends, "tile", 0)
     far = swapped(ends, "tile", 1)
 
-    tile_index = lax.axis_index("tile")
-    strip_of, place = pairs // strip_tiles, pairs % strip_tiles
-    row = strip_of - lax.axis_index("strip") + 1
-    local = place - tile_index * held
-    odd = tile_index % 2
-    column = jnp.where(
-        local < 0, held + 3 - 2 * odd, jnp.where(local >= held, held + 2 * odd, local)
-    )
-    slots = row * span + column
-    info = jnp.stack(
-        [
-            slots[:, 0],
-            slots[:, 1],
-            2 * (strip_of[:, 0] + strip_of[:, 1]),
-            2 * (place[:, 0] + place[:, 1]),
-        ]
-    )
-
     own = pl.pallas_call(
         functools.partial(frame_kernel, held),
         out_shape=packed,
@@ -327,36 +419,32 @@
     )(inside, near, far)
     below = shifted(own, "strip", 1)
     above = shifted(own, "strip", -1)
-    bonds = pl.pallas_call(
-        stage_kernel,
-        out_shape=jax.ShapeDtypeStruct(intact.shape, intact.dtype),
-        in_specs=[VMEM, HBM],
-        out_specs=VMEM,
-        scratch_shapes=[pltpu.SemaphoreType.DMA],
-        compiler_params=limit(1),
-        cost_estimate=pl.CostEstimate(
-            flops=0, bytes_accessed=4 * intact.size, transcendentals=0
-        ),
-        name="stage_bonds",
-    )(own, in_hbm(intact))
-
-    force, down, up, edges = bond_call(held, intact.shape[0], points)(
-        info, below, own, above, bonds
-    )
-    from_above = shifted(down, "strip", -1)
-    from_below = shifted(up, "strip", 1)
+    bonds, info = stage_call(held, strip_tiles, intact)(
+        own, jnp.transpose(pairs), in_hbm(intact)
+    )
+    force, edges, from_above = bond_sums(
+        held,
+        points,
+        info,
+        own,
+        below,
+        above,
+        bonds,
+        lambda up: shifted(up, "strip", 1),
+        lambda down: shifted(down, "strip", -1),
+    )
     tail = slice(3 * held, 3 * span)
-    edge = edges + (from_above[tail] + from_below[tail])
+    edge = edges + from_above[tail]
     near_force = swapped(edge[0:6], "tile", 0)
     far_force = swapped(edge[6:12], "tile", 1)
     merged = pl.pallas_call(
         functools.partial(merge_kernel, held),
         out_shape=jax.ShapeDtypeStruct((3 * held, points), f32),
-        in_specs=[VMEM] * 5,
+        in_specs=[VMEM] * 4,
         out_specs=VMEM,
         compiler_params=limit(1),
         name="merge_forces",
-    )(force, from_above, from_below, near_force, far_force)
+    )(force, from_above, near_force, far_force)
     return jnp.transpose(merged.reshape(3, held, points), (1, 0, 2))
 
 

time: 46.2 us -> 50 us (1.082)
  the two profiles are of different devices: /device:TPU:518 before, /device:TPU:194 now
where the time goes in v3:
time: 50 us; the launch traced here: 49.6 us
  starting transfers between devices  26.3 us (53%)
  Pallas kernels  14.5 us (29%)
  waiting for transfers between devices  7.99 us (16%)
  local copies, waits for them, and re-layouts  0.68 us (1%)
    ppermute x4, starting transfers between devices, shifted(): lax.ppermute(value, axis, [(i, i + step) for i in range(first, last)])  13.2 us
    ppermute x4, starting transfers between devices, swapped(): return lax.ppermute(value, axis, pairs)  13 us
    ppermute x4, waiting for transfers between devices, swapped(): return lax.ppermute(value, axis, pairs)  4.91 us
    pallas_call x1, Pallas kernels, bond_sums(): bond_call(functools.partial(first_across_kernel, ABOVE, MID_Z, held), hel...  4 us
    pallas_call x1, Pallas kernels, on_device(): stage_call(held, strip_tiles, intact)  3.46 us
    ppermute x4, waiting for transfers between devices, shifted(): lax.ppermute(value, axis, [(i, i + step) for i in range(first, last)])  3.08 us
    pallas_call x1, Pallas kernels, bond_sums(): bond_call(functools.partial(across_kernel, BELOW, MID_Z, held), held, poi...  2.91 us
    pallas_call x1, Pallas kernels, bond_sums(): bond_call(functools.partial(within_kernel, MID_Z, held), held, points, 4,...  2.53 us
  transfers between devices with their start and end apart: 8, of which 3 were waited for; matrix products, arithmetic and copies ran while one was open for 0% of the time, Pallas kernels for 26%

profile of v3, /device:TPU:194, one launch (start us, length us, event | category | flops | bytes accessed | tf_op | source)
XLA Modules:
  0.0 49.6 jit_solution(242864207666112072)
XLA Ops:
  0.0 0.9 %pack_payload.1 = (f32[312,128]{1,0:T(8,128)S(1)}, f32[12,128]{1,0:T(8,128)S(1)}) custom-call(f32[144,128]{1,0:T(8,128)} %bitcast.11, f32[144,128]{1,0:T(8,128)} %bitcast.12), custom_call_target="tpu_custom_call" | custom-call | tf_op jit(solution)/shard_map/pack_payload/pallas_call | solution.py:396
  0.9 1.9 %collective-permute-start = (f32[12,128]{1,0:T(8,128)S(1)}, f32[12,128]{1,0:T(8,128)S(1)}, u32[]{:S(2)}, u32[]{:S(2)}) collective-permute-start(f32[12,128]{1,0:T(8,128)S(1)} %get-tuple-element.16), channel_id=1, source_target_pairs={{0,1},{1,0},{2,3},{3,2},{4,5},{5,4},{6,7},{7,6},{8,9},{9,8},{10,11... | collective-permute-start | bytes 18440 | tf_op jit(solution)/shard_map/ppermute | solution.py:386
  2.9 5.5 %collective-permute-start.1 = (f32[12,128]{1,0:T(8,128)S(1)}, f32[12,128]{1,0:T(8,128)S(1)}, u32[]{:S(2)}, u32[]{:S(2)}) collective-permute-start(f32[12,128]{1,0:T(8,128)S(1)} %get-tuple-element.16), channel_id=1, source_target_pairs={{1,2},{2,1},{3,4},{4,3},{5,6},{6,5},{7,8},{8,7},{9,10},{10,9},{11,... | collective-permute-start | bytes 18440 | tf_op jit(solution)/shard_map/ppermute | solution.py:386
  8.3 0.0 collective-permute-done.near
  8.3 1.6 %collective-permute-done.1.far = f32[12,128]{1,0:T(8,128)S(1)} collective-permute-done((f32[12,128]{1,0:T(8,128)S(1)}, f32[12,128]{1,0:T(8,128)S(1)}, u32[]{:S(2)}, u32[]{:S(2)}) %collective-permute-start.1) | collective-permute-done | bytes 6176 | tf_op jit(solution)/shard_map/ppermute | solution.py:386
  10.0 1.9 %collective-permute-start.3 = (f32[312,128]{1,0:T(8,128)S(1)}, f32[312,128]{1,0:T(8,128)S(1)}, u32[]{:S(2)}, u32[]{:S(2)}) collective-permute-start(f32[312,128]{1,0:T(8,128)S(1)} %frame_payload.1.payload.own), channel_id=1, source_target_pairs={{64,0},{128,64},{192,128},{256,192},{320,256},{384,320},{448,384},... | collective-permute-start | bytes 479240 | tf_op jit(solution)/shard_map/ppermute | solution.py:27
  11.9 5.5 %collective-permute-start.2 = (f32[312,128]{1,0:T(8,128)S(1)}, f32[312,128]{1,0:T(8,128)S(1)}, u32[]{:S(2)}, u32[]{:S(2)}) collective-permute-start(f32[312,128]{1,0:T(8,128)S(1)} %frame_payload.1.payload.own), channel_id=1, source_target_pairs={{0,64},{64,128},{128,192},{192,256},{256,320},{320,384},{384,448},... | collective-permute-start | bytes 479240 | tf_op jit(solution)/shard_map/ppermute | solution.py:27
  17.4 0.0 copy-start
  17.4 0.7 %copy-done = s32[64,2]{0,1:T(2,128)S(1)} copy-done((s32[64,2]{0,1:T(2,128)S(1)}, s32[64,2]{0,1:T(2,128)}, u32[]{:S(2)}) %copy-start) | copy-done | bytes 536
  18.1 3.5 %stage_bonds.1 = (s32[64,128,128]{2,1,0:T(8,128)S(1)}, s32[6,256]{1,0:T(8,128)S(1)}) custom-call(f32[312,128]{1,0:T(8,128)S(1)} %frame_payload.1.payload.own, s32[2,64]{1,0:T(2,128)S(1)} %bitcast.10, s32[64,128,128]{2,1,0:T(8,128)} %intact.1), custom_call_target="tpu_custom_call" | custom-call | bytes 4194304 | tf_op jit(solution)/shard_map/stage_bonds/pallas_call | solution.py:422
  21.5 0.0 collective-permute-done.3.other
  21.5 4.0 %bonds_above.1 = (f32[144,128]{1,0:T(8,128)S(1)}, f32[160,128]{1,0:T(8,128)S(1)}) custom-call(s32[6,256]{1,0:T(8,128)S(1)} %get-tuple-element.17.info, f32[312,128]{1,0:T(8,128)S(1)} %frame_payload.1.payload.own, f32[312,128]{1,0:T(8,128)S(1)} %collective-permute-done.3.other, s32[64,128,128]{2,1,0:T(8,128)S(1)} %get-tuple-element.18.bonds), custom_call_target="tpu_custom_call" | custom-call | bytes 8388608 | tf_op jit(solution)/shard_map/bonds_above/pallas_call | solution.py:365
  25.5 3.9 %collective-permute-start.4 = (f32[160,128]{1,0:T(8,128)S(1)}, f32[160,128]{1,0:T(8,128)S(1)}, u32[]{:S(2)}, u32[]{:S(2)}) collective-permute-start(f32[160,128]{1,0:T(8,128)S(1)} %get-tuple-element.21), channel_id=1, source_target_pairs={{0,64},{64,128},{128,192},{192,256},{256,320},{320,384},{384,448},... | collective-permute-start | bytes 245768 | tf_op jit(solution)/shard_map/ppermute | solution.py:27
  29.5 0.0 collective-permute-done.2.other
  29.5 2.9 %bonds_below.1 = (f32[144,128]{1,0:T(8,128)S(1)}, f32[160,128]{1,0:T(8,128)S(1)}) custom-call(s32[6,256]{1,0:T(8,128)S(1)} %get-tuple-element.17.info, f32[312,128]{1,0:T(8,128)S(1)} %frame_payload.1.payload.own, f32[312,128]{1,0:T(8,128)S(1)} %collective-permute-done.2.other, s32[64,128,128]{2,1,0:T(8,128)S(1)} %get-tuple-element.18.bonds, ...), custom_call_target="tpu_custom_call" | custom-call | bytes 8388608 | tf_op jit(solution)/shard_map/bonds_below/pallas_call | solution.py:370
  32.4 1.9 %collective-permute-start.5 = (f32[160,128]{1,0:T(8,128)S(1)}, f32[160,128]{1,0:T(8,128)S(1)}, u32[]{:S(2)}, u32[]{:S(2)}) collective-permute-start(f32[160,128]{1,0:T(8,128)S(1)} %get-tuple-element.23), channel_id=1, source_target_pairs={{64,0},{128,64},{192,128},{256,192},{320,256},{384,320},{448,384},... | collective-permute-start | bytes 245768 | tf_op jit(solution)/shard_map/ppermute | solution.py:27
  34.3 0.0 collective-permute-done.4.from_below
  34.3 2.5 %bonds_within.1 = (f32[144,128]{1,0:T(8,128)S(1)}, f32[12,128]{1,0:T(8,128)S(1)}) custom-call(s32[6,256]{1,0:T(8,128)S(1)} %get-tuple-element.17.info, f32[312,128]{1,0:T(8,128)S(1)} %frame_payload.1.payload.own, s32[64,128,128]{2,1,0:T(8,128)S(1)} %get-tuple-element.18.bonds, f32[144,128]{1,0:T(8,128)S(1)} %get-tuple-element.20.before, ...), custom_call_target="tpu_custom_call" | custom-call | bytes 8388608 | tf_op jit(solution)/shard_map/bonds_within/pallas_call | solution.py:375
  36.9 3.1 %collective-permute-done.5.from_above = f32[160,128]{1,0:T(8,128)S(1)} collective-permute-done((f32[160,128]{1,0:T(8,128)S(1)}, f32[160,128]{1,0:T(8,128)S(1)}, u32[]{:S(2)}, u32[]{:S(2)}) %collective-permute-start.5) | collective-permute-done | bytes 81952 | tf_op jit(solution)/shard_map/ppermute | solution.py:27
  40.0 1.9 %collective-permute-start.6 = (f32[6,128]{1,0:T(8,128)S(1)}, f32[6,128]{1,0:T(8,128)S(1)}, u32[]{:S(2)}, u32[]{:S(2)}) collective-permute-start(f32[6,128]{1,0:T(8,128)S(1)} %get-tuple-element.26), channel_id=1, source_target_pairs={{0,1},{1,0},{2,3},{3,2},{4,5},{5,4},{6,7},{7,6},{8,9},{9,8},{10,11... | collective-permute-start | bytes 9224 | tf_op jit(solution)/shard_map/ppermute | solution.py:386
  41.9 3.7 %collective-permute-start.7 = (f32[6,128]{1,0:T(8,128)S(1)}, f32[6,128]{1,0:T(8,128)S(1)}, u32[]{:S(2)}, u32[]{:S(2)}) collective-permute-start(f32[6,128]{1,0:T(8,128)S(1)} %get-tuple-element.25), channel_id=1, source_target_pairs={{1,2},{2,1},{3,4},{4,3},{5,6},{6,5},{7,8},{8,7},{9,10},{10,9},{11,... | collective-permute-start | bytes 9224 | tf_op jit(solution)/shard_map/ppermute | solution.py:386
  45.6 0.0 collective-permute-done.6.near
  45.6 3.3 %collective-permute-done.7.far = f32[6,128]{1,0:T(8,128)S(1)} collective-permute-done((f32[6,128]{1,0:T(8,128)S(1)}, f32[6,128]{1,0:T(8,128)S(1)}, u32[]{:S(2)}, u32[]{:S(2)}) %collective-permute-start.7) | collective-permute-done | bytes 3104 | tf_op jit(solution)/shard_map/ppermute | solution.py:386
  48.9 0.7 %merge_forces.1 = f32[144,128]{1,0:T(8,128)} custom-call(f32[144,128]{1,0:T(8,128)S(1)} %get-tuple-element.22.force, f32[160,128]{1,0:T(8,128)S(1)} %collective-permute-done.5.from_above, f32[6,128]{1,0:T(8,128)S(1)} %collective-permute-done.6.near, f32[6,128]{1,0:T(8,128)S(1)} %collective-permute-done.7.far), custom_call_target="tpu_custom_call" | custom-call | tf_op jit(solution)/shard_map/merge_forces/pallas_call | solution.py:440
  (3 shorter events, 0.0 us)
Async XLA Ops:
  0.9 7.4 %collective-permute-start = (f32[12,128]{1,0:T(8,128)S(1)}, f32[12,128]{1,0:T(8,128)S(1)}, u32[]{:S(2)}, u32[]{:S(2)}) collective-permute-start(f32[12,128]{1,0:T(8,128)S(1)} %get-tuple-element.16), channel_id=1, source_target_pairs={{0,1},{1,0},{2,3},{3,2},{4,5},{5,4},{6,7},{7,6},{8,9},{9,8},{10,11... | collective-permute-start | bytes 18440 | tf_op jit(solution)/shard_map/ppermute | solution.py:386
  2.9 7.1 %collective-permute-start.1 = (f32[12,128]{1,0:T(8,128)S(1)}, f32[12,128]{1,0:T(8,128)S(1)}, u32[]{:S(2)}, u32[]{:S(2)}) collective-permute-start(f32[12,128]{1,0:T(8,128)S(1)} %get-tuple-element.16), channel_id=1, source_target_pairs={{1,2},{2,1},{3,4},{4,3},{5,6},{6,5},{7,8},{8,7},{9,10},{10,9},{11,... | collective-permute-start | bytes 18440 | tf_op jit(solution)/shard_map/ppermute | solution.py:386
  10.0 11.6 %collective-permute-start.3 = (f32[312,128]{1,0:T(8,128)S(1)}, f32[312,128]{1,0:T(8,128)S(1)}, u32[]{:S(2)}, u32[]{:S(2)}) collective-permute-start(f32[312,128]{1,0:T(8,128)S(1)} %frame_payload.1.payload.own), channel_id=1, source_target_pairs={{64,0},{128,64},{192,128},{256,192},{320,256},{384,320},{448,384},... | collective-permute-start | bytes 479240 | tf_op jit(solution)/shard_map/ppermute | solution.py:27
  11.9 17.6 %collective-permute-start.2 = (f32[312,128]{1,0:T(8,128)S(1)}, f32[312,128]{1,0:T(8,128)S(1)}, u32[]{:S(2)}, u32[]{:S(2)}) collective-permute-start(f32[312,128]{1,0:T(8,128)S(1)} %frame_payload.1.payload.own), channel_id=1, source_target_pairs={{0,64},{64,128},{128,192},{192,256},{256,320},{320,384},{384,448},... | collective-permute-start | bytes 479240 | tf_op jit(solution)/shard_map/ppermute | solution.py:27
  17.4 0.7 %copy-start = (s32[64,2]{0,1:T(2,128)S(1)}, s32[64,2]{0,1:T(2,128)}, u32[]{:S(2)}) copy-start(s32[64,2]{0,1:T(2,128)} %param.6) | copy-start | bytes 1540
  25.5 8.8 %collective-permute-start.4 = (f32[160,128]{1,0:T(8,128)S(1)}, f32[160,128]{1,0:T(8,128)S(1)}, u32[]{:S(2)}, u32[]{:S(2)}) collective-permute-start(f32[160,128]{1,0:T(8,128)S(1)} %get-tuple-element.21), channel_id=1, source_target_pairs={{0,64},{64,128},{128,192},{192,256},{256,320},{320,384},{384,448},... | collective-permute-start | bytes 245768 | tf_op jit(solution)/shard_map/ppermute | solution.py:27
  32.4 7.5 %collective-permute-start.5 = (f32[160,128]{1,0:T(8,128)S(1)}, f32[160,128]{1,0:T(8,128)S(1)}, u32[]{:S(2)}, u32[]{:S(2)}) collective-permute-start(f32[160,128]{1,0:T(8,128)S(1)} %get-tuple-element.23), channel_id=1, source_target_pairs={{64,0},{128,64},{192,128},{256,192},{320,256},{384,320},{448,384},... | collective-permute-start | bytes 245768 | tf_op jit(solution)/shard_map/ppermute | solution.py:27
  40.0 5.7 %collective-permute-start.6 = (f32[6,128]{1,0:T(8,128)S(1)}, f32[6,128]{1,0:T(8,128)S(1)}, u32[]{:S(2)}, u32[]{:S(2)}) collective-permute-start(f32[6,128]{1,0:T(8,128)S(1)} %get-tuple-element.26), channel_id=1, source_target_pairs={{0,1},{1,0},{2,3},{3,2},{4,5},{5,4},{6,7},{7,6},{8,9},{9,8},{10,11... | collective-permute-start | bytes 9224 | tf_op jit(solution)/shard_map/ppermute | solution.py:386
  41.9 7.0 %collective-permute-start.7 = (f32[6,128]{1,0:T(8,128)S(1)}, f32[6,128]{1,0:T(8,128)S(1)}, u32[]{:S(2)}, u32[]{:S(2)}) collective-permute-start(f32[6,128]{1,0:T(8,128)S(1)} %get-tuple-element.25), channel_id=1, source_target_pairs={{1,2},{2,1},{3,4},{4,3},{5,6},{6,5},{7,8},{8,7},{9,10},{10,9},{11,... | collective-permute-start | bytes 9224 | tf_op jit(solution)/shard_map/ppermute | solution.py:386

commit v4 on v2

--- a/solution.py
+++ b/solution.py
@@ -13,7 +13,10 @@
 FINAL = 0.05
 
 GROUP = 8
+LEFT_GROUP = 8
+MID_Z = 3.5
 EDGES = 4
+ALIGNED = 8
 VMEM = pl.BlockSpec(memory_space=pltpu.VMEM)
 HBM = pl.BlockSpec(memory_space=pltpu.HBM)
 SMEM = pl.BlockSpec(memory_space=pltpu.SMEM)
@@ -33,7 +36,30 @@
     return (rows + 7) // 8 * 8
 
 
-def pack_kernel(held, coords, displacement, out, edges, arrived):
+def ends_kernel(coords, displacement, ends, near_ends, arrived):
+    held = coords.shape[1]
+    copies = []
+    for i, source in enumerate((coords, displacement)):
+        for j, start in enumerate((0, held - ALIGNED)):
+            copies.append(
+                pltpu.make_async_copy(
+                    source.at[:, pl.ds(start, ALIGNED), :],
+                    near_ends.at[i, j],
+                    arrived.at[2 * i + j],
+                )
+            )
+    for copy in copies:
+        copy.start()
+    for copy in copies:
+        copy.wait()
+    for j, row in enumerate((0, ALIGNED - 1)):
+        for i in range(2):
+            for c in range(3):
+                at = 6 * j + 3 * i + c
+                ends[at : at + 1] = near_ends[i, j, c, row : row + 1]
+
+
+def pack_kernel(held, coords, displacement, out, arrived):
     rows = 3 * held
     copies = [
         pltpu.make_async_copy(source, out.at[pl.ds(i * rows, rows)], arrived.at[i])
@@ -43,8 +69,6 @@
         copy.start()
     for copy in copies:
         copy.wait()
-    for i, t in enumerate((0, held - 1)):
-        edges[6 * i : 6 * i + 6] = out[pl.ds(t, 6, stride=held)]
 
 
 def frame_kernel(held, payload, near, far, out):
@@ -53,9 +77,20 @@
     out[end + 12 : end + 24] = far[...]
 
 
-def stage_kernel(payload, bonds, out, arrived):
+def stage_kernel(held, info, own, bonds, out, left, table, arrived):
     copy = pltpu.make_async_copy(bonds, out, arrived)
     copy.start()
+    base = held + EDGES
+    for t in range(held):
+        table[t, 0:6] = own[pl.ds(t, 6, stride=held)]
+
+    @pl.loop(0, out.shape[0] // LEFT_GROUP)
+    def _(step):
+        for g in range(LEFT_GROUP):
+            k = step * LEFT_GROUP + g
+            here = centred(table[info[0, k] - base], info, k)
+            left[k] = jnp.transpose(left_rows(here)).astype(jnp.bfloat16)
+
     copy.wait()
 
 
@@ -71,6 +106,12 @@
     return jnp.where(
         row == 0, mid_x, jnp.where(row == 1, mid_y, jnp.where(row == 2, mid_z, 0.0))
     )
+
+
+def centred(tile, info, k):
+    mid_x = info[2, k].astype(jnp.float32) + 1.5
+    mid_y = info[3, k].astype(jnp.float32) + 1.5
+    return (tile - middle_of(mid_x, mid_y, MID_Z, tile.shape[-1])) * (1.0 / HORIZON)
 
 
 def side_rows(here, row):
@@ -91,26 +132,27 @@
     return jnp.concatenate([rows, rows], axis=1)
 
 
-def pair_squares(here_a, here_b):
-    points = here_a.shape[-1]
-    row = lax.broadcasted_iota(jnp.int32, (8, points), 0)
-    _, _, square_a, growth_a = side_rows(here_a, row)
-    moved_b, now_b, square_b, growth_b = side_rows(here_b, row)
-
-    six, seven = row == 6, row == 7
-    left = jnp.where(row < 6, -2.0 * here_a, jnp.where(six, square_a, growth_a))
-    l1, l2, l3 = pieces(left)
+def left_rows(here):
+    row = lax.broadcasted_iota(jnp.int32, here.shape, 0)
+    six = row == 6
+    _, _, square, growth = side_rows(here, row)
+    l1, l2, l3 = pieces(jnp.where(row < 6, -2.0 * here, jnp.where(six, square, growth)))
 
     def ones(value):
         return jnp.where(row < 6, value, jnp.where(six, 1.0, 0.0))
 
     o1, o2 = ones(l1), ones(l2)
-    lhs = jnp.concatenate([l1, l2, l3, o1, o2, o1], axis=0).astype(jnp.bfloat16)
-
-    shifted_b = pltpu.roll(now_b, 3, axis=0)
-    right_ref = jnp.where(row < 3, here_b, jnp.where(six, square_b, 0.0))
+    return jnp.concatenate([l1, l2, l3, o1, o2, o1], axis=0)
+
+
+def right_rows(here):
+    row = lax.broadcasted_iota(jnp.int32, here.shape, 0)
+    six, seven = row == 6, row == 7
+    moved, now, square, growth = side_rows(here, row)
+    lowered = pltpu.roll(now, 3, axis=0)
+    right_ref = jnp.where(row < 3, here, jnp.where(six, square, 0.0))
     right_gain = jnp.where(
-        row < 3, moved_b, jnp.where(row < 6, shifted_b, jnp.where(six, growth_b, 0.0))
+        row < 3, moved, jnp.where(row < 6, lowered, jnp.where(six, growth, 0.0))
     )
 
     def stack(value, at_six, at_seven):
@@ -119,10 +161,7 @@
         mixed = jnp.where(six, p1, p2)
         return jnp.concatenate([base, base, base, mixed, p2, p3], axis=0)
 
-    rhs = jnp.concatenate([stack(right_ref, 1.0, 0.0), stack(right_gain, 0.0, 1.0)], axis=1)
-    return lax.dot_general(
-        lhs, rhs.astype(jnp.bfloat16), (((0,), (0,)), ((), ())), preferred_element_type=jnp.float32
-    )
+    return jnp.concatenate([stack(right_ref, 1.0, 0.0), stack(right_gain, 0.0, 1.0)], axis=1)
 
 
 def pull_of(both, bond_mask):
@@ -159,7 +198,7 @@
 
 
 def bond_kernel(
-    mid_z, held, info, below, own, above, bonds, force, down, up, edges,
+    held, info, below, own, above, bonds, left, force, down, up, edges,
     table, total, squares0, squares1, pulls0, pulls1
 ):
     count, points, _ = bonds.shape
@@ -173,17 +212,11 @@
             table[r * span + held + i, 0:6] = payload[at : at + 6]
     total[...] = jnp.zeros_like(total)
 
-    def ends(k):
-        mid_x = info[2, k].astype(jnp.float32) + 1.5
-        mid_y = info[3, k].astype(jnp.float32) + 1.5
-        middle = middle_of(mid_x, mid_y, mid_z, points)
-        return (table[info[0, k]] - middle) * (1.0 / HORIZON), (
-            table[info[1, k]] - middle
-        ) * (1.0 / HORIZON)
-
     def measure(step, squares):
         for g in range(GROUP):
-            squares[g] = pair_squares(*ends(step * GROUP + g))
+            k = step * GROUP + g
+            rows = right_rows(centred(table[info[1, k]], info, k)).astype(jnp.bfloat16)
+            squares[g] = jnp.dot(left[k], rows, preferred_element_type=jnp.float32)
 
     def visit(step, squares, pulls):
         for g in range(GROUP):
@@ -194,7 +227,7 @@
         gains = []
         for g in range(GROUP):
             k = step * GROUP + g
-            here_a, here_b = ends(k)
+            here_a, here_b = centred(table[info[0, k]], info, k), centred(table[info[1, k]], info, k)
             gain_a, gain_b = gather_pair(
                 here_a + pltpu.roll(here_a, 5, axis=0),
                 here_b + pltpu.roll(here_b, 5, axis=0),
@@ -247,19 +280,41 @@
     return pltpu.CompilerParams(vmem_limit_bytes=mebibytes * 1024 * 1024)
 
 
+def stage_call(held, intact):
+    count, points, _ = intact.shape
+    return pl.pallas_call(
+        functools.partial(stage_kernel, held),
+        out_shape=(
+            jax.ShapeDtypeStruct(intact.shape, intact.dtype),
+            jax.ShapeDtypeStruct((count, points, 48), jnp.bfloat16),
+        ),
+        in_specs=[SMEM, VMEM, HBM],
+        out_specs=(VMEM, VMEM),
+        scratch_shapes=[
+            pltpu.VMEM((held, 8, points), jnp.float32),
+            pltpu.SemaphoreType.DMA,
+        ],
+        compiler_params=limit(2),
+        cost_estimate=pl.CostEstimate(
+            flops=0, bytes_accessed=4 * intact.size, transcendentals=0
+        ),
+        name="stage_bonds",
+    )
+
+
 def bond_call(held, count, points):
     span = held + EDGES
     f32 = jnp.float32
     sent = jax.ShapeDtypeStruct((padded_rows(3 * span), points), f32)
     return pl.pallas_call(
-        functools.partial(bond_kernel, 3.5, held),
+        functools.partial(bond_kernel, held),
         out_shape=(
             jax.ShapeDtypeStruct((3 * held, points), f32),
             sent,
             sent,
             jax.ShapeDtypeStruct((3 * EDGES, points), f32),
         ),
-        in_specs=[SMEM] + [VMEM] * 4,
+        in_specs=[SMEM] + [VMEM] * 5,
         out_specs=(VMEM,) * 4,
         scratch_shapes=[pltpu.VMEM((3 * span, 8, points), f32)] * 2
         + [pltpu.VMEM((GROUP, points, 2 * points), f32)] * 2
@@ -283,38 +338,31 @@
     f32 = jnp.float32
 
     packed = jax.ShapeDtypeStruct((padded_rows(6 * span), points), f32)
-    inside, ends = pl.pallas_call(
+    places, shifts = jnp.transpose(coords, (1, 0, 2)), jnp.transpose(displacement, (1, 0, 2))
+    ends = pl.pallas_call(
+        ends_kernel,
+        out_shape=jax.ShapeDtypeStruct((12, points), f32),
+        in_specs=[HBM] * 2,
+        out_specs=VMEM,
+        scratch_shapes=[
+            pltpu.VMEM((2, 2, 3, ALIGNED, points), f32),
+            pltpu.SemaphoreType.DMA((4,)),
+        ],
+        compiler_params=limit(1),
+        name="end_tiles",
+    )(in_hbm(places), in_hbm(shifts))
+    inside = pl.pallas_call(
         functools.partial(pack_kernel, held),
-        out_shape=(packed, jax.ShapeDtypeStruct((12, points), f32)),
+        out_shape=packed,
         in_specs=[HBM] * 2,
-        out_specs=(VMEM,) * 2,
+        out_specs=VMEM,
         scratch_shapes=[pltpu.SemaphoreType.DMA((2,))],
         compiler_params=limit(1),
+        cost_estimate=pl.CostEstimate(flops=0, bytes_accessed=4 << 20, transcendentals=0),
         name="pack_payload",
-    )(
-        in_hbm(jnp.transpose(coords, (1, 0, 2)).reshape(-1, points)),
-        in_hbm(jnp.transpose(displacement, (1, 0, 2)).reshape(-1, points)),
-    )
+    )(in_hbm(places.reshape(-1, points)), in_hbm(shifts.reshape(-1, points)))
     near = swapped(ends, "tile", 0)
     far = swapped(ends, "tile", 1)
-
-    tile_index = lax.axis_index("tile")
-    strip_of, place = pairs // strip_tiles, pairs % strip_tiles
-    row = strip_of - lax.axis_index("strip") + 1
-    local = place - tile_index * held
-    odd = tile_index % 2
-    column = jnp.where(
-        local < 0, held + 3 - 2 * odd, jnp.where(local >= held, held + 2 * odd, local)
-    )
-    slots = row * span + column
-    info = jnp.stack(
-        [
-            slots[:, 0],
-            slots[:, 1],
-            2 * (strip_of[:, 0] + strip_of[:, 1]),
-            2 * (place[:, 0] + place[:, 1]),
-        ]
-    )
 
     own = pl.pallas_call(
         functools.partial(frame_kernel, held),
@@ -327,21 +375,28 @@
     )(inside, near, far)
     below = shifted(own, "strip", 1)
     above = shifted(own, "strip", -1)
-    bonds = pl.pallas_call(
-        stage_kernel,
-        out_shape=jax.ShapeDtypeStruct(intact.shape, intact.dtype),
-        in_specs=[VMEM, HBM],
-        out_specs=VMEM,
-        scratch_shapes=[pltpu.SemaphoreType.DMA],
-        compiler_params=limit(1),
-        cost_estimate=pl.CostEstimate(
-            flops=0, bytes_accessed=4 * intact.size, transcendentals=0
-        ),
-        name="stage_bonds",
-    )(own, in_hbm(intact))
-
+    own, pairs = lax.optimization_barrier((own, pairs))
+    tile_index = lax.axis_index("tile")
+    strip_of, place = pairs // strip_tiles, pairs % strip_tiles
+    row = strip_of - lax.axis_index("strip") + 1
+    local = place - tile_index * held
+    odd = tile_index % 2
+    column = jnp.where(
+        local < 0, held + 3 - 2 * odd, jnp.where(local >= held, held + 2 * odd, local)
+    )
+    slots = row * span + column
+    info = jnp.stack(
+        [
+            slots[:, 0],
+            slots[:, 1],
+            2 * (strip_of[:, 0] + strip_of[:, 1]),
+            2 * (place[:, 0] + place[:, 1]),
+        ]
+    )
+
+    bonds, left = stage_call(held, intact)(info, own, in_hbm(intact))
     force, down, up, edges = bond_call(held, intact.shape[0], points)(
-        info, below, own, above, bonds
+        info, below, own, above, bonds, left
     )
     from_above = shifted(down, "strip", -1)
     from_below = shifted(up, "strip", 1)

time: 46.2 us -> 45.9 us (level)
  waiting for transfers between devices: 11 us -> 9.87 us
  Pallas kernels: 10.7 us -> 11.6 us
    ppermute x4, waiting for transfers between devices: 8.2 us -> 7.11 us  [shifted(): lax.ppermute(value, axis, [(i, i + step) for i in range(first, last)])]
    pallas_call x3 -> x4, Pallas kernels: 10 us -> 10.9 us  [the longest x1 6.43 us: on_device(): bond_call(held, intact.shape[0], points)]
  transfers between devices with their start and end apart: 8 -> 8, of which waited for: 5 -> 5; matrix products, arithmetic and copies ran while one was open for 2% -> 2% of each run, Pallas kernels for 5% -> 8%
where the time goes in v4:
time: 45.9 us; the launch traced here: 45.5 us
  starting transfers between devices  23.1 us (50%)
  Pallas kernels  11.6 us (25%)
  waiting for transfers between devices  9.87 us (22%)
  other arithmetic  0.72 us (2%)
    ppermute x4, starting transfers between devices, shifted(): lax.ppermute(value, axis, [(i, i + step) for i in range(first, last)])  11.7 us
    ppermute x4, starting transfers between devices, swapped(): return lax.ppermute(value, axis, pairs)  11.4 us
    ppermute x4, waiting for transfers between devices, shifted(): lax.ppermute(value, axis, [(i, i + step) for i in range(first, last)])  7.11 us
    pallas_call x1, Pallas kernels, on_device(): bond_call(held, intact.shape[0], points)  6.43 us
    ppermute x4, waiting for transfers between devices, swapped(): return lax.ppermute(value, axis, pairs)  2.77 us
    pallas_call x1, Pallas kernels, on_device(): bonds, left = stage_call(held, intact)(info, own, in_hbm(intact))  2.76 us
    pallas_call x1, Pallas kernels, on_device(): pl.pallas_call(functools.partial(pack_kernel, held), out_shape=packed, in...  0.94 us
  transfers between devices with their start and end apart: 8, of which 5 were waited for; matrix products, arithmetic and copies ran while one was open for 2% of the time, Pallas kernels for 8%

profile of v4, /device:TPU:518, one launch (start us, length us, event | category | flops | bytes accessed | tf_op | source)
XLA Modules:
  0.0 45.5 jit_solution(10933601022590365490)
XLA Ops:
  0.0 0.8 %end_tiles.1 = f32[12,128]{1,0:T(8,128)S(1)} custom-call(f32[3,48,128]{2,1,0:T(8,128)} %bitcast.17, f32[3,48,128]{2,1,0:T(8,128)} %bitcast.19), custom_call_target="tpu_custom_call" | custom-call | tf_op jit(solution)/shard_map/end_tiles/pallas_call | solution.py:342
  0.8 5.1 %collective-permute-start.1 = (f32[12,128]{1,0:T(8,128)S(1)}, f32[12,128]{1,0:T(8,128)S(1)}, u32[]{:S(2)}, u32[]{:S(2)}) collective-permute-start(f32[12,128]{1,0:T(8,128)S(1)} %end_tiles.1), channel_id=1, source_target_pairs={{1,2},{2,1},{3,4},{4,3},{5,6},{6,5},{7,8},{8,7},{9,10},{10,9},{11,... | collective-permute-start | bytes 18440 | tf_op jit(solution)/shard_map/ppermute | solution.py:331
  5.9 1.9 %collective-permute-start = (f32[12,128]{1,0:T(8,128)S(1)}, f32[12,128]{1,0:T(8,128)S(1)}, u32[]{:S(2)}, u32[]{:S(2)}) collective-permute-start(f32[12,128]{1,0:T(8,128)S(1)} %end_tiles.1), channel_id=1, source_target_pairs={{0,1},{1,0},{2,3},{3,2},{4,5},{5,4},{6,7},{7,6},{8,9},{9,8},{10,11... | collective-permute-start | bytes 18440 | tf_op jit(solution)/shard_map/ppermute | solution.py:331
  7.8 0.9 %pack_payload.1.payload = f32[312,128]{1,0:T(8,128)S(1)} custom-call(f32[144,128]{1,0:T(8,128)} %bitcast.18, f32[144,128]{1,0:T(8,128)} %bitcast.20), custom_call_target="tpu_custom_call" | custom-call | bytes 4194304 | tf_op jit(solution)/shard_map/pack_payload/pallas_call | solution.py:354
  8.8 0.0 collective-permute-done.1.far
  8.8 0.2 collective-permute-done.near
  9.0 3.7 %collective-permute-start.3 = (f32[312,128]{1,0:T(8,128)S(1)}, f32[312,128]{1,0:T(8,128)S(1)}, u32[]{:S(2)}, u32[]{:S(2)}) collective-permute-start(f32[312,128]{1,0:T(8,128)S(1)} %frame_payload.1.own), channel_id=1, source_target_pairs={{64,0},{128,64},{192,128},{256,192},{320,256},{384,320},{448,384},... | collective-permute-start | bytes 479240 | tf_op jit(solution)/shard_map/ppermute | solution.py:28
  12.6 2.2 %collective-permute-start.2 = (f32[312,128]{1,0:T(8,128)S(1)}, f32[312,128]{1,0:T(8,128)S(1)}, u32[]{:S(2)}, u32[]{:S(2)}) collective-permute-start(f32[312,128]{1,0:T(8,128)S(1)} %frame_payload.1.own), channel_id=1, source_target_pairs={{0,64},{64,128},{128,192},{192,256},{256,320},{320,384},{384,448},... | collective-permute-start | bytes 479240 | tf_op jit(solution)/shard_map/ppermute | solution.py:28
  14.8 0.7 %fusion.1 = (s32[64,2]{0,1:T(2,128)S(1)}, s32[64,2]{0,1:T(2,128)S(1)}, s32[64,2]{0,1:T(2,128)S(1)}) fusion(s32[]{:T(128)S(6)} %add.52, s32[]{:T(128)S(6)} %sub.26, s32[]{:T(128)S(6)} %mul.41, s32[]{:T(128)S(6)} %axis_index.23, s32[64,2]{0,1:T(2,128)} %param.6), kind=kLoop, calls=%fused_computation.7 | loop fusion | flops 2688 | bytes 2064 | tf_op jit(solution)/shard_map/add | solution.py:387
  15.6 2.8 %stage_bonds.1 = (s32[64,128,128]{2,1,0:T(8,128)S(1)}, bf16[64,128,48]{2,1,0:T(8,128)(2,1)S(1)}) custom-call(s32[4,64]{1,0:T(4,128)S(1)} %pad_add_fusion.info, f32[312,128]{1,0:T(8,128)S(1)} %frame_payload.1.own, s32[64,128,128]{2,1,0:T(8,128)} %bonds.1), custom_call_target="tpu_custom_call" | custom-call | bytes 4194304 | tf_op jit(solution)/shard_map/stage_bonds/pallas_call | solution.py:397
  18.3 0.0 collective-permute-done.3.above
  18.4 3.5 %collective-permute-done.2.below = f32[312,128]{1,0:T(8,128)S(1)} collective-permute-done((f32[312,128]{1,0:T(8,128)S(1)}, f32[312,128]{1,0:T(8,128)S(1)}, u32[]{:S(2)}, u32[]{:S(2)}) %collective-permute-start.2) | collective-permute-done | bytes 159776 | tf_op jit(solution)/shard_map/ppermute | solution.py:28
  21.8 6.4 %bond_forces.1 = (f32[144,128]{1,0:T(8,128)S(1)}, f32[160,128]{1,0:T(8,128)S(1)}, f32[160,128]{1,0:T(8,128)S(1)}, f32[12,128]{1,0:T(8,128)S(1)}) custom-call(s32[4,64]{1,0:T(4,128)S(1)} %pad_add_fusion.info, f32[312,128]{1,0:T(8,128)S(1)} %collective-permute-done.2.below, f32[312,128]{1,0:T(8,128)S(1)} %frame_payload.1.own, ...), custom_call_target="tpu_custom_call" | custom-call | tf_op jit(solution)/shard_map/bond_forces/pallas_call | solution.py:398
  28.3 1.9 %collective-permute-start.4 = (f32[160,128]{1,0:T(8,128)S(1)}, f32[160,128]{1,0:T(8,128)S(1)}, u32[]{:S(2)}, u32[]{:S(2)}) collective-permute-start(f32[160,128]{1,0:T(8,128)S(1)} %get-tuple-element.18), channel_id=1, source_target_pairs={{64,0},{128,64},{192,128},{256,192},{320,256},{384,320},{448,384},... | collective-permute-start | bytes 245768 | tf_op jit(solution)/shard_map/ppermute | solution.py:28
  30.2 3.9 %collective-permute-start.5 = (f32[160,128]{1,0:T(8,128)S(1)}, f32[160,128]{1,0:T(8,128)S(1)}, u32[]{:S(2)}, u32[]{:S(2)}) collective-permute-start(f32[160,128]{1,0:T(8,128)S(1)} %get-tuple-element.19), channel_id=1, source_target_pairs={{0,64},{64,128},{128,192},{192,256},{256,320},{320,384},{384,448},... | collective-permute-start | bytes 245768 | tf_op jit(solution)/shard_map/ppermute | solution.py:28
  34.1 0.5 %collective-permute-done.4.from_above = f32[160,128]{1,0:T(8,128)S(1)} collective-permute-done((f32[160,128]{1,0:T(8,128)S(1)}, f32[160,128]{1,0:T(8,128)S(1)}, u32[]{:S(2)}, u32[]{:S(2)}) %collective-permute-start.4) | collective-permute-done | bytes 81952 | tf_op jit(solution)/shard_map/ppermute | solution.py:28
  34.6 3.1 %collective-permute-done.5.from_below = f32[160,128]{1,0:T(8,128)S(1)} collective-permute-done((f32[160,128]{1,0:T(8,128)S(1)}, f32[160,128]{1,0:T(8,128)S(1)}, u32[]{:S(2)}, u32[]{:S(2)}) %collective-permute-start.5) | collective-permute-done | bytes 81952 | tf_op jit(solution)/shard_map/ppermute | solution.py:28
  37.8 2.5 %collective-permute-start.7 = (f32[6,128]{1,0:T(8,128)S(1)}, f32[6,128]{1,0:T(8,128)S(1)}, u32[]{:S(2)}, u32[]{:S(2)}) collective-permute-start(f32[6,128]{1,0:T(8,128)S(1)} %get-tuple-element.23), channel_id=1, source_target_pairs={{1,2},{2,1},{3,4},{4,3},{5,6},{6,5},{7,8},{8,7},{9,10},{10,9},{11,... | collective-permute-start | bytes 9224 | tf_op jit(solution)/shard_map/ppermute | solution.py:331
  40.3 1.9 %collective-permute-start.6 = (f32[6,128]{1,0:T(8,128)S(1)}, f32[6,128]{1,0:T(8,128)S(1)}, u32[]{:S(2)}, u32[]{:S(2)}) collective-permute-start(f32[6,128]{1,0:T(8,128)S(1)} %get-tuple-element.24), channel_id=1, source_target_pairs={{0,1},{1,0},{2,3},{3,2},{4,5},{5,4},{6,7},{7,6},{8,9},{9,8},{10,11... | collective-permute-start | bytes 9224 | tf_op jit(solution)/shard_map/ppermute | solution.py:331
  42.2 2.6 %collective-permute-done.7.far = f32[6,128]{1,0:T(8,128)S(1)} collective-permute-done((f32[6,128]{1,0:T(8,128)S(1)}, f32[6,128]{1,0:T(8,128)S(1)}, u32[]{:S(2)}, u32[]{:S(2)}) %collective-permute-start.7) | collective-permute-done | bytes 3104 | tf_op jit(solution)/shard_map/ppermute | solution.py:331
  44.8 0.0 collective-permute-done.6.near
  44.8 0.7 %merge_forces.1 = f32[144,128]{1,0:T(8,128)} custom-call(f32[144,128]{1,0:T(8,128)S(1)} %get-tuple-element.17.force, f32[160,128]{1,0:T(8,128)S(1)} %collective-permute-done.4.from_above, f32[160,128]{1,0:T(8,128)S(1)} %collective-permute-done.5.from_below, f32[6,128]{1,0:T(8,128)S(1)} %collective-permute-done.6.near, f32[6,128]{1,0:T(8,128)S(1)} %collective-permute-done.7.far), custom_call_target="tpu_custom_call" | custom-call | tf_op jit(solution)/shard_map/merge_forces/pallas_call | solution.py:407
  (6 shorter events, 0.0 us)
Async XLA Ops:
  0.8 8.0 %collective-permute-start.1 = (f32[12,128]{1,0:T(8,128)S(1)}, f32[12,128]{1,0:T(8,128)S(1)}, u32[]{:S(2)}, u32[]{:S(2)}) collective-permute-start(f32[12,128]{1,0:T(8,128)S(1)} %end_tiles.1), channel_id=1, source_target_pairs={{1,2},{2,1},{3,4},{4,3},{5,6},{6,5},{7,8},{8,7},{9,10},{10,9},{11,... | collective-permute-start | bytes 18440 | tf_op jit(solution)/shard_map/ppermute | solution.py:331
  5.9 3.1 %collective-permute-start = (f32[12,128]{1,0:T(8,128)S(1)}, f32[12,128]{1,0:T(8,128)S(1)}, u32[]{:S(2)}, u32[]{:S(2)}) collective-permute-start(f32[12,128]{1,0:T(8,128)S(1)} %end_tiles.1), channel_id=1, source_target_pairs={{0,1},{1,0},{2,3},{3,2},{4,5},{5,4},{6,7},{7,6},{8,9},{9,8},{10,11... | collective-permute-start | bytes 18440 | tf_op jit(solution)/shard_map/ppermute | solution.py:331
  9.0 9.4 %collective-permute-start.3 = (f32[312,128]{1,0:T(8,128)S(1)}, f32[312,128]{1,0:T(8,128)S(1)}, u32[]{:S(2)}, u32[]{:S(2)}) collective-permute-start(f32[312,128]{1,0:T(8,128)S(1)} %frame_payload.1.own), channel_id=1, source_target_pairs={{64,0},{128,64},{192,128},{256,192},{320,256},{384,320},{448,384},... | collective-permute-start | bytes 479240 | tf_op jit(solution)/shard_map/ppermute | solution.py:28
  12.6 9.2 %collective-permute-start.2 = (f32[312,128]{1,0:T(8,128)S(1)}, f32[312,128]{1,0:T(8,128)S(1)}, u32[]{:S(2)}, u32[]{:S(2)}) collective-permute-start(f32[312,128]{1,0:T(8,128)S(1)} %frame_payload.1.own), channel_id=1, source_target_pairs={{0,64},{64,128},{128,192},{192,256},{256,320},{320,384},{384,448},... | collective-permute-start | bytes 479240 | tf_op jit(solution)/shard_map/ppermute | solution.py:28
  28.3 6.3 %collective-permute-start.4 = (f32[160,128]{1,0:T(8,128)S(1)}, f32[160,128]{1,0:T(8,128)S(1)}, u32[]{:S(2)}, u32[]{:S(2)}) collective-permute-start(f32[160,128]{1,0:T(8,128)S(1)} %get-tuple-element.18), channel_id=1, source_target_pairs={{64,0},{128,64},{192,128},{256,192},{320,256},{384,320},{448,384},... | collective-permute-start | bytes 245768 | tf_op jit(solution)/shard_map/ppermute | solution.py:28
  30.2 7.5 %collective-permute-start.5 = (f32[160,128]{1,0:T(8,128)S(1)}, f32[160,128]{1,0:T(8,128)S(1)}, u32[]{:S(2)}, u32[]{:S(2)}) collective-permute-start(f32[160,128]{1,0:T(8,128)S(1)} %get-tuple-element.19), channel_id=1, source_target_pairs={{0,64},{64,128},{128,192},{192,256},{256,320},{320,384},{384,448},... | collective-permute-start | bytes 245768 | tf_op jit(solution)/shard_map/ppermute | solution.py:28
  37.8 7.0 %collective-permute-start.7 = (f32[6,128]{1,0:T(8,128)S(1)}, f32[6,128]{1,0:T(8,128)S(1)}, u32[]{:S(2)}, u32[]{:S(2)}) collective-permute-start(f32[6,128]{1,0:T(8,128)S(1)} %get-tuple-element.23), channel_id=1, source_target_pairs={{1,2},{2,1},{3,4},{4,3},{5,6},{6,5},{7,8},{8,7},{9,10},{10,9},{11,... | collective-permute-start | bytes 9224 | tf_op jit(solution)/shard_map/ppermute | solution.py:331
  40.3 4.5 %collective-permute-start.6 = (f32[6,128]{1,0:T(8,128)S(1)}, f32[6,128]{1,0:T(8,128)S(1)}, u32[]{:S(2)}, u32[]{:S(2)}) collective-permute-start(f32[6,128]{1,0:T(8,128)S(1)} %get-tuple-element.24), channel_id=1, source_target_pairs={{0,1},{1,0},{2,3},{3,2},{4,5},{5,4},{6,7},{7,6},{8,9},{9,8},{10,11... | collective-permute-start | bytes 9224 | tf_op jit(solution)/shard_map/ppermute | solution.py:331

commit v5 on v4

--- a/solution.py
+++ b/solution.py
@@ -12,7 +12,9 @@
 ONSET = 0.02
 FINAL = 0.05
 
-GROUP = 8
+GROUP = 64
+LAG = 3
+RING = 6
 LEFT_GROUP = 8
 MID_Z = 3.5
 EDGES = 4
@@ -199,10 +201,10 @@
 
 def bond_kernel(
     held, info, below, own, above, bonds, left, force, down, up, edges,
-    table, total, squares0, squares1, pulls0, pulls1
+    table, total, *rings
 ):
     count, points, _ = bonds.shape
-    steps = count // GROUP
+    squares, pulls = rings[:RING], rings[RING:]
     span = held + EDGES
     for r, payload in enumerate((below, own, above)):
         for t in range(held):
@@ -212,50 +214,36 @@
             table[r * span + held + i, 0:6] = payload[at : at + 6]
     total[...] = jnp.zeros_like(total)
 
-    def measure(step, squares):
-        for g in range(GROUP):
-            k = step * GROUP + g
-            rows = right_rows(centred(table[info[1, k]], info, k)).astype(jnp.bfloat16)
-            squares[g] = jnp.dot(left[k], rows, preferred_element_type=jnp.float32)
-
-    def visit(step, squares, pulls):
-        for g in range(GROUP):
-            high, low = pull_of(squares[g], bonds[step * GROUP + g])
-            pulls[g, 0:points], pulls[g, points:] = high, low
-
-    def collect(step, pulls):
-        gains = []
-        for g in range(GROUP):
-            k = step * GROUP + g
-            here_a, here_b = centred(table[info[0, k]], info, k), centred(table[info[1, k]], info, k)
-            gain_a, gain_b = gather_pair(
-                here_a + pltpu.roll(here_a, 5, axis=0),
-                here_b + pltpu.roll(here_b, 5, axis=0),
-                pulls[g, 0:points],
-                pulls[g, points:],
-            )
-            gains.append((info[0, k], gain_a))
-            gains.append((info[1, k], gain_b))
-        for slot, gain in gains:
-            total[slot] += gain
-
-    measure(0, squares0)
-    measure(1, squares1)
-    visit(0, squares0, pulls0)
-
-    @pl.loop(1, steps // 2)
-    def _(twice):
-        step = 2 * twice
-        measure(step, squares0)
-        visit(step - 1, squares1, pulls1)
-        collect(step - 2, pulls0)
-        measure(step + 1, squares1)
-        visit(step, squares0, pulls0)
-        collect(step - 1, pulls1)
-
-    visit(steps - 1, squares1, pulls1)
-    collect(steps - 2, pulls0)
-    collect(steps - 1, pulls1)
+    def measure(k, squares):
+        rows = right_rows(centred(table[info[1, k]], info, k)).astype(jnp.bfloat16)
+        squares[...] = jnp.dot(left[k], rows, preferred_element_type=jnp.float32)
+
+    def visit(k, squares, pulls):
+        high, low = pull_of(squares[...], bonds[k])
+        pulls[0:points], pulls[points:] = high, low
+
+    def collect(k, pulls):
+        here_a = centred(table[info[0, k]], info, k)
+        here_b = centred(table[info[1, k]], info, k)
+        gain_a, gain_b = gather_pair(
+            here_a + pltpu.roll(here_a, 5, axis=0),
+            here_b + pltpu.roll(here_b, 5, axis=0),
+            pulls[0:points],
+            pulls[points:],
+        )
+        total[info[0, k]] += gain_a
+        total[info[1, k]] += gain_b
+
+    @pl.loop(0, count // GROUP)
+    def _(turn):
+        first = turn * GROUP
+        for at in range(GROUP + 2 * LAG):
+            if at < GROUP:
+                measure(first + at, squares[at % RING])
+            if 0 <= at - LAG < GROUP:
+                visit(first + at - LAG, squares[(at - LAG) % RING], pulls[(at - LAG) % RING])
+            if 0 <= at - 2 * LAG < GROUP:
+                collect(first + at - 2 * LAG, pulls[(at - 2 * LAG) % RING])
 
     for r, out in enumerate((down, force, up)):
         for t in range(held):
@@ -317,8 +305,8 @@
         in_specs=[SMEM] + [VMEM] * 5,
         out_specs=(VMEM,) * 4,
         scratch_shapes=[pltpu.VMEM((3 * span, 8, points), f32)] * 2
-        + [pltpu.VMEM((GROUP, points, 2 * points), f32)] * 2
-        + [pltpu.VMEM((GROUP, 2 * points, points), jnp.bfloat16)] * 2,
+        + [pltpu.VMEM((points, 2 * points), f32)] * RING
+        + [pltpu.VMEM((2 * points, points), jnp.bfloat16)] * RING,
         compiler_params=limit(8),
         name="bond_forces",
     )

time: 45.9 us -> 45 us (0.980)
  Pallas kernels: 11.6 us -> 10.7 us
    pallas_call x1, Pallas kernels: 6.43 us -> 5.52 us  [on_device(): bond_call(held, intact.shape[0], points)]
where the time goes in v5:
time: 45 us; the launch traced here: 44.5 us
  starting transfers between devices  23.1 us (51%)
  Pallas kernels  10.7 us (24%)
  waiting for transfers between devices  9.86 us (22%)
  other arithmetic  0.72 us (2%)
    ppermute x4, starting transfers between devices, shifted(): lax.ppermute(value, axis, [(i, i + step) for i in range(first, last)])  11.7 us
    ppermute x4, starting transfers between devices, swapped(): return lax.ppermute(value, axis, pairs)  11.4 us
    ppermute x4, waiting for transfers between devices, shifted(): lax.ppermute(value, axis, [(i, i + step) for i in range(first, last)])  7.11 us
    pallas_call x1, Pallas kernels, on_device(): bond_call(held, intact.shape[0], points)  5.52 us
    pallas_call x1, Pallas kernels, on_device(): bonds, left = stage_call(held, intact)(info, own, in_hbm(intact))  2.76 us
    ppermute x4, waiting for transfers between devices, swapped(): return lax.ppermute(value, axis, pairs)  2.76 us
    pallas_call x1, Pallas kernels, on_device(): pl.pallas_call(functools.partial(pack_kernel, held), out_shape=packed, in...  0.94 us
  transfers between devices with their start and end apart: 8, of which 5 were waited for; matrix products, arithmetic and copies ran while one was open for 2% of the time, Pallas kernels for 8%

profile of v5, /device:TPU:518, one launch (start us, length us, event | category | flops | bytes accessed | tf_op | source)
XLA Modules:
  0.0 44.5 jit_solution(4589468176392798225)
XLA Ops:
  0.0 0.8 %end_tiles.1 = f32[12,128]{1,0:T(8,128)S(1)} custom-call(f32[3,48,128]{2,1,0:T(8,128)} %bitcast.17, f32[3,48,128]{2,1,0:T(8,128)} %bitcast.19), custom_call_target="tpu_custom_call" | custom-call | tf_op jit(solution)/shard_map/end_tiles/pallas_call | solution.py:330
  0.8 5.1 %collective-permute-start.1 = (f32[12,128]{1,0:T(8,128)S(1)}, f32[12,128]{1,0:T(8,128)S(1)}, u32[]{:S(2)}, u32[]{:S(2)}) collective-permute-start(f32[12,128]{1,0:T(8,128)S(1)} %end_tiles.1), channel_id=1, source_target_pairs={{1,2},{2,1},{3,4},{4,3},{5,6},{6,5},{7,8},{8,7},{9,10},{10,9},{11,... | collective-permute-start | bytes 18440 | tf_op jit(solution)/shard_map/ppermute | solution.py:319
  5.9 1.9 %collective-permute-start = (f32[12,128]{1,0:T(8,128)S(1)}, f32[12,128]{1,0:T(8,128)S(1)}, u32[]{:S(2)}, u32[]{:S(2)}) collective-permute-start(f32[12,128]{1,0:T(8,128)S(1)} %end_tiles.1), channel_id=1, source_target_pairs={{0,1},{1,0},{2,3},{3,2},{4,5},{5,4},{6,7},{7,6},{8,9},{9,8},{10,11... | collective-permute-start | bytes 18440 | tf_op jit(solution)/shard_map/ppermute | solution.py:319
  7.8 0.9 %pack_payload.1.payload = f32[312,128]{1,0:T(8,128)S(1)} custom-call(f32[144,128]{1,0:T(8,128)} %bitcast.18, f32[144,128]{1,0:T(8,128)} %bitcast.20), custom_call_target="tpu_custom_call" | custom-call | bytes 4194304 | tf_op jit(solution)/shard_map/pack_payload/pallas_call | solution.py:342
  8.8 0.0 collective-permute-done.1.far
  8.8 0.2 collective-permute-done.near
  9.0 3.7 %collective-permute-start.3 = (f32[312,128]{1,0:T(8,128)S(1)}, f32[312,128]{1,0:T(8,128)S(1)}, u32[]{:S(2)}, u32[]{:S(2)}) collective-permute-start(f32[312,128]{1,0:T(8,128)S(1)} %frame_payload.1.own), channel_id=1, source_target_pairs={{64,0},{128,64},{192,128},{256,192},{320,256},{384,320},{448,384},... | collective-permute-start | bytes 479240 | tf_op jit(solution)/shard_map/ppermute | solution.py:30
  12.6 2.2 %collective-permute-start.2 = (f32[312,128]{1,0:T(8,128)S(1)}, f32[312,128]{1,0:T(8,128)S(1)}, u32[]{:S(2)}, u32[]{:S(2)}) collective-permute-start(f32[312,128]{1,0:T(8,128)S(1)} %frame_payload.1.own), channel_id=1, source_target_pairs={{0,64},{64,128},{128,192},{192,256},{256,320},{320,384},{384,448},... | collective-permute-start | bytes 479240 | tf_op jit(solution)/shard_map/ppermute | solution.py:30
  14.8 0.7 %fusion.1 = (s32[64,2]{0,1:T(2,128)S(1)}, s32[64,2]{0,1:T(2,128)S(1)}, s32[64,2]{0,1:T(2,128)S(1)}) fusion(s32[]{:T(128)S(6)} %add.52, s32[]{:T(128)S(6)} %sub.26, s32[]{:T(128)S(6)} %mul.41, s32[]{:T(128)S(6)} %axis_index.23, s32[64,2]{0,1:T(2,128)} %param.6), kind=kLoop, calls=%fused_computation.7 | loop fusion | flops 2688 | bytes 2064 | tf_op jit(solution)/shard_map/add | solution.py:375
  15.6 2.8 %stage_bonds.1 = (s32[64,128,128]{2,1,0:T(8,128)S(1)}, bf16[64,128,48]{2,1,0:T(8,128)(2,1)S(1)}) custom-call(s32[4,64]{1,0:T(4,128)S(1)} %pad_add_fusion.info, f32[312,128]{1,0:T(8,128)S(1)} %frame_payload.1.own, s32[64,128,128]{2,1,0:T(8,128)} %bonds.1), custom_call_target="tpu_custom_call" | custom-call | bytes 4194304 | tf_op jit(solution)/shard_map/stage_bonds/pallas_call | solution.py:385
  18.3 0.0 collective-permute-done.3.above
  18.4 3.5 %collective-permute-done.2.below = f32[312,128]{1,0:T(8,128)S(1)} collective-permute-done((f32[312,128]{1,0:T(8,128)S(1)}, f32[312,128]{1,0:T(8,128)S(1)}, u32[]{:S(2)}, u32[]{:S(2)}) %collective-permute-start.2) | collective-permute-done | bytes 159776 | tf_op jit(solution)/shard_map/ppermute | solution.py:30
  21.8 5.5 %bond_forces.1 = (f32[144,128]{1,0:T(8,128)S(1)}, f32[160,128]{1,0:T(8,128)S(1)}, f32[160,128]{1,0:T(8,128)S(1)}, f32[12,128]{1,0:T(8,128)S(1)}) custom-call(s32[4,64]{1,0:T(4,128)S(1)} %pad_add_fusion.info, f32[312,128]{1,0:T(8,128)S(1)} %collective-permute-done.2.below, f32[312,128]{1,0:T(8,128)S(1)} %frame_payload.1.own, ...), custom_call_target="tpu_custom_call" | custom-call | tf_op jit(solution)/shard_map/bond_forces/pallas_call | solution.py:386
  27.4 1.9 %collective-permute-start.4 = (f32[160,128]{1,0:T(8,128)S(1)}, f32[160,128]{1,0:T(8,128)S(1)}, u32[]{:S(2)}, u32[]{:S(2)}) collective-permute-start(f32[160,128]{1,0:T(8,128)S(1)} %get-tuple-element.18), channel_id=1, source_target_pairs={{64,0},{128,64},{192,128},{256,192},{320,256},{384,320},{448,384},... | collective-permute-start | bytes 245768 | tf_op jit(solution)/shard_map/ppermute | solution.py:30
  29.3 3.9 %collective-permute-start.5 = (f32[160,128]{1,0:T(8,128)S(1)}, f32[160,128]{1,0:T(8,128)S(1)}, u32[]{:S(2)}, u32[]{:S(2)}) collective-permute-start(f32[160,128]{1,0:T(8,128)S(1)} %get-tuple-element.19), channel_id=1, source_target_pairs={{0,64},{64,128},{128,192},{192,256},{256,320},{320,384},{384,448},... | collective-permute-start | bytes 245768 | tf_op jit(solution)/shard_map/ppermute | solution.py:30
  33.2 0.5 %collective-permute-done.4.from_above = f32[160,128]{1,0:T(8,128)S(1)} collective-permute-done((f32[160,128]{1,0:T(8,128)S(1)}, f32[160,128]{1,0:T(8,128)S(1)}, u32[]{:S(2)}, u32[]{:S(2)}) %collective-permute-start.4) | collective-permute-done | bytes 81952 | tf_op jit(solution)/shard_map/ppermute | solution.py:30
  33.7 3.1 %collective-permute-done.5.from_below = f32[160,128]{1,0:T(8,128)S(1)} collective-permute-done((f32[160,128]{1,0:T(8,128)S(1)}, f32[160,128]{1,0:T(8,128)S(1)}, u32[]{:S(2)}, u32[]{:S(2)}) %collective-permute-start.5) | collective-permute-done | bytes 81952 | tf_op jit(solution)/shard_map/ppermute | solution.py:30
  36.9 2.5 %collective-permute-start.7 = (f32[6,128]{1,0:T(8,128)S(1)}, f32[6,128]{1,0:T(8,128)S(1)}, u32[]{:S(2)}, u32[]{:S(2)}) collective-permute-start(f32[6,128]{1,0:T(8,128)S(1)} %get-tuple-element.23), channel_id=1, source_target_pairs={{1,2},{2,1},{3,4},{4,3},{5,6},{6,5},{7,8},{8,7},{9,10},{10,9},{11,... | collective-permute-start | bytes 9224 | tf_op jit(solution)/shard_map/ppermute | solution.py:319
  39.4 1.9 %collective-permute-start.6 = (f32[6,128]{1,0:T(8,128)S(1)}, f32[6,128]{1,0:T(8,128)S(1)}, u32[]{:S(2)}, u32[]{:S(2)}) collective-permute-start(f32[6,128]{1,0:T(8,128)S(1)} %get-tuple-element.24), channel_id=1, source_target_pairs={{0,1},{1,0},{2,3},{3,2},{4,5},{5,4},{6,7},{7,6},{8,9},{9,8},{10,11... | collective-permute-start | bytes 9224 | tf_op jit(solution)/shard_map/ppermute | solution.py:319
  41.3 2.6 %collective-permute-done.7.far = f32[6,128]{1,0:T(8,128)S(1)} collective-permute-done((f32[6,128]{1,0:T(8,128)S(1)}, f32[6,128]{1,0:T(8,128)S(1)}, u32[]{:S(2)}, u32[]{:S(2)}) %collective-permute-start.7) | collective-permute-done | bytes 3104 | tf_op jit(solution)/shard_map/ppermute | solution.py:319
  43.9 0.0 collective-permute-done.6.near
  43.9 0.7 %merge_forces.1 = f32[144,128]{1,0:T(8,128)} custom-call(f32[144,128]{1,0:T(8,128)S(1)} %get-tuple-element.17.force, f32[160,128]{1,0:T(8,128)S(1)} %collective-permute-done.4.from_above, f32[160,128]{1,0:T(8,128)S(1)} %collective-permute-done.5.from_below, f32[6,128]{1,0:T(8,128)S(1)} %collective-permute-done.6.near, f32[6,128]{1,0:T(8,128)S(1)} %collective-permute-done.7.far), custom_call_target="tpu_custom_call" | custom-call | tf_op jit(solution)/shard_map/merge_forces/pallas_call | solution.py:395
  (6 shorter events, 0.0 us)
Async XLA Ops:
  0.8 8.0 %collective-permute-start.1 = (f32[12,128]{1,0:T(8,128)S(1)}, f32[12,128]{1,0:T(8,128)S(1)}, u32[]{:S(2)}, u32[]{:S(2)}) collective-permute-start(f32[12,128]{1,0:T(8,128)S(1)} %end_tiles.1), channel_id=1, source_target_pairs={{1,2},{2,1},{3,4},{4,3},{5,6},{6,5},{7,8},{8,7},{9,10},{10,9},{11,... | collective-permute-start | bytes 18440 | tf_op jit(solution)/shard_map/ppermute | solution.py:319
  5.9 3.1 %collective-permute-start = (f32[12,128]{1,0:T(8,128)S(1)}, f32[12,128]{1,0:T(8,128)S(1)}, u32[]{:S(2)}, u32[]{:S(2)}) collective-permute-start(f32[12,128]{1,0:T(8,128)S(1)} %end_tiles.1), channel_id=1, source_target_pairs={{0,1},{1,0},{2,3},{3,2},{4,5},{5,4},{6,7},{7,6},{8,9},{9,8},{10,11... | collective-permute-start | bytes 18440 | tf_op jit(solution)/shard_map/ppermute | solution.py:319
  9.0 9.4 %collective-permute-start.3 = (f32[312,128]{1,0:T(8,128)S(1)}, f32[312,128]{1,0:T(8,128)S(1)}, u32[]{:S(2)}, u32[]{:S(2)}) collective-permute-start(f32[312,128]{1,0:T(8,128)S(1)} %frame_payload.1.own), channel_id=1, source_target_pairs={{64,0},{128,64},{192,128},{256,192},{320,256},{384,320},{448,384},... | collective-permute-start | bytes 479240 | tf_op jit(solution)/shard_map/ppermute | solution.py:30
  12.6 9.2 %collective-permute-start.2 = (f32[312,128]{1,0:T(8,128)S(1)}, f32[312,128]{1,0:T(8,128)S(1)}, u32[]{:S(2)}, u32[]{:S(2)}) collective-permute-start(f32[312,128]{1,0:T(8,128)S(1)} %frame_payload.1.own), channel_id=1, source_target_pairs={{0,64},{64,128},{128,192},{192,256},{256,320},{320,384},{384,448},... | collective-permute-start | bytes 479240 | tf_op jit(solution)/shard_map/ppermute | solution.py:30
  27.4 6.3 %collective-permute-start.4 = (f32[160,128]{1,0:T(8,128)S(1)}, f32[160,128]{1,0:T(8,128)S(1)}, u32[]{:S(2)}, u32[]{:S(2)}) collective-permute-start(f32[160,128]{1,0:T(8,128)S(1)} %get-tuple-element.18), channel_id=1, source_target_pairs={{64,0},{128,64},{192,128},{256,192},{320,256},{384,320},{448,384},... | collective-permute-start | bytes 245768 | tf_op jit(solution)/shard_map/ppermute | solution.py:30
  29.3 7.5 %collective-permute-start.5 = (f32[160,128]{1,0:T(8,128)S(1)}, f32[160,128]{1,0:T(8,128)S(1)}, u32[]{:S(2)}, u32[]{:S(2)}) collective-permute-start(f32[160,128]{1,0:T(8,128)S(1)} %get-tuple-element.19), channel_id=1, source_target_pairs={{0,64},{64,128},{128,192},{192,256},{256,320},{320,384},{384,448},... | collective-permute-start | bytes 245768 | tf_op jit(solution)/shard_map/ppermute | solution.py:30
  36.9 7.0 %collective-permute-start.7 = (f32[6,128]{1,0:T(8,128)S(1)}, f32[6,128]{1,0:T(8,128)S(1)}, u32[]{:S(2)}, u32[]{:S(2)}) collective-permute-start(f32[6,128]{1,0:T(8,128)S(1)} %get-tuple-element.23), channel_id=1, source_target_pairs={{1,2},{2,1},{3,4},{4,3},{5,6},{6,5},{7,8},{8,7},{9,10},{10,9},{11,... | collective-permute-start | bytes 9224 | tf_op jit(solution)/shard_map/ppermute | solution.py:319
  39.4 4.5 %collective-permute-start.6 = (f32[6,128]{1,0:T(8,128)S(1)}, f32[6,128]{1,0:T(8,128)S(1)}, u32[]{:S(2)}, u32[]{:S(2)}) collective-permute-start(f32[6,128]{1,0:T(8,128)S(1)} %get-tuple-element.24), channel_id=1, source_target_pairs={{0,1},{1,0},{2,3},{3,2},{4,5},{5,4},{6,7},{7,6},{8,9},{9,8},{10,11... | collective-permute-start | bytes 9224 | tf_op jit(solution)/shard_map/ppermute | solution.py:319

commit v6 on v5

--- a/solution.py
+++ b/solution.py
@@ -257,9 +257,9 @@
             out[end:] = jnp.zeros((out.shape[0] - end, out.shape[1]), jnp.float32)
 
 
-def merge_kernel(held, force, from_above, from_below, near, far, out):
+def merge_kernel(held, force, from_below, from_above, near, far, out):
     rows = 3 * held
-    out[...] = force[...] + (from_above[0:rows] + from_below[0:rows])
+    out[...] = force[...] + (from_below[0:rows] + from_above[0:rows])
     out[pl.ds(0, 3, stride=held)] += near[0:3] + far[0:3]
     out[pl.ds(held - 1, 3, stride=held)] += near[3:6] + far[3:6]
 
@@ -386,10 +386,10 @@
     force, down, up, edges = bond_call(held, intact.shape[0], points)(
         info, below, own, above, bonds, left
     )
+    from_below = shifted(up, "strip", 1)
     from_above = shifted(down, "strip", -1)
-    from_below = shifted(up, "strip", 1)
     tail = slice(3 * held, 3 * span)
-    edge = edges + (from_above[tail] + from_below[tail])
+    edge = edges + (from_below[tail] + from_above[tail])
     near_force = swapped(edge[0:6], "tile", 0)
     far_force = swapped(edge[6:12], "tile", 1)
     merged = pl.pallas_call(
@@ -399,7 +399,7 @@
         out_specs=VMEM,
         compiler_params=limit(1),
         name="merge_forces",
-    )(force, from_above, from_below, near_force, far_force)
+    )(force, from_below, from_above, near_force, far_force)
     return jnp.transpose(merged.reshape(3, held, points), (1, 0, 2))
 
 

time: 45 us -> 47.1 us (1.047)
  the two profiles are of different devices: /device:TPU:518 before, /device:TPU:198 now
where the time goes in v6:
time: 47.1 us; the launch traced here: 46.6 us
  starting transfers between devices  25.8 us (55%)
  Pallas kernels  10.7 us (23%)
  waiting for transfers between devices  9.26 us (20%)
  other arithmetic  0.72 us (2%)
    ppermute x4, starting transfers between devices, shifted(): lax.ppermute(value, axis, [(i, i + step) for i in range(first, last)])  14.9 us
    ppermute x4, starting transfers between devices, swapped(): return lax.ppermute(value, axis, pairs)  10.9 us
    ppermute x4, waiting for transfers between devices, shifted(): lax.ppermute(value, axis, [(i, i + step) for i in range(first, last)])  5.96 us
    pallas_call x1, Pallas kernels, on_device(): bond_call(held, intact.shape[0], points)  5.52 us
    ppermute x4, waiting for transfers between devices, swapped(): return lax.ppermute(value, axis, pairs)  3.3 us
    pallas_call x1, Pallas kernels, on_device(): bonds, left = stage_call(held, intact)(info, own, in_hbm(intact))  2.76 us
  transfers between devices with their start and end apart: 8, of which 5 were waited for; matrix products, arithmetic and copies ran while one was open for 2% of the time, Pallas kernels for 8%

profile of v6, /device:TPU:198, one launch (start us, length us, event | category | flops | bytes accessed | tf_op | source)
XLA Modules:
  0.0 46.6 jit_solution(4097074097738772415)
XLA Ops:
  0.0 0.8 %end_tiles.1 = f32[12,128]{1,0:T(8,128)S(1)} custom-call(f32[3,48,128]{2,1,0:T(8,128)} %bitcast.17, f32[3,48,128]{2,1,0:T(8,128)} %bitcast.19), custom_call_target="tpu_custom_call" | custom-call | tf_op jit(solution)/shard_map/end_tiles/pallas_call | solution.py:330
  0.8 5.1 %collective-permute-start.1 = (f32[12,128]{1,0:T(8,128)S(1)}, f32[12,128]{1,0:T(8,128)S(1)}, u32[]{:S(2)}, u32[]{:S(2)}) collective-permute-start(f32[12,128]{1,0:T(8,128)S(1)} %end_tiles.1), channel_id=1, source_target_pairs={{1,2},{2,1},{3,4},{4,3},{5,6},{6,5},{7,8},{8,7},{9,10},{10,9},{11,... | collective-permute-start | bytes 18440 | tf_op jit(solution)/shard_map/ppermute | solution.py:319
  5.9 1.9 %collective-permute-start = (f32[12,128]{1,0:T(8,128)S(1)}, f32[12,128]{1,0:T(8,128)S(1)}, u32[]{:S(2)}, u32[]{:S(2)}) collective-permute-start(f32[12,128]{1,0:T(8,128)S(1)} %end_tiles.1), channel_id=1, source_target_pairs={{0,1},{1,0},{2,3},{3,2},{4,5},{5,4},{6,7},{7,6},{8,9},{9,8},{10,11... | collective-permute-start | bytes 18440 | tf_op jit(solution)/shard_map/ppermute | solution.py:319
  7.8 0.9 %pack_payload.1.payload = f32[312,128]{1,0:T(8,128)S(1)} custom-call(f32[144,128]{1,0:T(8,128)} %bitcast.18, f32[144,128]{1,0:T(8,128)} %bitcast.20), custom_call_target="tpu_custom_call" | custom-call | bytes 4194304 | tf_op jit(solution)/shard_map/pack_payload/pallas_call | solution.py:342
  8.8 0.0 collective-permute-done.1.far
  8.8 0.2 collective-permute-done.near
  9.0 1.9 %collective-permute-start.3 = (f32[312,128]{1,0:T(8,128)S(1)}, f32[312,128]{1,0:T(8,128)S(1)}, u32[]{:S(2)}, u32[]{:S(2)}) collective-permute-start(f32[312,128]{1,0:T(8,128)S(1)} %frame_payload.1.own), channel_id=1, source_target_pairs={{64,0},{128,64},{192,128},{256,192},{320,256},{384,320},{448,384},... | collective-permute-start | bytes 479240 | tf_op jit(solution)/shard_map/ppermute | solution.py:30
  10.9 5.5 %collective-permute-start.2 = (f32[312,128]{1,0:T(8,128)S(1)}, f32[312,128]{1,0:T(8,128)S(1)}, u32[]{:S(2)}, u32[]{:S(2)}) collective-permute-start(f32[312,128]{1,0:T(8,128)S(1)} %frame_payload.1.own), channel_id=1, source_target_pairs={{0,64},{64,128},{128,192},{192,256},{256,320},{320,384},{384,448},... | collective-permute-start | bytes 479240 | tf_op jit(solution)/shard_map/ppermute | solution.py:30
  16.4 0.7 %fusion.1 = (s32[64,2]{0,1:T(2,128)S(1)}, s32[64,2]{0,1:T(2,128)S(1)}, s32[64,2]{0,1:T(2,128)S(1)}) fusion(s32[]{:T(128)S(6)} %add.52, s32[]{:T(128)S(6)} %sub.26, s32[]{:T(128)S(6)} %mul.41, s32[]{:T(128)S(6)} %axis_index.23, s32[64,2]{0,1:T(2,128)} %param.6), kind=kLoop, calls=%fused_computation.7 | loop fusion | flops 2688 | bytes 2064 | tf_op jit(solution)/shard_map/add | solution.py:375
  17.1 2.8 %stage_bonds.1 = (s32[64,128,128]{2,1,0:T(8,128)S(1)}, bf16[64,128,48]{2,1,0:T(8,128)(2,1)S(1)}) custom-call(s32[4,64]{1,0:T(4,128)S(1)} %pad_add_fusion.info, f32[312,128]{1,0:T(8,128)S(1)} %frame_payload.1.own, s32[64,128,128]{2,1,0:T(8,128)} %bonds.1), custom_call_target="tpu_custom_call" | custom-call | bytes 4194304 | tf_op jit(solution)/shard_map/stage_bonds/pallas_call | solution.py:385
  19.9 0.0 collective-permute-done.3.above
  19.9 0.3 collective-permute-done.2.below
  20.3 5.5 %bond_forces.1 = (f32[144,128]{1,0:T(8,128)S(1)}, f32[160,128]{1,0:T(8,128)S(1)}, f32[160,128]{1,0:T(8,128)S(1)}, f32[12,128]{1,0:T(8,128)S(1)}) custom-call(s32[4,64]{1,0:T(4,128)S(1)} %pad_add_fusion.info, f32[312,128]{1,0:T(8,128)S(1)} %collective-permute-done.2.below, f32[312,128]{1,0:T(8,128)S(1)} %frame_payload.1.own, ...), custom_call_target="tpu_custom_call" | custom-call | tf_op jit(solution)/shard_map/bond_forces/pallas_call | solution.py:386
  25.8 5.6 %collective-permute-start.4 = (f32[160,128]{1,0:T(8,128)S(1)}, f32[160,128]{1,0:T(8,128)S(1)}, u32[]{:S(2)}, u32[]{:S(2)}) collective-permute-start(f32[160,128]{1,0:T(8,128)S(1)} %get-tuple-element.18), channel_id=1, source_target_pairs={{0,64},{64,128},{128,192},{192,256},{256,320},{320,384},{384,448},... | collective-permute-start | bytes 245768 | tf_op jit(solution)/shard_map/ppermute | solution.py:30
  31.4 1.9 %collective-permute-start.5 = (f32[160,128]{1,0:T(8,128)S(1)}, f32[160,128]{1,0:T(8,128)S(1)}, u32[]{:S(2)}, u32[]{:S(2)}) collective-permute-start(f32[160,128]{1,0:T(8,128)S(1)} %get-tuple-element.19), channel_id=1, source_target_pairs={{64,0},{128,64},{192,128},{256,192},{320,256},{384,320},{448,384},... | collective-permute-start | bytes 245768 | tf_op jit(solution)/shard_map/ppermute | solution.py:30
  33.3 0.1 collective-permute-done.4.from_below
  33.4 5.5 %collective-permute-done.5.from_above = f32[160,128]{1,0:T(8,128)S(1)} collective-permute-done((f32[160,128]{1,0:T(8,128)S(1)}, f32[160,128]{1,0:T(8,128)S(1)}, u32[]{:S(2)}, u32[]{:S(2)}) %collective-permute-start.5) | collective-permute-done | bytes 81952 | tf_op jit(solution)/shard_map/ppermute | solution.py:30
  39.0 2.0 %collective-permute-start.7 = (f32[6,128]{1,0:T(8,128)S(1)}, f32[6,128]{1,0:T(8,128)S(1)}, u32[]{:S(2)}, u32[]{:S(2)}) collective-permute-start(f32[6,128]{1,0:T(8,128)S(1)} %get-tuple-element.23), channel_id=1, source_target_pairs={{1,2},{2,1},{3,4},{4,3},{5,6},{6,5},{7,8},{8,7},{9,10},{10,9},{11,... | collective-permute-start | bytes 9224 | tf_op jit(solution)/shard_map/ppermute | solution.py:319
  40.9 1.9 %collective-permute-start.6 = (f32[6,128]{1,0:T(8,128)S(1)}, f32[6,128]{1,0:T(8,128)S(1)}, u32[]{:S(2)}, u32[]{:S(2)}) collective-permute-start(f32[6,128]{1,0:T(8,128)S(1)} %get-tuple-element.24), channel_id=1, source_target_pairs={{0,1},{1,0},{2,3},{3,2},{4,5},{5,4},{6,7},{7,6},{8,9},{9,8},{10,11... | collective-permute-start | bytes 9224 | tf_op jit(solution)/shard_map/ppermute | solution.py:319
  42.8 3.1 %collective-permute-done.7.far = f32[6,128]{1,0:T(8,128)S(1)} collective-permute-done((f32[6,128]{1,0:T(8,128)S(1)}, f32[6,128]{1,0:T(8,128)S(1)}, u32[]{:S(2)}, u32[]{:S(2)}) %collective-permute-start.7) | collective-permute-done | bytes 3104 | tf_op jit(solution)/shard_map/ppermute | solution.py:319
  46.0 0.0 collective-permute-done.6.near
  46.0 0.7 %merge_forces.1 = f32[144,128]{1,0:T(8,128)} custom-call(f32[144,128]{1,0:T(8,128)S(1)} %get-tuple-element.17.force, f32[160,128]{1,0:T(8,128)S(1)} %collective-permute-done.4.from_below, f32[160,128]{1,0:T(8,128)S(1)} %collective-permute-done.5.from_above, f32[6,128]{1,0:T(8,128)S(1)} %collective-permute-done.6.near, f32[6,128]{1,0:T(8,128)S(1)} %collective-permute-done.7.far), custom_call_target="tpu_custom_call" | custom-call | tf_op jit(solution)/shard_map/merge_forces/pallas_call | solution.py:395
  (6 shorter events, 0.0 us)
Async XLA Ops:
  0.8 8.0 %collective-permute-start.1 = (f32[12,128]{1,0:T(8,128)S(1)}, f32[12,128]{1,0:T(8,128)S(1)}, u32[]{:S(2)}, u32[]{:S(2)}) collective-permute-start(f32[12,128]{1,0:T(8,128)S(1)} %end_tiles.1), channel_id=1, source_target_pairs={{1,2},{2,1},{3,4},{4,3},{5,6},{6,5},{7,8},{8,7},{9,10},{10,9},{11,... | collective-permute-start | bytes 18440 | tf_op jit(solution)/shard_map/ppermute | solution.py:319
  5.9 3.1 %collective-permute-start = (f32[12,128]{1,0:T(8,128)S(1)}, f32[12,128]{1,0:T(8,128)S(1)}, u32[]{:S(2)}, u32[]{:S(2)}) collective-permute-start(f32[12,128]{1,0:T(8,128)S(1)} %end_tiles.1), channel_id=1, source_target_pairs={{0,1},{1,0},{2,3},{3,2},{4,5},{5,4},{6,7},{7,6},{8,9},{9,8},{10,11... | collective-permute-start | bytes 18440 | tf_op jit(solution)/shard_map/ppermute | solution.py:319
  9.0 10.9 %collective-permute-start.3 = (f32[312,128]{1,0:T(8,128)S(1)}, f32[312,128]{1,0:T(8,128)S(1)}, u32[]{:S(2)}, u32[]{:S(2)}) collective-permute-start(f32[312,128]{1,0:T(8,128)S(1)} %frame_payload.1.own), channel_id=1, source_target_pairs={{64,0},{128,64},{192,128},{256,192},{320,256},{384,320},{448,384},... | collective-permute-start | bytes 479240 | tf_op jit(solution)/shard_map/ppermute | solution.py:30
  10.9 9.4 %collective-permute-start.2 = (f32[312,128]{1,0:T(8,128)S(1)}, f32[312,128]{1,0:T(8,128)S(1)}, u32[]{:S(2)}, u32[]{:S(2)}) collective-permute-start(f32[312,128]{1,0:T(8,128)S(1)} %frame_payload.1.own), channel_id=1, source_target_pairs={{0,64},{64,128},{128,192},{192,256},{256,320},{320,384},{384,448},... | collective-permute-start | bytes 479240 | tf_op jit(solution)/shard_map/ppermute | solution.py:30
  25.8 7.6 %collective-permute-start.4 = (f32[160,128]{1,0:T(8,128)S(1)}, f32[160,128]{1,0:T(8,128)S(1)}, u32[]{:S(2)}, u32[]{:S(2)}) collective-permute-start(f32[160,128]{1,0:T(8,128)S(1)} %get-tuple-element.18), channel_id=1, source_target_pairs={{0,64},{64,128},{128,192},{192,256},{256,320},{320,384},{384,448},... | collective-permute-start | bytes 245768 | tf_op jit(solution)/shard_map/ppermute | solution.py:30
  31.4 7.5 %collective-permute-start.5 = (f32[160,128]{1,0:T(8,128)S(1)}, f32[160,128]{1,0:T(8,128)S(1)}, u32[]{:S(2)}, u32[]{:S(2)}) collective-permute-start(f32[160,128]{1,0:T(8,128)S(1)} %get-tuple-element.19), channel_id=1, source_target_pairs={{64,0},{128,64},{192,128},{256,192},{320,256},{384,320},{448,384},... | collective-permute-start | bytes 245768 | tf_op jit(solution)/shard_map/ppermute | solution.py:30
  39.0 7.0 %collective-permute-start.7 = (f32[6,128]{1,0:T(8,128)S(1)}, f32[6,128]{1,0:T(8,128)S(1)}, u32[]{:S(2)}, u32[]{:S(2)}) collective-permute-start(f32[6,128]{1,0:T(8,128)S(1)} %get-tuple-element.23), channel_id=1, source_target_pairs={{1,2},{2,1},{3,4},{4,3},{5,6},{6,5},{7,8},{8,7},{9,10},{10,9},{11,... | collective-permute-start | bytes 9224 | tf_op jit(solution)/shard_map/ppermute | solution.py:319
  40.9 5.1 %collective-permute-start.6 = (f32[6,128]{1,0:T(8,128)S(1)}, f32[6,128]{1,0:T(8,128)S(1)}, u32[]{:S(2)}, u32[]{:S(2)}) collective-permute-start(f32[6,128]{1,0:T(8,128)S(1)} %get-tuple-element.24), channel_id=1, source_target_pairs={{0,1},{1,0},{2,3},{3,2},{4,5},{5,4},{6,7},{7,6},{8,9},{9,8},{10,11... | collective-permute-start | bytes 9224 | tf_op jit(solution)/shard_map/ppermute | solution.py:319

commit v7 on v5

--- a/solution.py
+++ b/solution.py
@@ -257,11 +257,28 @@
             out[end:] = jnp.zeros((out.shape[0] - end, out.shape[1]), jnp.float32)
 
 
-def merge_kernel(held, force, from_above, from_below, near, far, out):
+def merge_kernel(held, force, from_above, from_below, out, blocks):
     rows = 3 * held
     out[...] = force[...] + (from_above[0:rows] + from_below[0:rows])
-    out[pl.ds(0, 3, stride=held)] += near[0:3] + far[0:3]
-    out[pl.ds(held - 1, 3, stride=held)] += near[3:6] + far[3:6]
+    for j, start in enumerate((0, held - ALIGNED)):
+        for c in range(3):
+            blocks[j, c] = out[c * held + start : c * held + start + ALIGNED]
+
+
+def finish_kernel(held, merged, blocks, near, far, out, ready, sent):
+    ready[...] = blocks[...]
+    for j, row in enumerate((0, ALIGNED - 1)):
+        for c in range(3):
+            at = 3 * j + c
+            ready[j, c, row : row + 1] += near[at : at + 1] + far[at : at + 1]
+    copies = []
+    for j, start in enumerate((0, held - ALIGNED)):
+        part = out.at[:, pl.ds(start, ALIGNED), :]
+        copies.append(pltpu.make_async_copy(ready.at[j], part, sent.at[j]))
+    for copy in copies:
+        copy.start()
+    for copy in copies:
+        copy.wait()
 
 
 def limit(mebibytes):
@@ -392,15 +409,32 @@
     edge = edges + (from_above[tail] + from_below[tail])
     near_force = swapped(edge[0:6], "tile", 0)
     far_force = swapped(edge[6:12], "tile", 1)
-    merged = pl.pallas_call(
+    merged, blocks = pl.pallas_call(
         functools.partial(merge_kernel, held),
-        out_shape=jax.ShapeDtypeStruct((3 * held, points), f32),
-        in_specs=[VMEM] * 5,
-        out_specs=VMEM,
+        out_shape=(
+            jax.ShapeDtypeStruct((3 * held, points), f32),
+            jax.ShapeDtypeStruct((2, 3, ALIGNED, points), f32),
+        ),
+        in_specs=[VMEM] * 3,
+        out_specs=(VMEM, VMEM),
         compiler_params=limit(1),
+        cost_estimate=pl.CostEstimate(flops=0, bytes_accessed=4 << 20, transcendentals=0),
         name="merge_forces",
-    )(force, from_above, from_below, near_force, far_force)
-    return jnp.transpose(merged.reshape(3, held, points), (1, 0, 2))
+    )(force, from_above, from_below)
+    finished = pl.pallas_call(
+        functools.partial(finish_kernel, held),
+        out_shape=jax.ShapeDtypeStruct((3, held, points), f32),
+        in_specs=[HBM] + [VMEM] * 3,
+        out_specs=HBM,
+        scratch_shapes=[
+            pltpu.VMEM((2, 3, ALIGNED, points), f32),
+            pltpu.SemaphoreType.DMA((2,)),
+        ],
+        input_output_aliases={0: 0},
+        compiler_params=limit(1),
+        name="finish_ends",
+    )(in_hbm(merged.reshape(3, held, points)), blocks, near_force, far_force)
+    return jnp.transpose(finished, (1, 0, 2))
 
 
 def solution(mesh):

time: 45 us -> 44.9 us (level)
  waiting for transfers between devices: 9.86 us -> 9.23 us
  Pallas kernels: 10.7 us -> 11.3 us
    ppermute x4, waiting for transfers between devices: 2.76 us -> 2.12 us  [swapped(): return lax.ppermute(value, axis, pairs)]
    pallas_call x1 -> x2, Pallas kernels: 0.66 us -> 1.28 us  [the longest x1 0.65 us: on_device(): pl.pallas_call(functools.partial(merge_kernel, held), out_shape=(jax.Shap...]
  transfers between devices with their start and end apart: 8 -> 8, of which waited for: 5 -> 5; matrix products, arithmetic and copies ran while one was open for 2% -> 2% of each run, Pallas kernels for 8% -> 10%
where the time goes in v7:
time: 44.9 us; the launch traced here: 44.5 us
  starting transfers between devices  23.1 us (51%)
  Pallas kernels  11.3 us (25%)
  waiting for transfers between devices  9.23 us (21%)
  other arithmetic  0.72 us (2%)
    ppermute x4, starting transfers between devices, shifted(): lax.ppermute(value, axis, [(i, i + step) for i in range(first, last)])  11.7 us
    ppermute x4, starting transfers between devices, swapped(): return lax.ppermute(value, axis, pairs)  11.4 us
    ppermute x4, waiting for transfers between devices, shifted(): lax.ppermute(value, axis, [(i, i + step) for i in range(first, last)])  7.11 us
    pallas_call x1, Pallas kernels, on_device(): bond_call(held, intact.shape[0], points)  5.52 us
    pallas_call x1, Pallas kernels, on_device(): bonds, left = stage_call(held, intact)(info, own, in_hbm(intact))  2.76 us
    ppermute x4, waiting for transfers between devices, swapped(): return lax.ppermute(value, axis, pairs)  2.12 us
    pallas_call x1, Pallas kernels, on_device(): pl.pallas_call(functools.partial(pack_kernel, held), out_shape=packed, in...  0.94 us
  transfers between devices with their start and end apart: 8, of which 5 were waited for; matrix products, arithmetic and copies ran while one was open for 2% of the time, Pallas kernels for 10%

profile of v7, /device:TPU:518, one launch (start us, length us, event | category | flops | bytes accessed | tf_op | source)
XLA Modules:
  0.0 44.5 jit_solution(7466976013866890551)
XLA Ops:
  0.0 0.8 %end_tiles.1 = f32[12,128]{1,0:T(8,128)S(1)} custom-call(f32[3,48,128]{2,1,0:T(8,128)} %bitcast.16, f32[3,48,128]{2,1,0:T(8,128)} %bitcast.18), custom_call_target="tpu_custom_call" | custom-call | tf_op jit(solution)/shard_map/end_tiles/pallas_call | solution.py:347
  0.8 5.1 %collective-permute-start.1 = (f32[12,128]{1,0:T(8,128)S(1)}, f32[12,128]{1,0:T(8,128)S(1)}, u32[]{:S(2)}, u32[]{:S(2)}) collective-permute-start(f32[12,128]{1,0:T(8,128)S(1)} %end_tiles.1), channel_id=1, source_target_pairs={{1,2},{2,1},{3,4},{4,3},{5,6},{6,5},{7,8},{8,7},{9,10},{10,9},{11,... | collective-permute-start | bytes 18440 | tf_op jit(solution)/shard_map/ppermute | solution.py:336
  5.9 1.9 %collective-permute-start = (f32[12,128]{1,0:T(8,128)S(1)}, f32[12,128]{1,0:T(8,128)S(1)}, u32[]{:S(2)}, u32[]{:S(2)}) collective-permute-start(f32[12,128]{1,0:T(8,128)S(1)} %end_tiles.1), channel_id=1, source_target_pairs={{0,1},{1,0},{2,3},{3,2},{4,5},{5,4},{6,7},{7,6},{8,9},{9,8},{10,11... | collective-permute-start | bytes 18440 | tf_op jit(solution)/shard_map/ppermute | solution.py:336
  7.8 0.9 %pack_payload.1.payload = f32[312,128]{1,0:T(8,128)S(1)} custom-call(f32[144,128]{1,0:T(8,128)} %bitcast.17, f32[144,128]{1,0:T(8,128)} %bitcast.19), custom_call_target="tpu_custom_call" | custom-call | bytes 4194304 | tf_op jit(solution)/shard_map/pack_payload/pallas_call | solution.py:359
  8.8 0.0 collective-permute-done.1.far
  8.8 0.2 collective-permute-done.near
  9.0 3.7 %collective-permute-start.3 = (f32[312,128]{1,0:T(8,128)S(1)}, f32[312,128]{1,0:T(8,128)S(1)}, u32[]{:S(2)}, u32[]{:S(2)}) collective-permute-start(f32[312,128]{1,0:T(8,128)S(1)} %frame_payload.1.own), channel_id=1, source_target_pairs={{64,0},{128,64},{192,128},{256,192},{320,256},{384,320},{448,384},... | collective-permute-start | bytes 479240 | tf_op jit(solution)/shard_map/ppermute | solution.py:30
  12.6 2.2 %collective-permute-start.2 = (f32[312,128]{1,0:T(8,128)S(1)}, f32[312,128]{1,0:T(8,128)S(1)}, u32[]{:S(2)}, u32[]{:S(2)}) collective-permute-start(f32[312,128]{1,0:T(8,128)S(1)} %frame_payload.1.own), channel_id=1, source_target_pairs={{0,64},{64,128},{128,192},{192,256},{256,320},{320,384},{384,448},... | collective-permute-start | bytes 479240 | tf_op jit(solution)/shard_map/ppermute | solution.py:30
  14.8 0.7 %fusion.1 = (s32[64,2]{0,1:T(2,128)S(1)}, s32[64,2]{0,1:T(2,128)S(1)}, s32[64,2]{0,1:T(2,128)S(1)}) fusion(s32[]{:T(128)S(6)} %add.52, s32[]{:T(128)S(6)} %sub.26, s32[]{:T(128)S(6)} %mul.41, s32[]{:T(128)S(6)} %axis_index.23, s32[64,2]{0,1:T(2,128)} %param.6), kind=kLoop, calls=%fused_computation.7 | loop fusion | flops 2688 | bytes 2064 | tf_op jit(solution)/shard_map/add | solution.py:392
  15.6 2.8 %stage_bonds.1 = (s32[64,128,128]{2,1,0:T(8,128)S(1)}, bf16[64,128,48]{2,1,0:T(8,128)(2,1)S(1)}) custom-call(s32[4,64]{1,0:T(4,128)S(1)} %pad_add_fusion.info, f32[312,128]{1,0:T(8,128)S(1)} %frame_payload.1.own, s32[64,128,128]{2,1,0:T(8,128)} %bonds.1), custom_call_target="tpu_custom_call" | custom-call | bytes 4194304 | tf_op jit(solution)/shard_map/stage_bonds/pallas_call | solution.py:402
  18.3 0.0 collective-permute-done.3.above
  18.4 3.5 %collective-permute-done.2.below = f32[312,128]{1,0:T(8,128)S(1)} collective-permute-done((f32[312,128]{1,0:T(8,128)S(1)}, f32[312,128]{1,0:T(8,128)S(1)}, u32[]{:S(2)}, u32[]{:S(2)}) %collective-permute-start.2) | collective-permute-done | bytes 159776 | tf_op jit(solution)/shard_map/ppermute | solution.py:30
  21.8 5.5 %bond_forces.1 = (f32[144,128]{1,0:T(8,128)S(1)}, f32[160,128]{1,0:T(8,128)S(1)}, f32[160,128]{1,0:T(8,128)S(1)}, f32[12,128]{1,0:T(8,128)S(1)}) custom-call(s32[4,64]{1,0:T(4,128)S(1)} %pad_add_fusion.info, f32[312,128]{1,0:T(8,128)S(1)} %collective-permute-done.2.below, f32[312,128]{1,0:T(8,128)S(1)} %frame_payload.1.own, ...), custom_call_target="tpu_custom_call" | custom-call | tf_op jit(solution)/shard_map/bond_forces/pallas_call | solution.py:403
  27.4 1.9 %collective-permute-start.4 = (f32[160,128]{1,0:T(8,128)S(1)}, f32[160,128]{1,0:T(8,128)S(1)}, u32[]{:S(2)}, u32[]{:S(2)}) collective-permute-start(f32[160,128]{1,0:T(8,128)S(1)} %get-tuple-element.20), channel_id=1, source_target_pairs={{64,0},{128,64},{192,128},{256,192},{320,256},{384,320},{448,384},... | collective-permute-start | bytes 245768 | tf_op jit(solution)/shard_map/ppermute | solution.py:30
  29.3 3.9 %collective-permute-start.5 = (f32[160,128]{1,0:T(8,128)S(1)}, f32[160,128]{1,0:T(8,128)S(1)}, u32[]{:S(2)}, u32[]{:S(2)}) collective-permute-start(f32[160,128]{1,0:T(8,128)S(1)} %get-tuple-element.21), channel_id=1, source_target_pairs={{0,64},{64,128},{128,192},{192,256},{256,320},{320,384},{384,448},... | collective-permute-start | bytes 245768 | tf_op jit(solution)/shard_map/ppermute | solution.py:30
  33.2 0.5 %collective-permute-done.4.from_above = f32[160,128]{1,0:T(8,128)S(1)} collective-permute-done((f32[160,128]{1,0:T(8,128)S(1)}, f32[160,128]{1,0:T(8,128)S(1)}, u32[]{:S(2)}, u32[]{:S(2)}) %collective-permute-start.4) | collective-permute-done | bytes 81952 | tf_op jit(solution)/shard_map/ppermute | solution.py:30
  33.7 3.1 %collective-permute-done.5.from_below = f32[160,128]{1,0:T(8,128)S(1)} collective-permute-done((f32[160,128]{1,0:T(8,128)S(1)}, f32[160,128]{1,0:T(8,128)S(1)}, u32[]{:S(2)}, u32[]{:S(2)}) %collective-permute-start.5) | collective-permute-done | bytes 81952 | tf_op jit(solution)/shard_map/ppermute | solution.py:30
  36.9 2.5 %collective-permute-start.7 = (f32[6,128]{1,0:T(8,128)S(1)}, f32[6,128]{1,0:T(8,128)S(1)}, u32[]{:S(2)}, u32[]{:S(2)}) collective-permute-start(f32[6,128]{1,0:T(8,128)S(1)} %get-tuple-element.27), channel_id=1, source_target_pairs={{1,2},{2,1},{3,4},{4,3},{5,6},{6,5},{7,8},{8,7},{9,10},{10,9},{11,... | collective-permute-start | bytes 9224 | tf_op jit(solution)/shard_map/ppermute | solution.py:336
  39.3 1.9 %collective-permute-start.6 = (f32[6,128]{1,0:T(8,128)S(1)}, f32[6,128]{1,0:T(8,128)S(1)}, u32[]{:S(2)}, u32[]{:S(2)}) collective-permute-start(f32[6,128]{1,0:T(8,128)S(1)} %get-tuple-element.28), channel_id=1, source_target_pairs={{0,1},{1,0},{2,3},{3,2},{4,5},{5,4},{6,7},{7,6},{8,9},{9,8},{10,11... | collective-permute-start | bytes 9224 | tf_op jit(solution)/shard_map/ppermute | solution.py:336
  41.3 0.7 %merge_forces.1 = (f32[144,128]{1,0:T(8,128)}, f32[2,3,8,128]{3,2,1,0:T(8,128)S(1)}) custom-call(f32[144,128]{1,0:T(8,128)S(1)} %get-tuple-element.19.force, f32[160,128]{1,0:T(8,128)S(1)} %collective-permute-done.4.from_above, f32[160,128]{1,0:T(8,128)S(1)} %collective-permute-done.5.from_below), custom_call_target="tpu_custom_call" | custom-call | bytes 4194304 | tf_op jit(solution)/shard_map/merge_forces/pallas_call | solution.py:412
  41.9 2.0 %collective-permute-done.7.far = f32[6,128]{1,0:T(8,128)S(1)} collective-permute-done((f32[6,128]{1,0:T(8,128)S(1)}, f32[6,128]{1,0:T(8,128)S(1)}, u32[]{:S(2)}, u32[]{:S(2)}) %collective-permute-start.7) | collective-permute-done | bytes 3104 | tf_op jit(solution)/shard_map/ppermute | solution.py:336
  43.9 0.0 collective-permute-done.6.near
  43.9 0.6 %finish_ends.1 = f32[3,48,128]{2,1,0:T(8,128)} custom-call(f32[3,48,128]{2,1,0:T(8,128)} %bitcast.20, f32[2,3,8,128]{3,2,1,0:T(8,128)S(1)} %get-tuple-element.23.blocks, f32[6,128]{1,0:T(8,128)S(1)} %collective-permute-done.6.near, f32[6,128]{1,0:T(8,128)S(1)} %collective-permute-done.7.far), custom_call_target="tpu_custom_call", output_to_operand_aliasing={{}: (0, {})} | custom-call | tf_op jit(solution)/shard_map/finish_ends/pallas_call | solution.py:424
  (6 shorter events, 0.0 us)
Async XLA Ops:
  0.8 8.0 %collective-permute-start.1 = (f32[12,128]{1,0:T(8,128)S(1)}, f32[12,128]{1,0:T(8,128)S(1)}, u32[]{:S(2)}, u32[]{:S(2)}) collective-permute-start(f32[12,128]{1,0:T(8,128)S(1)} %end_tiles.1), channel_id=1, source_target_pairs={{1,2},{2,1},{3,4},{4,3},{5,6},{6,5},{7,8},{8,7},{9,10},{10,9},{11,... | collective-permute-start | bytes 18440 | tf_op jit(solution)/shard_map/ppermute | solution.py:336
  5.9 3.1 %collective-permute-start = (f32[12,128]{1,0:T(8,128)S(1)}, f32[12,128]{1,0:T(8,128)S(1)}, u32[]{:S(2)}, u32[]{:S(2)}) collective-permute-start(f32[12,128]{1,0:T(8,128)S(1)} %end_tiles.1), channel_id=1, source_target_pairs={{0,1},{1,0},{2,3},{3,2},{4,5},{5,4},{6,7},{7,6},{8,9},{9,8},{10,11... | collective-permute-start | bytes 18440 | tf_op jit(solution)/shard_map/ppermute | solution.py:336
  9.0 9.4 %collective-permute-start.3 = (f32[312,128]{1,0:T(8,128)S(1)}, f32[312,128]{1,0:T(8,128)S(1)}, u32[]{:S(2)}, u32[]{:S(2)}) collective-permute-start(f32[312,128]{1,0:T(8,128)S(1)} %frame_payload.1.own), channel_id=1, source_target_pairs={{64,0},{128,64},{192,128},{256,192},{320,256},{384,320},{448,384},... | collective-permute-start | bytes 479240 | tf_op jit(solution)/shard_map/ppermute | solution.py:30
  12.6 9.2 %collective-permute-start.2 = (f32[312,128]{1,0:T(8,128)S(1)}, f32[312,128]{1,0:T(8,128)S(1)}, u32[]{:S(2)}, u32[]{:S(2)}) collective-permute-start(f32[312,128]{1,0:T(8,128)S(1)} %frame_payload.1.own), channel_id=1, source_target_pairs={{0,64},{64,128},{128,192},{192,256},{256,320},{320,384},{384,448},... | collective-permute-start | bytes 479240 | tf_op jit(solution)/shard_map/ppermute | solution.py:30
  27.4 6.3 %collective-permute-start.4 = (f32[160,128]{1,0:T(8,128)S(1)}, f32[160,128]{1,0:T(8,128)S(1)}, u32[]{:S(2)}, u32[]{:S(2)}) collective-permute-start(f32[160,128]{1,0:T(8,128)S(1)} %get-tuple-element.20), channel_id=1, source_target_pairs={{64,0},{128,64},{192,128},{256,192},{320,256},{384,320},{448,384},... | collective-permute-start | bytes 245768 | tf_op jit(solution)/shard_map/ppermute | solution.py:30
  29.3 7.5 %collective-permute-start.5 = (f32[160,128]{1,0:T(8,128)S(1)}, f32[160,128]{1,0:T(8,128)S(1)}, u32[]{:S(2)}, u32[]{:S(2)}) collective-permute-start(f32[160,128]{1,0:T(8,128)S(1)} %get-tuple-element.21), channel_id=1, source_target_pairs={{0,64},{64,128},{128,192},{192,256},{256,320},{320,384},{384,448},... | collective-permute-start | bytes 245768 | tf_op jit(solution)/shard_map/ppermute | solution.py:30
  36.9 7.0 %collective-permute-start.7 = (f32[6,128]{1,0:T(8,128)S(1)}, f32[6,128]{1,0:T(8,128)S(1)}, u32[]{:S(2)}, u32[]{:S(2)}) collective-permute-start(f32[6,128]{1,0:T(8,128)S(1)} %get-tuple-element.27), channel_id=1, source_target_pairs={{1,2},{2,1},{3,4},{4,3},{5,6},{6,5},{7,8},{8,7},{9,10},{10,9},{11,... | collective-permute-start | bytes 9224 | tf_op jit(solution)/shard_map/ppermute | solution.py:336
  39.3 4.5 %collective-permute-start.6 = (f32[6,128]{1,0:T(8,128)S(1)}, f32[6,128]{1,0:T(8,128)S(1)}, u32[]{:S(2)}, u32[]{:S(2)}) collective-permute-start(f32[6,128]{1,0:T(8,128)S(1)} %get-tuple-element.28), channel_id=1, source_target_pairs={{0,1},{1,0},{2,3},{3,2},{4,5},{5,4},{6,7},{7,6},{8,9},{9,8},{10,11... | collective-permute-start | bytes 9224 | tf_op jit(solution)/shard_map/ppermute | solution.py:336
